TPU v7x, 256 devices: a whole 4x4x8 slice. The times are simulated.
256 devices in a mesh: row: 8 (over z), col: 32 (over x, y, core).
Axes of the slice: x: 4, y: 4, z: 8, core: 2. Of those that a mesh axis runs over, the one named last changes fastest.
Arguments:
- tokens: bfloat16 [2, 2048, 4096], P(None, 'col', 'row'), may hold values from -12 to 12
- cotangent: bfloat16 [2, 2048, 4096], P(None, 'col', 'row'), may hold values from -1.5 to 1.5
- wi_gate: bfloat16 [4096, 10240], P('row', 'col'), may hold values from -1 to 1
- wi_lin: bfloat16 [4096, 10240], P('row', 'col'), may hold values from -1 to 1
- wo: bfloat16 [10240, 4096], P('col', 'row'), may hold values from -1 to 1
- rows_gate: float32 [4096], P('row'), may hold values from 0.5 to 2
- cols_gate: float32 [10240], P('col'), may hold values from 0.5 to 2
- rows_lin: float32 [4096], P('row'), may hold values from 0.5 to 2
- cols_lin: float32 [10240], P('col'), may hold values from 0.5 to 2
- rows_out: float32 [10240], P('col'), may hold values from 0.5 to 2
- cols_out: float32 [4096], P('row'), may hold values from 0.5 to 2
- rate: float32 [1], replicated, may hold values from 0.5 to 2
Outputs:
- grad_tokens: bfloat16 [2, 2048, 4096], P(None, 'col', 'row')
- update_gate: float32 [4096, 10240], P('row', 'col')
- update_lin: float32 [4096, 10240], P('row', 'col')
- update_out: float32 [10240, 4096], P('col', 'row')
- rows_gate_new: float32 [4096], P('row')
- cols_gate_new: float32 [10240], P('col')
- rows_lin_new: float32 [4096], P('row')
- cols_lin_new: float32 [10240], P('col')
- rows_out_new: float32 [10240], P('col')
- cols_out_new: float32 [4096], P('row')
All inputs are finite; a program needn't handle non-finite values.
Results may differ from a plain program's by a relative error of at most 0.034.
Values may be sent and summed in bfloat16 or wider, within the bound.
No kernel may reach another device: no remote copies, remote signals or barrier semaphores. Data moves between devices by JAX's collectives and lax.ppermute only.
A program may use at most 128 MiB of HBM per device.

v0:
```python
import math

import jax
import jax.numpy as jnp
from jax import lax
from jax.sharding import PartitionSpec as P

D = 4096
FF = 10240


decay_rate = 0.8
gelu_coeff = math.sqrt(2.0 / math.pi)


def gelu_parts(value):
    inner = gelu_coeff * (value + 0.044715 * value * value * value)
    tangent = jnp.tanh(inner)
    gelu_value = 0.5 * value * (1.0 + tangent)
    gelu_slope = 0.5 * (1.0 + tangent) + 0.5 * value * (1.0 - tangent * tangent) * gelu_coeff * (
        1.0 + 3.0 * 0.044715 * value * value
    )
    return (gelu_value, gelu_slope)


def pointwise(terms, width):
    pre_gate = terms[:, :width]
    pre_lin = terms[:, width : 2 * width]
    grad_act = terms[:, 2 * width :]
    gelu_value, gelu_slope = gelu_parts(pre_gate)
    act = (gelu_value * pre_lin).astype(jnp.bfloat16)
    grad_pre = jnp.concatenate([grad_act * pre_lin * gelu_slope, grad_act * gelu_value], 1).astype(
        jnp.bfloat16
    )
    return (act, grad_pre)


def contract_rows(left, right):
    return lax.dot_general(
        left, right, (((0,), (0,)), ((), ())), preferred_element_type=jnp.float32
    )


def contract_cols(left, right):
    return lax.dot_general(
        left, right, (((1,), (1,)), ((), ())), preferred_element_type=jnp.float32
    )


def local(
    tokens,
    cotangent,
    wi_gate,
    wi_lin,
    wo,
    rows_gate,
    cols_gate,
    rows_lin,
    cols_lin,
    rows_out,
    cols_out,
    rate,
):
    micro = tokens.shape[0]
    width = wi_gate.shape[1]
    model_local = wi_gate.shape[0]
    weight_in = jnp.concatenate([wi_gate, wi_lin], 1)
    grad_in_w = jnp.zeros((model_local, 2 * width), jnp.float32)
    grad_out_w = jnp.zeros((width, model_local), jnp.float32)
    results = []
    tok_total = 0
    for micro_index in range(micro):
        inputs, upstream = (
            lax.all_gather(tokens[micro_index], "col", axis=0, tiled=True),
            lax.all_gather(cotangent[micro_index], "col", axis=0, tiled=True),
        )
        tok_total = inputs.shape[0]
        forward = jnp.dot(inputs, weight_in, preferred_element_type=jnp.float32)
        backward = contract_cols(upstream, wo)
        terms = lax.psum_scatter(
            jnp.concatenate([forward, backward], 1).astype(jnp.bfloat16),
            "row",
            scatter_dimension=0,
            tiled=True,
        ).astype(jnp.float32)
        act_part, grad_pre_part = pointwise(terms, width)
        act_all, grad_pre_all = (
            lax.all_gather(act_part, "row", axis=0, tiled=True),
            lax.all_gather(grad_pre_part, "row", axis=0, tiled=True),
        )
        grad_in_w = grad_in_w + contract_rows(inputs, grad_pre_all)
        grad_out_w = grad_out_w + contract_rows(act_all, upstream)
        grad_rows = lax.psum_scatter(
            contract_cols(grad_pre_all, weight_in).astype(jnp.bfloat16),
            "col",
            scatter_dimension=0,
            tiled=True,
        )
        results.append(grad_rows)
    scale = 1.0 / math.sqrt(micro * tok_total)
    grad_gate = grad_in_w[:, :width] * scale
    grad_lin = grad_in_w[:, width:] * scale
    grad_out = grad_out_w * scale
    squares_gate = grad_gate * grad_gate + 1e-30
    squares_lin = grad_lin * grad_lin + 1e-30
    squares_out = grad_out * grad_out + 1e-30
    keep = 1.0 - decay_rate
    over_ff = lax.psum(
        (jnp.sum(squares_gate, 1), jnp.sum(squares_lin, 1), jnp.sum(squares_out, 0)), "col"
    )
    over_d = lax.psum(
        (jnp.sum(squares_gate, 0), jnp.sum(squares_lin, 0), jnp.sum(squares_out, 1)), "row"
    )
    rows_gate_new = decay_rate * rows_gate + keep * over_ff[0] / FF
    rows_lin_new = decay_rate * rows_lin + keep * over_ff[1] / FF
    cols_out_new = decay_rate * cols_out + keep * over_ff[2] / FF
    cols_gate_new = decay_rate * cols_gate + keep * over_d[0] / D
    cols_lin_new = decay_rate * cols_lin + keep * over_d[1] / D
    rows_out_new = decay_rate * rows_out + keep * over_d[2] / D
    unit_gate = grad_gate / jnp.sqrt(rows_gate_new[:, None] * cols_gate_new[None, :])
    unit_lin = grad_lin / jnp.sqrt(rows_lin_new[:, None] * cols_lin_new[None, :])
    unit_out = grad_out / jnp.sqrt(rows_out_new[:, None] * cols_out_new[None, :])
    clip_totals = lax.psum(
        (
            jnp.sum(unit_gate * unit_gate),
            jnp.sum(unit_lin * unit_lin),
            jnp.sum(unit_out * unit_out),
        ),
        ("row", "col"),
    )
    count = D * FF
    update_gate = -rate[0] * unit_gate / jnp.sqrt(clip_totals[0] / count + 1e-06)
    update_lin = -rate[0] * unit_lin / jnp.sqrt(clip_totals[1] / count + 1e-06)
    update_out = -rate[0] * unit_out / jnp.sqrt(clip_totals[2] / count + 1e-06)
    return (
        jnp.stack(results, 0),
        update_gate,
        update_lin,
        update_out,
        rows_gate_new,
        cols_gate_new,
        rows_lin_new,
        cols_lin_new,
        rows_out_new,
        cols_out_new,
    )


def solution(mesh):
    return jax.shard_map(
        local,
        mesh=mesh,
        in_specs=(
            P(None, "col", "row"),
            P(None, "col", "row"),
            P("row", "col"),
            P("row", "col"),
            P("col", "row"),
            P("row"),
            P("col"),
            P("row"),
            P("col"),
            P("col"),
            P("row"),
            P(),
        ),
        out_specs=(
            P(None, "col", "row"),
            P("row", "col"),
            P("row", "col"),
            P("col", "row"),
            P("row"),
            P("col"),
            P("row"),
            P("col"),
            P("col"),
            P("row"),
        ),
        check_vma=False,
    )
```

profile of v0, /device:TPU:8, one launch (start us, length us, event | category | flops | bytes accessed | tf_op | source)
XLA Modules:
  0.0 767.0 jit_solution(11795421457336101363)
XLA Ops:
  7.2 0.0 all-gather.27.cloned.1.call-start
  7.2 1.6 fusion.47
  8.8 0.0 all-gather.25.cloned.1.call-start
  8.9 1.5 fusion.46
  10.4 0.0 all-gather.23.cloned.1.call-start
  10.5 0.7 all-gather.23.cloned.1.call-update
  11.2 0.0 all-gather.21.cloned.1.call-start
  11.2 0.5 all-gather.21.cloned.1.call-update
  11.7 0.0 reduce-scatter.9.cloned.1.call-start
  11.8 1.0 constant_dynamic-update-slice_fusion.1
  12.8 1.0 constant_dynamic-update-slice_fusion
  13.8 48.7 %all-gather.27.cloned.1.call-done = bf16[1,2048,512]{2,1,0:T(8,128)(2,1)} async-done(((bf16[1,64,512]{2,1,0:T(8,128)(2,1)}), bf16[1,2048,512]{2,1,0:T(8,128)(2,1)}) %all-gather.27.cloned.1.call-update) | async-done | bytes 2097168 | tf_op jit(solution)/shard_map/all_gather | solution.py:75
  62.5 2.5 convolution_convert_fusion.4
  64.9 48.8 %all-gather.25.cloned.1.call-done = bf16[1,2048,512]{2,1,0:T(8,128)(2,1)} async-done(((bf16[1,64,512]{2,1,0:T(8,128)(2,1)}), bf16[1,2048,512]{2,1,0:T(8,128)(2,1)}) %all-gather.25.cloned.1.call-update) | async-done | bytes 2097168 | tf_op jit(solution)/shard_map/all_gather | solution.py:74
  113.8 3.1 fusion.1
  116.9 2.4 pad_maximum_fusion.1
  119.3 0.0 reduce-scatter.5.cloned.1.call-start
  119.4 45.7 %all-gather.23.cloned.1.call-done = bf16[1,2048,512]{2,1,0:T(8,128)(2,1)} async-done(((bf16[1,64,512]{2,1,0:T(8,128)(2,1)}), bf16[1,2048,512]{2,1,0:T(8,128)(2,1)}) %all-gather.23.cloned.1.call-update) | async-done | bytes 2097168 | tf_op jit(solution)/shard_map/all_gather | solution.py:75
  165.1 2.5 convolution_convert_fusion.5
  167.5 48.7 %all-gather.21.cloned.1.call-done = bf16[1,2048,512]{2,1,0:T(8,128)(2,1)} async-done(((bf16[1,64,512]{2,1,0:T(8,128)(2,1)}), bf16[1,2048,512]{2,1,0:T(8,128)(2,1)}) %all-gather.21.cloned.1.call-update) | async-done | bytes 2097168 | tf_op jit(solution)/shard_map/all_gather | solution.py:74
  216.2 3.1 fusion
  219.4 2.4 pad_maximum_fusion
  221.7 0.0 all-gather.15.cloned.1.call-start
  221.8 49.4 %reduce-scatter.9.cloned.1.call-done = bf16[256,960]{0,1:T(8,128)(2,1)} async-done(((bf16[2048,960]{0,1:T(8,128)(2,1)}), bf16[256,960]{0,1:T(8,128)(2,1)}) %reduce-scatter.9.cloned.1.call-update) | async-done | bytes 491536 | tf_op jit(solution)/shard_map/reduce_scatter | solution.py:80
  271.2 1.1 convert_element_type.24
  272.3 0.9 multiply_convert_fusion
  273.2 0.7 pad_maximum_fusion.3
  274.0 0.0 all-gather.19.cloned.1.call-start
  274.1 0.7 all-gather.19.cloned.1.call-update
  274.8 0.0 all-gather.13.cloned.1.call-start
  274.8 50.4 %reduce-scatter.5.cloned.1.call-done = bf16[256,960]{0,1:T(8,128)(2,1)} async-done(((bf16[2048,960]{0,1:T(8,128)(2,1)}), bf16[256,960]{0,1:T(8,128)(2,1)}) %reduce-scatter.5.cloned.1.call-update) | async-done | bytes 491536 | tf_op jit(solution)/shard_map/reduce_scatter | solution.py:80
  325.2 1.1 convert_element_type.22
  326.3 0.9 multiply_convert_fusion.1
  327.3 0.7 pad_maximum_fusion.2
  328.0 0.0 all-gather.17.cloned.1.call-start
  328.1 0.5 all-gather.17.cloned.1.call-update
  328.6 0.0 reduce-scatter.11.cloned.1.call-start
  328.7 48.8 %all-gather.15.cloned.1.call-done = bf16[2048,640]{0,1:T(8,128)(2,1)} async-done(((bf16[256,640]{0,1:T(8,128)(2,1)}), bf16[2048,640]{0,1:T(8,128)(2,1)}) %all-gather.15.cloned.1.call-update) | async-done | bytes 2621456 | tf_op jit(solution)/shard_map/all_gather | solution.py:89
  377.4 4.9 convolution_convert_fusion.2
  382.4 0.2 reduce-scatter.7.cloned.1.call-start
  383.4 36.8 %all-gather.19.cloned.1.call-done = bf16[2048,320]{0,1:T(8,128)(2,1)} async-done(((bf16[256,320]{0,1:T(8,128)(2,1)}), bf16[2048,320]{0,1:T(8,128)(2,1)}) %all-gather.19.cloned.1.call-update) | async-done | bytes 1310736 | tf_op jit(solution)/shard_map/all_gather | solution.py:88
  420.2 3.0 fusion.2
  423.1 49.5 %all-gather.13.cloned.1.call-done = bf16[2048,640]{0,1:T(8,128)(2,1)} async-done(((bf16[256,640]{0,1:T(8,128)(2,1)}), bf16[2048,640]{0,1:T(8,128)(2,1)}) %all-gather.13.cloned.1.call-update) | async-done | bytes 2621456 | tf_op jit(solution)/shard_map/all_gather | solution.py:89
  472.6 4.9 convolution_convert_fusion.3
  477.6 37.1 %all-gather.17.cloned.1.call-done = bf16[2048,320]{0,1:T(8,128)(2,1)} async-done(((bf16[256,320]{0,1:T(8,128)(2,1)}), bf16[2048,320]{0,1:T(8,128)(2,1)}) %all-gather.17.cloned.1.call-update) | async-done | bytes 1310736 | tf_op jit(solution)/shard_map/all_gather | solution.py:88
  514.7 3.1 fusion.31
  517.8 0.3 copy-done.15
  518.1 1.5 fusion.5
  519.6 0.2 copy-done.14
  519.8 0.6 copy-done.17
  520.5 1.5 fusion.17
  522.0 0.2 fusion.29
  522.2 58.4 %psum.66 = f32[512]{0:T(512)S(1)} all-reduce(f32[512]{0:T(512)S(1)} %get-tuple-element.13), channel_id=1, replica_groups=mesh['row'=8,'col'=32] {'col'}, use_global_device_ids=true, to_apply=%region_11.0 | all-reduce | flops 512 | bytes 4096 | tf_op jit(solution)/shard_map/psum | solution.py:108
  580.6 16.1 %psum.67 = f32[320]{0:T(512)S(1)} all-reduce(f32[320]{0:T(512)S(1)} %get-tuple-element.14), channel_id=1, replica_groups=mesh['row'=8,'col'=32] {'row'}, use_global_device_ids=true, to_apply=%region_13.0 | all-reduce | flops 320 | bytes 2560 | tf_op jit(solution)/shard_map/psum | solution.py:111
  596.8 0.9 multiply_reduce_fusion.1
  597.8 62.7 %all-reduce.1 = (f32[512]{0:T(512)S(1)}, f32[512]{0:T(512)S(1)}) all-reduce(f32[512]{0:T(512)S(1)} %get-tuple-element.12, f32[512]{0:T(512)S(1)} %get-tuple-element.16), channel_id=1, replica_groups=mesh['row'=8,'col'=32] {'col'}, use_global_device_ids=true, to_apply=%region_5.0 | all-reduce | flops 1024 | bytes 8192 | tf_op jit(solution)/shard_map/psum | solution.py:108
  660.4 14.2 %all-reduce.2 = (f32[320]{0:T(512)S(1)}, f32[320]{0:T(512)S(1)}) all-reduce(f32[320]{0:T(512)S(1)} %get-tuple-element.11, f32[320]{0:T(512)S(1)} %get-tuple-element.15), channel_id=1, replica_groups=mesh['row'=8,'col'=32] {'row'}, use_global_device_ids=true, to_apply=%region_7.0 | all-reduce | flops 640 | bytes 5120 | tf_op jit(solution)/shard_map/psum | solution.py:111
  674.7 0.9 multiply_reduce_fusion
  675.6 0.9 multiply_reduce_fusion.2
  676.5 77.6 %all-reduce = (f32[]{:T(128)}, f32[]{:T(128)}, f32[]{:T(128)}) all-reduce(f32[]{:T(128)} %multiply_reduce_fusion.2, f32[]{:T(128)} %get-tuple-element.10, f32[]{:T(128)} %multiply_reduce_fusion), channel_id=1, replica_groups=mesh['row'=8,'col'=32] {'row','col'}, use_global_device_ids=true, to_apply=%region_9.0 | all-reduce | flops 3 | bytes 24 | tf_op jit(solution)/shard_map/psum | solution.py:123
  756.1 1.0 multiply_divide_fusion
  757.1 1.4 multiply_divide_fusion.1
  758.5 0.0 reduce-scatter.11.cloned.1.call-done
  758.6 1.5 pad_maximum_fusion.4
  (48 shorter events, 0.3 us)
Async XLA Ops:
  7.2 55.3 %copy-start = (bf16[320,512]{1,0:T(8,128)(2,1)S(1)}, bf16[320,512]{1,0:T(8,128)(2,1)}, u32[]{:S(2)}) copy-start(bf16[320,512]{1,0:T(8,128)(2,1)} %param.16) | copy-start | bytes 983044
  7.2 55.3 %all-gather.27.cloned.1.call-start = ((), (), s32[]{:S(2)}) async-start(), calls=%async_computation.15 | async-start | bytes 2162688 | tf_op jit(solution)/shard_map/all_gather | solution.py:75
  8.8 104.9 %all-gather.25.cloned.1.call-start = ((), (), s32[]{:S(2)}) async-start(), calls=%async_computation.14 | async-start | bytes 2162688 | tf_op jit(solution)/shard_map/all_gather | solution.py:74
  10.4 154.6 %all-gather.23.cloned.1.call-start = ((), (), s32[]{:S(2)}) async-start(), calls=%async_computation.13 | async-start | bytes 2162688 | tf_op jit(solution)/shard_map/all_gather | solution.py:75
  11.2 205.0 %all-gather.21.cloned.1.call-start = ((), (), s32[]{:S(2)}) async-start(), calls=%async_computation.12 | async-start | bytes 2162688 | tf_op jit(solution)/shard_map/all_gather | solution.py:74
  11.7 259.5 %reduce-scatter.9.cloned.1.call-start = ((), (), s32[]{:S(2)}) async-start(), calls=%async_computation.7 | async-start | bytes 4423680 | tf_op jit(solution)/shard_map/reduce_scatter | solution.py:80
  119.3 205.9 %reduce-scatter.5.cloned.1.call-start = ((), (), s32[]{:S(2)}) async-start(), calls=%async_computation.4 | async-start | bytes 4423680 | tf_op jit(solution)/shard_map/reduce_scatter | solution.py:80
  221.7 155.7 %all-gather.15.cloned.1.call-start = ((), (), s32[]{:S(2)}) async-start(), calls=%async_computation.8 | async-start | bytes 2949120 | tf_op jit(solution)/shard_map/all_gather | solution.py:89
  274.0 146.1 %all-gather.19.cloned.1.call-start = ((), (), s32[]{:S(2)}) async-start(), calls=%async_computation.11 | async-start | bytes 1474560 | tf_op jit(solution)/shard_map/all_gather | solution.py:88
  274.8 197.9 %all-gather.13.cloned.1.call-start = ((), (), s32[]{:S(2)}) async-start(), calls=%async_computation.5 | async-start | bytes 2949120 | tf_op jit(solution)/shard_map/all_gather | solution.py:89
  328.0 186.6 %all-gather.17.cloned.1.call-start = ((), (), s32[]{:S(2)}) async-start(), calls=%async_computation.10 | async-start | bytes 1474560 | tf_op jit(solution)/shard_map/all_gather | solution.py:88
  328.6 429.9 %reduce-scatter.11.cloned.1.call-start = ((), (), s32[]{:S(2)}) async-start(), calls=%async_computation.9 | async-start | bytes 2162688 | tf_op jit(solution)/shard_map/reduce_scatter | solution.py:93
  382.3 37.8 %copy-start.16 = (bf16[1,2048,512]{2,1,0:T(8,128)(2,1)S(1)}, bf16[1,2048,512]{2,1,0:T(8,128)(2,1)}, u32[]{:S(2)}) copy-start(bf16[1,2048,512]{2,1,0:T(8,128)(2,1)} %all-gather.27.cloned.1.call-done) | copy-start | bytes 6291460
  382.4 376.2 %reduce-scatter.7.cloned.1.call-start = ((), (), s32[]{:S(2)}) async-start(), calls=%async_computation.6 | async-start | bytes 2162688 | tf_op jit(solution)/shard_map/reduce_scatter | solution.py:93
  477.5 37.1 %copy-start.18 = (f32[320,512]{1,0:T(8,128)S(1)}, f32[320,512]{1,0:T(8,128)}, u32[]{:S(2)}) copy-start(f32[320,512]{1,0:T(8,128)} %fusion.2) | copy-start | bytes 1966084
  514.7 3.1 copy-start.13
  514.7 3.4 copy-start.15
  518.1 1.7 copy-start.14
  518.1 2.4 copy-start.17
  520.4 76.3 %copy-start.7 = (f32[512]{0:T(512)S(1)}, f32[512]{0:T(512)}, u32[]{:S(2)}) copy-start(f32[512]{0:T(512)} %param.19) | copy-start | bytes 6148
  520.4 76.3 %copy-start.8 = (f32[320]{0:T(512)S(1)}, f32[320]{0:T(512)}, u32[]{:S(2)}) copy-start(f32[320]{0:T(512)} %param.20) | copy-start | bytes 3844
  520.4 154.1 %copy-start.9 = (f32[320]{0:T(512)S(1)}, f32[320]{0:T(512)}, u32[]{:S(2)}) copy-start(f32[320]{0:T(512)} %param.21) | copy-start | bytes 3844
  520.4 154.1 %copy-start.10 = (f32[320]{0:T(512)S(1)}, f32[320]{0:T(512)}, u32[]{:S(2)}) copy-start(f32[320]{0:T(512)} %param.18) | copy-start | bytes 3844
  520.5 154.2 %copy-start.11 = (f32[512]{0:T(512)S(1)}, f32[512]{0:T(512)}, u32[]{:S(2)}) copy-start(f32[512]{0:T(512)} %param.22) | copy-start | bytes 6148
  520.5 154.2 %copy-start.12 = (f32[512]{0:T(512)S(1)}, f32[512]{0:T(512)}, u32[]{:S(2)}) copy-start(f32[512]{0:T(512)} %param.17) | copy-start | bytes 6148
  596.8 161.7 %copy-start.3 = (f32[512]{0:T(512)}, f32[512]{0:T(512)S(1)}, u32[]{:S(2)}) copy-start(f32[512]{0:T(512)S(1)} %multiply_add_fusion.8) | copy-start | bytes 6148
  596.8 161.7 %copy-start.4 = (f32[320]{0:T(512)}, f32[320]{0:T(512)S(1)}, u32[]{:S(2)}) copy-start(f32[320]{0:T(512)S(1)} %multiply_add_fusion.7) | copy-start | bytes 3844
  674.6 83.9 %copy-start.1 = (f32[320]{0:T(512)}, f32[320]{0:T(512)S(1)}, u32[]{:S(2)}) copy-start(f32[320]{0:T(512)S(1)} %get-tuple-element.37) | copy-start | bytes 3844
  674.6 83.9 %copy-start.5 = (f32[320]{0:T(512)}, f32[320]{0:T(512)S(1)}, u32[]{:S(2)}) copy-start(f32[320]{0:T(512)S(1)} %get-tuple-element.38) | copy-start | bytes 3844
  674.6 83.9 %copy-start.2 = (f32[512]{0:T(512)}, f32[512]{0:T(512)S(1)}, u32[]{:S(2)}) copy-start(f32[512]{0:T(512)S(1)} %get-tuple-element.39) | copy-start | bytes 6148
  674.7 83.9 %copy-start.6 = (f32[512]{0:T(512)}, f32[512]{0:T(512)S(1)}, u32[]{:S(2)}) copy-start(f32[512]{0:T(512)S(1)} %get-tuple-element.40) | copy-start | bytes 6148
Sparse Core Ops, SparseCore 0:
  11.2 51.2 all-gather.26
  65.6 48.1 all-gather.24
  116.9 48.1 all-gather.22
  168.0 48.1 all-gather.20
  218.6 52.5 reduce-scatter.8
  273.6 51.5 reduce-scatter.4
  327.5 49.8 all-gather.14
  379.7 40.3 all-gather.18
  422.4 50.1 all-gather.12
  474.2 40.3 all-gather.16
  518.5 85.1 reduce-scatter.10
  607.4 85.8 reduce-scatter.6
where the time goes:
time: 769 us; the launch traced here: 767 us
  waiting for transfers between devices  466 us (61%)
  blocking collectives  229 us (30%)
  matrix products  30.2 us (4%)
  between operations  17.3 us (2%)
  other arithmetic  17.2 us (2%)
    psum x2, blocking collectives, local(): lax.psum((jnp.sum(squares_gate, 1), jnp.sum(squares_lin, 1), jnp.sum(squa...  121 us
    reduce_scatter x2, waiting for transfers between devices, local(): lax.psum_scatter(jnp.concatenate([forward, backward], 1).astype(jnp.bfloa...  99.8 us
    all_gather x2, waiting for transfers between devices, local(): lax.all_gather(grad_pre_part, 'row', axis=0, tiled=True)  98.3 us
    all_gather x2, waiting for transfers between devices, local(): lax.all_gather(tokens[micro_index], 'col', axis=0, tiled=True)  97.5 us
    all_gather x2, waiting for transfers between devices, local(): lax.all_gather(cotangent[micro_index], 'col', axis=0, tiled=True)  94.4 us
    psum x1, blocking collectives, local(): lax.psum((jnp.sum(unit_gate * unit_gate), jnp.sum(unit_lin * unit_lin), j...  77.6 us
    all_gather x2, waiting for transfers between devices, local(): lax.all_gather(act_part, 'row', axis=0, tiled=True)  73.9 us
    psum x2, blocking collectives, local(): lax.psum((jnp.sum(squares_gate, 0), jnp.sum(squares_lin, 0), jnp.sum(squa...  30.3 us
  transfers between devices with their start and end apart: 12, of which 10 were waited for; matrix products, arithmetic and copies ran while one was open for 6% of the time, Pallas kernels for 0%

commit v1 on v0

v1 whole, which is shorter than its diff:
```python
import math

import jax
import jax.numpy as jnp
from jax import lax
from jax.experimental import pallas as pl
from jax.experimental.pallas import tpu as pltpu
from jax.sharding import Mesh
from jax.sharding import PartitionSpec as P

D = 4096
FF = 10240
NZ, NX, NY, NC = 8, 4, 4, 2
TOK = 512
GRP = 128
DB = D // NZ
FB = FF // (NX * NY * NC)

decay_rate = 0.8
gelu_coeff = math.sqrt(2.0 / math.pi)
COL = ("x", "y", "c")
ALL = ("z", "x", "y", "c")
VMEM = 48 * 1024 * 1024


def device(z, x, y, c):
    return ((z * NX + x) * NY + y) * NC + c


def token_moves():
    moves = []
    for z in range(NZ):
        for x in range(NX):
            for y in range(NY):
                for c in range(NC):
                    target = device(2 * x + c, (z // 2 + x) % NX, y, z % 2)
                    moves.append((device(z, x, y, c), target))
    return moves


MOVES = token_moves()
BACK = [(target, source) for source, target in MOVES]


def shifted(value, axis, step):
    return lax.ppermute(value, axis, [((i + step) % 4, i) for i in range(4)])


def partner(value, axis, size, bits):
    return lax.ppermute(value, axis, [(i, i ^ bits) for i in range(size)])


def swap(value):
    return partner(value, "c", 2, 1)


def gather4(value, axis):
    return jnp.stack([value] + [shifted(value, axis, step) for step in (1, 2, 3)], 0)


def sum4(value, axis):
    a = [value] + [partner(value, axis, 4, bits) for bits in (1, 2, 3)]
    return (a[0] + a[1]) + (a[2] + a[3])


def sum_col(value):
    value = value + swap(value)
    return sum4(sum4(value, "x"), "y")


def sum_z(value):
    a = [value] + [partner(value, "z", 8, bits) for bits in range(1, 8)]
    return ((a[0] + a[1]) + (a[2] + a[3])) + ((a[4] + a[5]) + (a[6] + a[7]))


def gelu_parts(value):
    inner = gelu_coeff * (value + 0.044715 * value * value * value)
    tangent = jnp.tanh(inner)
    gelu_value = 0.5 * value * (1.0 + tangent)
    gelu_slope = 0.5 * (1.0 + tangent) + 0.5 * value * (1.0 - tangent * tangent) * gelu_coeff * (
        1.0 + 3.0 * 0.044715 * value * value
    )
    return (gelu_value, gelu_slope)


def dot_nt(left, right):
    return lax.dot_general(
        left, right, (((1,), (1,)), ((), ())), preferred_element_type=jnp.float32
    )


def forward_kernel(order, tok0, tok1, cot0, cot1, weight, hidden_t, hidden, acc):
    i = pl.program_id(0)

    @pl.when(i == 0)
    def _():
        acc[...] = jnp.zeros_like(acc)

    def add(tok, cot):
        acc[: 2 * FB] += dot_nt(weight[0, : 2 * FB], tok[...].reshape(TOK, DB))
        acc[2 * FB :] += dot_nt(weight[0, 2 * FB :], cot[...].reshape(TOK, DB))

    @pl.when(i < 4)
    def _():
        add(tok0, cot0)

    @pl.when(i >= 4)
    def _():
        add(tok1, cot1)

    @pl.when(i == NZ - 1)
    def _():
        pre_gate = acc[:FB]
        pre_lin = acc[FB : 2 * FB]
        grad_act = acc[2 * FB :]
        gelu_value, gelu_slope = gelu_parts(pre_gate)
        gate = grad_act * pre_lin * gelu_slope
        lin = grad_act * gelu_value
        hidden_t[:FB] = gate.astype(jnp.bfloat16)
        hidden_t[FB : 2 * FB] = lin.astype(jnp.bfloat16)
        hidden_t[2 * FB :] = (gelu_value * pre_lin).astype(jnp.bfloat16)
        hidden[...] = hidden_t[: 2 * FB].T


def weight_grad_kernel(order, tok0, tok1, cot0, cot1, hidden_t, grad):
    i = pl.program_id(0)

    def emit(tok, cot):
        grad[0, : 2 * FB] = jnp.dot(
            hidden_t[: 2 * FB], tok[...].reshape(TOK, DB), preferred_element_type=jnp.float32
        ).astype(jnp.bfloat16)
        grad[0, 2 * FB :] = jnp.dot(
            hidden_t[2 * FB :], cot[...].reshape(TOK, DB), preferred_element_type=jnp.float32
        ).astype(jnp.bfloat16)

    @pl.when(i < 4)
    def _():
        emit(tok0, cot0)

    @pl.when(i >= 4)
    def _():
        emit(tok1, cot1)


def token_grad_kernel(order, hidden, weight, grad):
    product = jnp.dot(hidden[...], weight[0], preferred_element_type=jnp.float32)
    product = product.astype(jnp.bfloat16)
    for shift in range(4):
        grad[0, 0, order[12 + shift]] = product[shift * GRP : (shift + 1) * GRP]


def block_specs():
    tok0 = pl.BlockSpec((4, 1, GRP, DB), lambda i, o: (0, jnp.minimum(i, 3), 0, 0))
    tok1 = pl.BlockSpec((4, 1, GRP, DB), lambda i, o: (0, jnp.maximum(i - 4, 0), 0, 0))
    cot0 = pl.BlockSpec((1, 4, GRP, DB), lambda i, o: (jnp.minimum(i, 3), 0, 0, 0))
    cot1 = pl.BlockSpec((1, 4, GRP, DB), lambda i, o: (jnp.maximum(i - 4, 0), 0, 0, 0))
    return [tok0, tok1, cot0, cot1]


def forward(order, blocks, weight):
    return pl.pallas_call(
        forward_kernel,
        grid_spec=pltpu.PrefetchScalarGridSpec(
            num_scalar_prefetch=1,
            grid=(NZ,),
            in_specs=block_specs() + [pl.BlockSpec((1, 3 * FB, DB), lambda i, o: (o[i], 0, 0))],
            out_specs=[
                pl.BlockSpec((3 * FB, TOK), lambda i, o: (0, 0)),
                pl.BlockSpec((TOK, 2 * FB), lambda i, o: (0, 0)),
            ],
            scratch_shapes=[pltpu.VMEM((3 * FB, TOK), jnp.float32)],
        ),
        out_shape=[
            jax.ShapeDtypeStruct((3 * FB, TOK), jnp.bfloat16),
            jax.ShapeDtypeStruct((TOK, 2 * FB), jnp.bfloat16),
        ],
        compiler_params=pltpu.CompilerParams(vmem_limit_bytes=VMEM),
        cost_estimate=pl.CostEstimate(
            flops=2 * 3 * FB * TOK * D, bytes_accessed=17000000, transcendentals=FB * TOK
        ),
    )(order, *blocks, weight)


def weight_grad(order, blocks, hidden_t):
    return pl.pallas_call(
        weight_grad_kernel,
        grid_spec=pltpu.PrefetchScalarGridSpec(
            num_scalar_prefetch=1,
            grid=(NZ,),
            in_specs=block_specs() + [pl.BlockSpec((3 * FB, TOK), lambda i, o: (0, 0))],
            out_specs=pl.BlockSpec((1, 3 * FB, DB), lambda i, o: (o[i], 0, 0)),
        ),
        out_shape=jax.ShapeDtypeStruct((NZ, 3 * FB, DB), jnp.bfloat16),
        compiler_params=pltpu.CompilerParams(vmem_limit_bytes=VMEM),
        cost_estimate=pl.CostEstimate(
            flops=2 * 3 * FB * TOK * D, bytes_accessed=17000000, transcendentals=0
        ),
    )(order, *blocks, hidden_t)


def token_grad(order, hidden, weight):
    return pl.pallas_call(
        token_grad_kernel,
        grid_spec=pltpu.PrefetchScalarGridSpec(
            num_scalar_prefetch=1,
            grid=(NZ,),
            in_specs=[
                pl.BlockSpec((TOK, 2 * FB), lambda i, o: (0, 0)),
                pl.BlockSpec((1, 2 * FB, DB), lambda i, o: (o[i], 0, 0)),
            ],
            out_specs=pl.BlockSpec((1, 1, 4, GRP, DB), lambda i, o: (i // 4, o[8 + i % 4], 0, 0, 0)),
        ),
        out_shape=jax.ShapeDtypeStruct((2, 4, 4, GRP, DB), jnp.bfloat16),
        compiler_params=pltpu.CompilerParams(vmem_limit_bytes=VMEM),
        cost_estimate=pl.CostEstimate(
            flops=2 * 2 * FB * TOK * D, bytes_accessed=10000000, transcendentals=0
        ),
    )(order, hidden, weight)


def local(
    tokens,
    cotangent,
    wi_gate,
    wi_lin,
    wo,
    rows_gate,
    cols_gate,
    rows_lin,
    cols_lin,
    rows_out,
    cols_out,
    rate,
):
    bf16 = jnp.bfloat16
    z, x, y, c = (lax.axis_index(axis) for axis in ALL)
    weight = lax.all_gather(jnp.concatenate([wi_gate.T, wi_lin.T, wo], 0), "z", axis=0)

    pair = jnp.stack([tokens.reshape(GRP, DB), cotangent.reshape(GRP, DB)], 0)
    pair = lax.ppermute(pair, ALL, MOVES)
    tok0 = gather4(gather4(pair[0], "x"), "y")
    cot0 = gather4(gather4(pair[1], "y"), "x")
    blocks = [tok0, swap(tok0), cot0, swap(cot0)]
    shift = jnp.arange(4, dtype=jnp.int32)
    high = (x + shift - z // 2 + NX) % NX
    order = jnp.concatenate(
        [2 * high + c, 2 * high + (1 - c), (x + shift) % NX, (y + shift) % NY]
    ).astype(jnp.int32)

    hidden_t, hidden = forward(order, blocks, weight)
    grad_w = lax.psum_scatter(weight_grad(order, blocks, hidden_t), "z", scatter_dimension=0)

    part = token_grad(order, hidden, weight)
    part = (part[0].astype(jnp.float32) + swap(part[1]).astype(jnp.float32)).astype(bf16)
    part = part.reshape(NX * NY, GRP, DB)
    part = lax.all_to_all(part, ("x", "y"), 0, 0, tiled=True)
    part = jnp.sum(part.astype(jnp.float32), 0).astype(bf16)
    grad_tokens = lax.ppermute(part, ALL, BACK).reshape(tokens.shape)

    grad = grad_w.astype(jnp.float32) * (1.0 / math.sqrt(4096.0))
    keep = 1.0 - decay_rate
    squares = grad * grad + 1e-30
    over_model = sum_z(jnp.sum(squares, 1))
    hidden_old = jnp.concatenate([cols_gate, cols_lin, rows_out])
    hidden_new = decay_rate * hidden_old + keep * over_model / D
    model_old = jnp.stack([rows_gate, rows_lin, cols_out], 0)
    weighted = grad * grad / hidden_new[:, None]
    over_hidden = sum_col(
        jnp.concatenate(
            [
                jnp.sum(squares.reshape(3, FB, DB), 1),
                jnp.sum(weighted.reshape(3, FB, DB), 1),
            ],
            0,
        )
    )
    model_new = decay_rate * model_old + keep * over_hidden[:3] / FF
    totals = sum_z(jnp.sum(over_hidden[3:] / model_new, 1, keepdims=True))
    factor = -rate[0] / jnp.sqrt(totals / (D * FF) + 1e-06)
    update = (
        grad.reshape(3, FB, DB)
        * lax.rsqrt(hidden_new).reshape(3, FB, 1)
        * (factor * lax.rsqrt(model_new)).reshape(3, 1, DB)
    )
    return (
        grad_tokens,
        update[0].T,
        update[1].T,
        update[2],
        model_new[0],
        hidden_new[:FB],
        model_new[1],
        hidden_new[FB : 2 * FB],
        hidden_new[2 * FB :],
        model_new[2],
    )


def solution(mesh):
    fine = Mesh(mesh.devices.reshape(NZ, NX, NY, NC), ALL)
    return jax.shard_map(
        local,
        mesh=fine,
        in_specs=(
            P(None, COL, "z"),
            P(None, COL, "z"),
            P("z", COL),
            P("z", COL),
            P(COL, "z"),
            P("z"),
            P(COL),
            P("z"),
            P(COL),
            P(COL),
            P("z"),
            P(),
        ),
        out_specs=(
            P(None, COL, "z"),
            P("z", COL),
            P("z", COL),
            P(COL, "z"),
            P("z"),
            P(COL),
            P("z"),
            P(COL),
            P(COL),
            P("z"),
        ),
        check_vma=False,
    )
```

time: 769 us -> 296 us (0.38)
  waiting for transfers between devices: 466 us -> 138 us
  blocking collectives: 229 us -> 0 us
  starting transfers between devices: 0.66 us -> 92.4 us
  Pallas kernels: 0 us -> 30.6 us
  matrix products: 30.2 us -> 0 us
    all_gather x8 -> x1, waiting for transfers between devices: 364 us -> 10.4 us  [local(): lax.all_gather(jnp.concatenate([wi_gate.T, wi_lin.T, wo], 0), 'z', axis=0)]
    psum x5 -> x0, blocking collectives: 229 us -> none  [the longest x2 121 us: local(): lax.psum((jnp.sum(squares_gate, 1), jnp.sum(squares_lin, 1), jnp.sum(squa...]
    ppermute x0 -> x38, starting transfers between devices: none -> 86.4 us  [the longest x12 45.2 us: shifted(): return lax.ppermute(value, axis, [((i + step) % 4, i) for i in range(4)])]
    ppermute x0 -> x38, waiting for transfers between devices: none -> 56.2 us  [the longest x12 37.4 us: shifted(): return lax.ppermute(value, axis, [((i + step) % 4, i) for i in range(4)])]
    pallas_call x0 -> x3, Pallas kernels: none -> 30.6 us  [the longest x1 11.6 us: forward(): pl.pallas_call(forward_kernel, grid_spec=pltpu.PrefetchScalarGridSpec(num...]
    dot_general x10 -> x0, matrix products: 30.2 us -> none  [the longest x4 14.7 us: contract_cols(): lax.dot_general(left, right, (((1,), (1,)), ((), ())), preferred_element_...]
    reduce_scatter x4 -> x1, waiting for transfers between devices: 99.9 us -> 71.5 us  [local(): lax.psum_scatter(weight_grad(order, blocks, hidden_t), 'z', scatter_dimen...]
  transfers between devices with their start and end apart: 12 -> 41, of which waited for: 10 -> 21; matrix products, arithmetic and copies ran while one was open for 6% -> 4% of each run, Pallas kernels for 0% -> 3%
where the time goes in v1:
time: 296 us; the launch traced here: 293 us
  waiting for transfers between devices  138 us (47%)
  starting transfers between devices  92.4 us (31%)
  Pallas kernels  30.6 us (10%)
  between operations  15 us (5%)
  other arithmetic  13.5 us (5%)
  local copies, waits for them, and re-layouts  3.63 us (1%)
    reduce_scatter x1, waiting for transfers between devices, local(): lax.psum_scatter(weight_grad(order, blocks, hidden_t), 'z', scatter_dimen...  71.5 us
    ppermute x12, starting transfers between devices, shifted(): return lax.ppermute(value, axis, [((i + step) % 4, i) for i in range(4)])  45.2 us
    ppermute x24, starting transfers between devices, partner(): return lax.ppermute(value, axis, [(i, i ^ bits) for i in range(size)])  39.9 us
    ppermute x12, waiting for transfers between devices, shifted(): return lax.ppermute(value, axis, [((i + step) % 4, i) for i in range(4)])  37.4 us
    ppermute x24, waiting for transfers between devices, partner(): return lax.ppermute(value, axis, [(i, i ^ bits) for i in range(size)])  18.8 us
    pallas_call x1, Pallas kernels, forward(): pl.pallas_call(forward_kernel, grid_spec=pltpu.PrefetchScalarGridSpec(num...  11.6 us
    pallas_call x1, Pallas kernels, weight_grad(): pl.pallas_call(weight_grad_kernel, grid_spec=pltpu.PrefetchScalarGridSpec...  11 us
    all_gather x1, waiting for transfers between devices, local(): lax.all_gather(jnp.concatenate([wi_gate.T, wi_lin.T, wo], 0), 'z', axis=0)  10.4 us
  transfers between devices with their start and end apart: 41, of which 21 were waited for; matrix products, arithmetic and copies ran while one was open for 4% of the time, Pallas kernels for 3%

profile of v1, /device:TPU:8, one launch (start us, length us, event | category | flops | bytes accessed | tf_op | source)
XLA Modules:
  0.0 293.1 jit_solution(9971695632404311857)
XLA Ops:
  7.2 2.3 pad_maximum_fusion.2
  9.7 0.7 collective-permute-start
  10.4 30.2 %collective-permute-start.3 = (bf16[128,512]{1,0:T(8,128)(2,1)S(1)}, bf16[128,512]{1,0:T(8,128)(2,1)S(1)}, u32[]{:S(2)}, u32[]{:S(2)}) collective-permute-start(bf16[128,512]{1,0:T(8,128)(2,1)S(1)} %get-tuple-element.29), channel_id=1, source_target_pairs={{24,0},{0,8},{8,16},{16,24},{25,1},{1,9},{9,17},{17,25},{26,2},{2,... | collective-permute-start | bytes 393224 | tf_op jit(solution)/shard_map/ppermute | solution.py:46
  40.6 4.2 %collective-permute-start.2 = (bf16[128,512]{1,0:T(8,128)(2,1)S(1)}, bf16[128,512]{1,0:T(8,128)(2,1)S(1)}, u32[]{:S(2)}, u32[]{:S(2)}) collective-permute-start(bf16[128,512]{1,0:T(8,128)(2,1)S(1)} %get-tuple-element.29), channel_id=1, source_target_pairs={{16,0},{24,8},{0,16},{8,24},{17,1},{25,9},{1,17},{9,25},{18,2},{26... | collective-permute-start | bytes 393224 | tf_op jit(solution)/shard_map/ppermute | solution.py:46
  44.8 2.0 collective-permute-done.3
  46.8 3.4 %collective-permute-done.2 = bf16[128,512]{1,0:T(8,128)(2,1)S(1)} collective-permute-done((bf16[128,512]{1,0:T(8,128)(2,1)S(1)}, bf16[128,512]{1,0:T(8,128)(2,1)S(1)}, u32[]{:S(2)}, u32[]{:S(2)}) %collective-permute-start.2) | collective-permute-done | bytes 131104 | tf_op jit(solution)/shard_map/ppermute | solution.py:46
  50.3 1.7 collective-permute-start.6
  52.0 1.3 collective-permute-start.10
  53.3 1.2 collective-permute-start.9
  54.5 1.1 collective-permute-start.8
  55.6 1.4 collective-permute-start.5
  56.9 11.1 %collective-permute-done.10 = bf16[128,512]{1,0:T(8,128)(2,1)S(1)} collective-permute-done((bf16[128,512]{1,0:T(8,128)(2,1)S(1)}, bf16[128,512]{1,0:T(8,128)(2,1)S(1)}, u32[]{:S(2)}, u32[]{:S(2)}) %collective-permute-start.10) | collective-permute-done | bytes 131104 | tf_op jit(solution)/shard_map/ppermute | solution.py:46
  68.1 0.5 collective-permute-start.4
  68.8 3.6 %collective-permute-start.12 = (bf16[4,128,512]{2,1,0:T(8,128)(2,1)S(1)}, bf16[4,128,512]{2,1,0:T(8,128)(2,1)S(1)}, u32[]{:S(2)}, u32[]{:S(2)}) collective-permute-start(bf16[4,128,512]{2,1,0:T(8,128)(2,1)S(1)} %get-tuple-element.25), channel_id=1, source_target_pairs={{16,0},{24,8},{0,16},{8,24},{17,1},{25,9},{1,17},{9,25},{18,2},{26... | collective-permute-start | bytes 1572872 | tf_op jit(solution)/shard_map/ppermute | solution.py:46
  72.4 2.9 collective-permute-done.5
  75.3 13.3 %collective-permute-done.4 = bf16[4,128,512]{2,1,0:T(8,128)(2,1)S(1)} collective-permute-done((bf16[4,128,512]{2,1,0:T(8,128)(2,1)S(1)}, bf16[4,128,512]{2,1,0:T(8,128)(2,1)S(1)}, u32[]{:S(2)}, u32[]{:S(2)}) %collective-permute-start.4) | collective-permute-done | bytes 524320 | tf_op jit(solution)/shard_map/ppermute | solution.py:46
  88.6 0.3 pad_maximum_fusion.tok0
  89.0 4.6 %collective-permute-done.12 = bf16[4,128,512]{2,1,0:T(8,128)(2,1)S(1)} collective-permute-done((bf16[4,128,512]{2,1,0:T(8,128)(2,1)S(1)}, bf16[4,128,512]{2,1,0:T(8,128)(2,1)S(1)}, u32[]{:S(2)}, u32[]{:S(2)}) %collective-permute-start.12) | collective-permute-done | bytes 524320 | tf_op jit(solution)/shard_map/ppermute | solution.py:46
  93.6 1.6 pad_maximum_fusion.1.cot0
  95.3 4.4 %collective-permute-done.14.cot1 = bf16[4,4,128,512]{3,2,1,0:T(8,128)(2,1)} collective-permute-done((bf16[4,4,128,512]{3,2,1,0:T(8,128)(2,1)}, bf16[4,4,128,512]{3,2,1,0:T(8,128)(2,1)}, u32[]{:S(2)}, u32[]{:S(2)}) %collective-permute-start.14) | collective-permute-done | bytes 2097184 | tf_op jit(solution)/shard_map/ppermute | solution.py:50
  99.6 10.4 %all-gather.3.cloned.1.call-done = bf16[7680,512]{1,0:T(8,128)(2,1)} async-done(((bf16[960,512]{1,0:T(8,128)(2,1)}), bf16[7680,512]{1,0:T(8,128)(2,1)}) %all-gather.3.cloned.1.call-update) | async-done | bytes 7864336 | tf_op jit(solution)/shard_map/all_gather | solution.py:237
  110.0 11.6 %shard_map.195 = (bf16[960,512]{1,0:T(8,128)(2,1)S(1)}, bf16[512,640]{1,0:T(8,128)(2,1)S(1)}) custom-call(s32[16]{0:T(128)S(1)} %pad_add_fusion.order, bf16[4,4,128,512]{3,2,1,0:T(8,128)(2,1)S(1)} %pad_maximum_fusion.tok0, bf16[4,4,128,512]{3,2,1,0:T(8,128)(2,1)} %collective-permute-done.7.tok1, bf16[4,4,128,512]{3,2,1,0:T(8,128)(2,1)} %pad_maximum_fusion.1.cot0, ...), custom_call_target="tpu_custom_call" | custom-call | flops 4026531840 | bytes 17000000 | tf_op jit(solution)/shard_map/pallas_call | solution.py:161
  121.6 11.0 %shard_map.197 = bf16[8,960,512]{2,1,0:T(8,128)(2,1)} custom-call(s32[16]{0:T(128)S(1)} %pad_add_fusion.order, bf16[4,4,128,512]{3,2,1,0:T(8,128)(2,1)S(1)} %pad_maximum_fusion.tok0, bf16[4,4,128,512]{3,2,1,0:T(8,128)(2,1)} %collective-permute-done.7.tok1, bf16[4,4,128,512]{3,2,1,0:T(8,128)(2,1)} %pad_maximum_fusion.1.cot0, ...), custom_call_target="tpu_custom_call" | custom-call | flops 4026531840 | bytes 17000000 | tf_op jit(solution)/shard_map/pallas_call | solution.py:185
  132.6 8.0 %shard_map.196 = bf16[2,4,4,128,512]{4,3,2,1,0:T(8,128)(2,1)S(1)} custom-call(s32[16]{0:T(128)S(1)} %pad_add_fusion.order, bf16[512,640]{1,0:T(8,128)(2,1)S(1)} %get-tuple-element.12.hidden, bf16[8,960,512]{2,1,0:T(8,128)(2,1)} %bitcast.58), custom_call_target="tpu_custom_call" | custom-call | flops 2684354560 | bytes 10000000 | tf_op jit(solution)/shard_map/pallas_call | solution.py:202
  140.6 0.2 slice_bitcast_fusion
  141.0 4.1 %collective-permute-done.15 = bf16[4,4,128,512]{3,2,1,0:T(8,128)(2,1)S(1)} collective-permute-done((bf16[4,4,128,512]{3,2,1,0:T(8,128)(2,1)S(1)}, bf16[4,4,128,512]{3,2,1,0:T(8,128)(2,1)S(1)}, u32[]{:S(2)}, u32[]{:S(2)}) %collective-permute-start.15) | collective-permute-done | bytes 2097184 | tf_op jit(solution)/shard_map/ppermute | solution.py:50
  145.1 2.0 fusion
  147.1 5.9 %all-to-all-start = ((bf16[16,128,512]{2,1,0:T(8,128)(2,1)}), bf16[16,128,512]{2,1,0:T(8,128)(2,1)S(1)}, u32[]{:S(2)}, u32[]{:S(2)}) async-start(bf16[16,128,512]{2,1,0:T(8,128)(2,1)} %bitcast.23), calls=%async_computation | async-start | bytes 4194304 | tf_op jit(solution)/shard_map/all_to_all | solution.py:256
  153.0 71.5 %reduce-scatter.2.cloned.1.call-done = bf16[1,960,512]{2,1,0:T(8,128)(2,1)} async-done(((bf16[8,960,512]{2,1,0:T(8,128)(2,1)}), bf16[1,960,512]{2,1,0:T(8,128)(2,1)}) %reduce-scatter.2.cloned.1.call-update) | async-done | bytes 983056 | tf_op jit(solution)/shard_map/reduce_scatter | solution.py:251
  224.5 1.6 add_reduce_fusion.1
  226.1 2.3 collective-permute-start.22
  228.4 0.3 collective-permute-start.23
  228.7 4.6 %collective-permute-start.20 = (f32[960]{0:T(1024)S(1)}, f32[960]{0:T(1024)S(1)}, u32[]{:S(2)}, u32[]{:S(2)}) collective-permute-start(f32[960]{0:T(1024)S(1)} %add_reduce_fusion.1), channel_id=1, source_target_pairs={{0,128},{32,160},{64,192},{96,224},{128,0},{160,32},{192,64},{224,... | collective-permute-start | bytes 11528 | tf_op jit(solution)/shard_map/ppermute | solution.py:50
  233.3 2.9 %collective-permute-start.21 = (f32[960]{0:T(1024)S(1)}, f32[960]{0:T(1024)S(1)}, u32[]{:S(2)}, u32[]{:S(2)}) collective-permute-start(f32[960]{0:T(1024)S(1)} %add_reduce_fusion.1), channel_id=1, source_target_pairs={{0,160},{32,128},{64,224},{96,192},{128,32},{160,0},{192,96},{224,... | collective-permute-start | bytes 11528 | tf_op jit(solution)/shard_map/ppermute | solution.py:50
  236.3 3.0 %collective-permute-start.19 = (f32[960]{0:T(1024)S(1)}, f32[960]{0:T(1024)S(1)}, u32[]{:S(2)}, u32[]{:S(2)}) collective-permute-start(f32[960]{0:T(1024)S(1)} %add_reduce_fusion.1), channel_id=1, source_target_pairs={{0,96},{32,64},{64,32},{96,0},{128,224},{160,192},{192,160},{224,1... | collective-permute-start | bytes 11528 | tf_op jit(solution)/shard_map/ppermute | solution.py:50
  239.3 0.7 collective-permute-start.17
  239.9 0.8 collective-permute-done.18
  240.8 0.9 collective-permute-done.19
  241.7 1.2 collective-permute-done.17
  243.0 3.0 %add_reduce_fusion = (f32[3,512]{1,0:T(4,128)S(1)}, f32[3,512]{1,0:T(4,128)S(1)}, f32[3,320,512]{2,1,0:T(8,128)}) fusion(f32[3,320]{1,0:T(4,128)S(1)} %div.52, bf16[3,320,512]{2,1,0:T(8,128)(2,1)} %bitcast.59), kind=kLoop, calls=%fused_computation.6 | loop fusion | flops 3437568 | bytes 2965248 | tf_op jit(solution)/shard_map/reduce_sum | solution.py:271
  246.2 0.3 reduce_sum.48
  246.5 0.7 collective-permute-start.16
  247.2 0.2 collective-permute-done.24
  247.4 7.0 %collective-permute-start.26 = (f32[6,512]{1,0:T(8,128)S(1)}, f32[6,512]{1,0:T(8,128)S(1)}, u32[]{:S(2)}, u32[]{:S(2)}) collective-permute-start(f32[6,512]{1,0:T(8,128)S(1)} %fusion.8), channel_id=1, source_target_pairs={{0,16},{8,24},{16,0},{24,8},{1,17},{9,25},{17,1},{25,9},{2,18},{10... | collective-permute-start | bytes 36872 | tf_op jit(solution)/shard_map/ppermute | solution.py:50
  254.4 0.3 collective-permute-start.27
  255.3 0.8 collective-permute-done.26
  256.1 3.2 %collective-permute-done.27 = f32[6,512]{1,0:T(8,128)S(1)} collective-permute-done((f32[6,512]{1,0:T(8,128)S(1)}, f32[6,512]{1,0:T(8,128)S(1)}, u32[]{:S(2)}, u32[]{:S(2)}) %collective-permute-start.27) | collective-permute-done | bytes 12320 | tf_op jit(solution)/shard_map/ppermute | solution.py:50
  259.4 2.2 collective-permute-start.29
  261.6 2.6 collective-permute-start.28
  264.1 0.7 fusion.15
  264.9 0.4 collective-permute-done.30
  265.3 0.6 collective-permute-done.28
  266.0 3.4 %collective-permute-start.36 = (f32[3,1]{0,1:T(1,128)S(1)}, f32[3,1]{0,1:T(1,128)S(1)}, u32[]{:S(2)}, u32[]{:S(2)}) collective-permute-start(f32[3,1]{0,1:T(1,128)S(1)} %bitcast.77), channel_id=1, source_target_pairs={{0,192},{32,224},{64,128},{96,160},{128,64},{160,96},{192,0},{224,... | collective-permute-start | bytes 44 | tf_op jit(solution)/shard_map/ppermute | solution.py:50
  269.4 3.7 %collective-permute-start.34 = (f32[3,1]{0,1:T(1,128)S(1)}, f32[3,1]{0,1:T(1,128)S(1)}, u32[]{:S(2)}, u32[]{:S(2)}) collective-permute-start(f32[3,1]{0,1:T(1,128)S(1)} %bitcast.79), channel_id=1, source_target_pairs={{0,128},{32,160},{64,192},{96,224},{128,0},{160,32},{192,64},{224,... | collective-permute-start | bytes 44 | tf_op jit(solution)/shard_map/ppermute | solution.py:50
  273.2 3.0 %collective-permute-start.35 = (f32[3,1]{0,1:T(1,128)S(1)}, f32[3,1]{0,1:T(1,128)S(1)}, u32[]{:S(2)}, u32[]{:S(2)}) collective-permute-start(f32[3,1]{0,1:T(1,128)S(1)} %bitcast.80), channel_id=1, source_target_pairs={{0,160},{32,128},{64,224},{96,192},{128,32},{160,0},{192,96},{224,... | collective-permute-start | bytes 44 | tf_op jit(solution)/shard_map/ppermute | solution.py:50
  276.2 0.6 fusion.14
  276.8 2.1 collective-permute-start.33
  278.9 1.4 collective-permute-start.31
  280.3 0.3 collective-permute-done.32
  280.6 1.5 collective-permute-done.33
  282.1 0.3 collective-permute-done.31
  282.5 1.8 multiply_multiply_fusion.1
  284.3 1.3 slice_bitcast_fusion.2
  285.6 0.7 copy.24
  (69 shorter events, 1.5 us)
Async XLA Ops:
  7.2 2.5 copy-start
  7.2 2.5 copy-start.1
  7.2 102.8 %all-gather.3.cloned.1.call-start = ((), (), s32[]{:S(2)}) async-start(), calls=%async_computation.3 | async-start | bytes 8847360 | tf_op jit(solution)/shard_map/all_gather | solution.py:237
  9.6 214.9 %reduce-scatter.2.cloned.1.call-start = ((), (), s32[]{:S(2)}) async-start(), calls=%async_computation.2 | async-start | bytes 8847360 | tf_op jit(solution)/shard_map/reduce_scatter | solution.py:251
  9.7 0.7 collective-permute-start
  10.4 36.4 %collective-permute-start.3 = (bf16[128,512]{1,0:T(8,128)(2,1)S(1)}, bf16[128,512]{1,0:T(8,128)(2,1)S(1)}, u32[]{:S(2)}, u32[]{:S(2)}) collective-permute-start(bf16[128,512]{1,0:T(8,128)(2,1)S(1)} %get-tuple-element.29), channel_id=1, source_target_pairs={{24,0},{0,8},{8,16},{16,24},{25,1},{1,9},{9,17},{17,25},{26,2},{2,... | collective-permute-start | bytes 393224 | tf_op jit(solution)/shard_map/ppermute | solution.py:46
  40.6 9.6 %collective-permute-start.2 = (bf16[128,512]{1,0:T(8,128)(2,1)S(1)}, bf16[128,512]{1,0:T(8,128)(2,1)S(1)}, u32[]{:S(2)}, u32[]{:S(2)}) collective-permute-start(bf16[128,512]{1,0:T(8,128)(2,1)S(1)} %get-tuple-element.29), channel_id=1, source_target_pairs={{16,0},{24,8},{0,16},{8,24},{17,1},{25,9},{1,17},{9,25},{18,2},{26... | collective-permute-start | bytes 393224 | tf_op jit(solution)/shard_map/ppermute | solution.py:46
  44.8 5.5 %collective-permute-start.1 = (bf16[128,512]{1,0:T(8,128)(2,1)S(1)}, bf16[128,512]{1,0:T(8,128)(2,1)S(1)}, u32[]{:S(2)}, u32[]{:S(2)}) collective-permute-start(bf16[128,512]{1,0:T(8,128)(2,1)S(1)} %get-tuple-element.29), channel_id=1, source_target_pairs={{8,0},{16,8},{24,16},{0,24},{9,1},{17,9},{25,17},{1,25},{10,2},{18... | collective-permute-start | bytes 393224 | tf_op jit(solution)/shard_map/ppermute | solution.py:46
  50.3 22.1 %collective-permute-start.6 = (bf16[4,128,512]{2,1,0:T(8,128)(2,1)S(1)}, bf16[4,128,512]{2,1,0:T(8,128)(2,1)S(1)}, u32[]{:S(2)}, u32[]{:S(2)}) collective-permute-start(bf16[4,128,512]{2,1,0:T(8,128)(2,1)S(1)} %get-tuple-element.27), channel_id=1, source_target_pairs={{6,0},{0,2},{2,4},{4,6},{7,1},{1,3},{3,5},{5,7},{14,8},{8,10},{10,... | collective-permute-start | bytes 1572872 | tf_op jit(solution)/shard_map/ppermute | solution.py:46
  52.0 16.1 %collective-permute-start.10 = (bf16[128,512]{1,0:T(8,128)(2,1)S(1)}, bf16[128,512]{1,0:T(8,128)(2,1)S(1)}, u32[]{:S(2)}, u32[]{:S(2)}) collective-permute-start(bf16[128,512]{1,0:T(8,128)(2,1)S(1)} %get-tuple-element.30), channel_id=1, source_target_pairs={{6,0},{0,2},{2,4},{4,6},{7,1},{1,3},{3,5},{5,7},{14,8},{8,10},{10,... | collective-permute-start | bytes 393224 | tf_op jit(solution)/shard_map/ppermute | solution.py:46
  53.3 15.4 %collective-permute-start.9 = (bf16[128,512]{1,0:T(8,128)(2,1)S(1)}, bf16[128,512]{1,0:T(8,128)(2,1)S(1)}, u32[]{:S(2)}, u32[]{:S(2)}) collective-permute-start(bf16[128,512]{1,0:T(8,128)(2,1)S(1)} %get-tuple-element.30), channel_id=1, source_target_pairs={{4,0},{6,2},{0,4},{2,6},{5,1},{7,3},{1,5},{3,7},{12,8},{14,10},{8,... | collective-permute-start | bytes 393224 | tf_op jit(solution)/shard_map/ppermute | solution.py:46
  54.5 14.1 %collective-permute-start.8 = (bf16[128,512]{1,0:T(8,128)(2,1)S(1)}, bf16[128,512]{1,0:T(8,128)(2,1)S(1)}, u32[]{:S(2)}, u32[]{:S(2)}) collective-permute-start(bf16[128,512]{1,0:T(8,128)(2,1)S(1)} %get-tuple-element.30), channel_id=1, source_target_pairs={{2,0},{4,2},{6,4},{0,6},{3,1},{5,3},{7,5},{1,7},{10,8},{12,10},{14... | collective-permute-start | bytes 393224 | tf_op jit(solution)/shard_map/ppermute | solution.py:46
  55.6 19.7 %collective-permute-start.5 = (bf16[4,128,512]{2,1,0:T(8,128)(2,1)S(1)}, bf16[4,128,512]{2,1,0:T(8,128)(2,1)S(1)}, u32[]{:S(2)}, u32[]{:S(2)}) collective-permute-start(bf16[4,128,512]{2,1,0:T(8,128)(2,1)S(1)} %get-tuple-element.27), channel_id=1, source_target_pairs={{4,0},{6,2},{0,4},{2,6},{5,1},{7,3},{1,5},{3,7},{12,8},{14,10},{8,... | collective-permute-start | bytes 1572872 | tf_op jit(solution)/shard_map/ppermute | solution.py:46
  68.1 20.5 %collective-permute-start.4 = (bf16[4,128,512]{2,1,0:T(8,128)(2,1)S(1)}, bf16[4,128,512]{2,1,0:T(8,128)(2,1)S(1)}, u32[]{:S(2)}, u32[]{:S(2)}) collective-permute-start(bf16[4,128,512]{2,1,0:T(8,128)(2,1)S(1)} %get-tuple-element.27), channel_id=1, source_target_pairs={{2,0},{4,2},{6,4},{0,6},{3,1},{5,3},{7,5},{1,7},{10,8},{12,10},{14... | collective-permute-start | bytes 1572872 | tf_op jit(solution)/shard_map/ppermute | solution.py:46
  68.7 20.3 %collective-permute-start.13 = (bf16[4,128,512]{2,1,0:T(8,128)(2,1)S(1)}, bf16[4,128,512]{2,1,0:T(8,128)(2,1)S(1)}, u32[]{:S(2)}, u32[]{:S(2)}) collective-permute-start(bf16[4,128,512]{2,1,0:T(8,128)(2,1)S(1)} %get-tuple-element.25), channel_id=1, source_target_pairs={{24,0},{0,8},{8,16},{16,24},{25,1},{1,9},{9,17},{17,25},{26,2},{2,... | collective-permute-start | bytes 1572872 | tf_op jit(solution)/shard_map/ppermute | solution.py:46
  68.8 24.7 %collective-permute-start.12 = (bf16[4,128,512]{2,1,0:T(8,128)(2,1)S(1)}, bf16[4,128,512]{2,1,0:T(8,128)(2,1)S(1)}, u32[]{:S(2)}, u32[]{:S(2)}) collective-permute-start(bf16[4,128,512]{2,1,0:T(8,128)(2,1)S(1)} %get-tuple-element.25), channel_id=1, source_target_pairs={{16,0},{24,8},{0,16},{8,24},{17,1},{25,9},{1,17},{9,25},{18,2},{26... | collective-permute-start | bytes 1572872 | tf_op jit(solution)/shard_map/ppermute | solution.py:46
  72.4 21.1 %collective-permute-start.11 = (bf16[4,128,512]{2,1,0:T(8,128)(2,1)S(1)}, bf16[4,128,512]{2,1,0:T(8,128)(2,1)S(1)}, u32[]{:S(2)}, u32[]{:S(2)}) collective-permute-start(bf16[4,128,512]{2,1,0:T(8,128)(2,1)S(1)} %get-tuple-element.25), channel_id=1, source_target_pairs={{8,0},{16,8},{24,16},{0,24},{9,1},{17,9},{25,17},{1,25},{10,2},{18... | collective-permute-start | bytes 1572872 | tf_op jit(solution)/shard_map/ppermute | solution.py:46
  88.9 6.4 %collective-permute-start.7 = (bf16[4,4,128,512]{3,2,1,0:T(8,128)(2,1)S(1)}, bf16[4,4,128,512]{3,2,1,0:T(8,128)(2,1)}, u32[]{:S(2)}, u32[]{:S(2)}) collective-permute-start(bf16[4,4,128,512]{3,2,1,0:T(8,128)(2,1)S(1)} %pad_maximum_fusion.tok0), channel_id=1, source_target_pairs={{0,1},{1,0},{2,3},{3,2},{4,5},{5,4},{6,7},{7,6},{8,9},{9,8},{10,11... | collective-permute-start | bytes 6291464 | tf_op jit(solution)/shard_map/ppermute | solution.py:50
  95.1 4.5 %collective-permute-start.14 = (bf16[4,4,128,512]{3,2,1,0:T(8,128)(2,1)}, bf16[4,4,128,512]{3,2,1,0:T(8,128)(2,1)}, u32[]{:S(2)}, u32[]{:S(2)}) collective-permute-start(bf16[4,4,128,512]{3,2,1,0:T(8,128)(2,1)} %pad_maximum_fusion.1.cot0), channel_id=1, source_target_pairs={{0,1},{1,0},{2,3},{3,2},{4,5},{5,4},{6,7},{7,6},{8,9},{9,8},{10,11... | collective-permute-start | bytes 6291464 | tf_op jit(solution)/shard_map/ppermute | solution.py:50
  140.8 4.2 %collective-permute-start.15 = (bf16[4,4,128,512]{3,2,1,0:T(8,128)(2,1)S(1)}, bf16[4,4,128,512]{3,2,1,0:T(8,128)(2,1)S(1)}, u32[]{:S(2)}, u32[]{:S(2)}) collective-permute-start(bf16[4,4,128,512]{3,2,1,0:T(8,128)(2,1)S(1)} %slice_bitcast_fusion), channel_id=1, source_target_pairs={{0,1},{1,0},{2,3},{3,2},{4,5},{5,4},{6,7},{7,6},{8,9},{9,8},{10,11... | collective-permute-start | bytes 6291464 | tf_op jit(solution)/shard_map/ppermute | solution.py:50
  147.1 95.8 %copy-start.2 = (f32[320]{0:T(512)S(1)}, f32[320]{0:T(512)}, u32[]{:S(2)}) copy-start(f32[320]{0:T(512)} %param.21) | copy-start | bytes 3844
  147.1 95.8 %copy-start.3 = (f32[320]{0:T(512)S(1)}, f32[320]{0:T(512)}, u32[]{:S(2)}) copy-start(f32[320]{0:T(512)} %param.20) | copy-start | bytes 3844
  147.1 95.8 %copy-start.4 = (f32[320]{0:T(512)S(1)}, f32[320]{0:T(512)}, u32[]{:S(2)}) copy-start(f32[320]{0:T(512)} %param.18) | copy-start | bytes 3844
  147.1 99.1 %all-to-all-start = ((bf16[16,128,512]{2,1,0:T(8,128)(2,1)}), bf16[16,128,512]{2,1,0:T(8,128)(2,1)S(1)}, u32[]{:S(2)}, u32[]{:S(2)}) async-start(bf16[16,128,512]{2,1,0:T(8,128)(2,1)} %bitcast.23), calls=%async_computation | async-start | bytes 4194304 | tf_op jit(solution)/shard_map/all_to_all | solution.py:256
  226.1 10.2 %collective-permute-start.22 = (f32[960]{0:T(1024)S(1)}, f32[960]{0:T(1024)S(1)}, u32[]{:S(2)}, u32[]{:S(2)}) collective-permute-start(f32[960]{0:T(1024)S(1)} %add_reduce_fusion.1), channel_id=1, source_target_pairs={{0,192},{32,224},{64,128},{96,160},{128,64},{160,96},{192,0},{224,... | collective-permute-start | bytes 11528 | tf_op jit(solution)/shard_map/ppermute | solution.py:50
  228.4 10.9 %collective-permute-start.23 = (f32[960]{0:T(1024)S(1)}, f32[960]{0:T(1024)S(1)}, u32[]{:S(2)}, u32[]{:S(2)}) collective-permute-start(f32[960]{0:T(1024)S(1)} %add_reduce_fusion.1), channel_id=1, source_target_pairs={{0,224},{32,192},{64,160},{96,128},{128,96},{160,64},{192,32},{224... | collective-permute-start | bytes 11528 | tf_op jit(solution)/shard_map/ppermute | solution.py:50
  228.7 11.2 %collective-permute-start.20 = (f32[960]{0:T(1024)S(1)}, f32[960]{0:T(1024)S(1)}, u32[]{:S(2)}, u32[]{:S(2)}) collective-permute-start(f32[960]{0:T(1024)S(1)} %add_reduce_fusion.1), channel_id=1, source_target_pairs={{0,128},{32,160},{64,192},{96,224},{128,0},{160,32},{192,64},{224,... | collective-permute-start | bytes 11528 | tf_op jit(solution)/shard_map/ppermute | solution.py:50
  233.3 6.6 %collective-permute-start.21 = (f32[960]{0:T(1024)S(1)}, f32[960]{0:T(1024)S(1)}, u32[]{:S(2)}, u32[]{:S(2)}) collective-permute-start(f32[960]{0:T(1024)S(1)} %add_reduce_fusion.1), channel_id=1, source_target_pairs={{0,160},{32,128},{64,224},{96,192},{128,32},{160,0},{192,96},{224,... | collective-permute-start | bytes 11528 | tf_op jit(solution)/shard_map/ppermute | solution.py:50
  236.3 4.5 %collective-permute-start.18 = (f32[960]{0:T(1024)S(1)}, f32[960]{0:T(1024)S(1)}, u32[]{:S(2)}, u32[]{:S(2)}) collective-permute-start(f32[960]{0:T(1024)S(1)} %add_reduce_fusion.1), channel_id=1, source_target_pairs={{0,64},{32,96},{64,0},{96,32},{128,192},{160,224},{192,128},{224,1... | collective-permute-start | bytes 11528 | tf_op jit(solution)/shard_map/ppermute | solution.py:50
  236.3 5.4 %collective-permute-start.19 = (f32[960]{0:T(1024)S(1)}, f32[960]{0:T(1024)S(1)}, u32[]{:S(2)}, u32[]{:S(2)}) collective-permute-start(f32[960]{0:T(1024)S(1)} %add_reduce_fusion.1), channel_id=1, source_target_pairs={{0,96},{32,64},{64,32},{96,0},{128,224},{160,192},{192,160},{224,1... | collective-permute-start | bytes 11528 | tf_op jit(solution)/shard_map/ppermute | solution.py:50
  239.3 3.6 %collective-permute-start.17 = (f32[960]{0:T(1024)S(1)}, f32[960]{0:T(1024)S(1)}, u32[]{:S(2)}, u32[]{:S(2)}) collective-permute-start(f32[960]{0:T(1024)S(1)} %add_reduce_fusion.1), channel_id=1, source_target_pairs={{0,32},{32,0},{64,96},{96,64},{128,160},{160,128},{192,224},{224,1... | collective-permute-start | bytes 11528 | tf_op jit(solution)/shard_map/ppermute | solution.py:50
  243.0 22.8 %copy-start.5 = (f32[512]{0:T(512)S(1)}, f32[512]{0:T(512)}, u32[]{:S(2)}) copy-start(f32[512]{0:T(512)} %param.22) | copy-start | bytes 6148
  243.0 22.8 %copy-start.6 = (f32[512]{0:T(512)S(1)}, f32[512]{0:T(512)}, u32[]{:S(2)}) copy-start(f32[512]{0:T(512)} %param.19) | copy-start | bytes 6148
  243.0 22.8 %copy-start.7 = (f32[512]{0:T(512)S(1)}, f32[512]{0:T(512)}, u32[]{:S(2)}) copy-start(f32[512]{0:T(512)} %param.17) | copy-start | bytes 6148
  246.1 1.3 collective-permute-start.24
  246.5 8.8 %collective-permute-start.16 = (bf16[128,512]{1,0:T(8,128)(2,1)S(1)}, bf16[128,512]{1,0:T(8,128)(2,1)S(1)}, u32[]{:S(2)}, u32[]{:S(2)}) collective-permute-start(bf16[128,512]{1,0:T(8,128)(2,1)S(1)} %reduce_sum.48), channel_id=1, source_target_pairs={{0,0},{32,1},{2,2},{34,3},{4,4},{36,5},{6,6},{38,7},{72,8},{104,9}... | collective-permute-start | bytes 393224 | tf_op jit(solution)/shard_map/ppermute | solution.py:258
  247.4 8.8 %collective-permute-start.26 = (f32[6,512]{1,0:T(8,128)S(1)}, f32[6,512]{1,0:T(8,128)S(1)}, u32[]{:S(2)}, u32[]{:S(2)}) collective-permute-start(f32[6,512]{1,0:T(8,128)S(1)} %fusion.8), channel_id=1, source_target_pairs={{0,16},{8,24},{16,0},{24,8},{1,17},{9,25},{17,1},{25,9},{2,18},{10... | collective-permute-start | bytes 36872 | tf_op jit(solution)/shard_map/ppermute | solution.py:50
  254.4 4.9 %collective-permute-start.27 = (f32[6,512]{1,0:T(8,128)S(1)}, f32[6,512]{1,0:T(8,128)S(1)}, u32[]{:S(2)}, u32[]{:S(2)}) collective-permute-start(f32[6,512]{1,0:T(8,128)S(1)} %fusion.8), channel_id=1, source_target_pairs={{0,24},{8,16},{16,8},{24,0},{1,25},{9,17},{17,9},{25,1},{2,26},{10... | collective-permute-start | bytes 36872 | tf_op jit(solution)/shard_map/ppermute | solution.py:50
  254.7 4.7 %collective-permute-start.25 = (f32[6,512]{1,0:T(8,128)S(1)}, f32[6,512]{1,0:T(8,128)S(1)}, u32[]{:S(2)}, u32[]{:S(2)}) collective-permute-start(f32[6,512]{1,0:T(8,128)S(1)} %fusion.8), channel_id=1, source_target_pairs={{0,8},{8,0},{16,24},{24,16},{1,9},{9,1},{17,25},{25,17},{2,10},{10... | collective-permute-start | bytes 36872 | tf_op jit(solution)/shard_map/ppermute | solution.py:50
  259.4 5.5 %collective-permute-start.29 = (f32[6,512]{1,0:T(8,128)S(1)}, f32[6,512]{1,0:T(8,128)S(1)}, u32[]{:S(2)}, u32[]{:S(2)}) collective-permute-start(f32[6,512]{1,0:T(8,128)S(1)} %add_add_fusion.1), channel_id=1, source_target_pairs={{0,4},{2,6},{4,0},{6,2},{1,5},{3,7},{5,1},{7,3},{8,12},{10,14},{12... | collective-permute-start | bytes 36872 | tf_op jit(solution)/shard_map/ppermute | solution.py:50
  261.6 3.7 %collective-permute-start.30 = (f32[6,512]{1,0:T(8,128)S(1)}, f32[6,512]{1,0:T(8,128)S(1)}, u32[]{:S(2)}, u32[]{:S(2)}) collective-permute-start(f32[6,512]{1,0:T(8,128)S(1)} %add_add_fusion.1), channel_id=1, source_target_pairs={{0,6},{2,4},{4,2},{6,0},{1,7},{3,5},{5,3},{7,1},{8,14},{10,12},{12... | collective-permute-start | bytes 36872 | tf_op jit(solution)/shard_map/ppermute | solution.py:50
  261.6 4.3 %collective-permute-start.28 = (f32[6,512]{1,0:T(8,128)S(1)}, f32[6,512]{1,0:T(8,128)S(1)}, u32[]{:S(2)}, u32[]{:S(2)}) collective-permute-start(f32[6,512]{1,0:T(8,128)S(1)} %add_add_fusion.1), channel_id=1, source_target_pairs={{0,2},{2,0},{4,6},{6,4},{1,3},{3,1},{5,7},{7,5},{8,10},{10,8},{12,... | collective-permute-start | bytes 36872 | tf_op jit(solution)/shard_map/ppermute | solution.py:50
  266.0 10.8 %collective-permute-start.36 = (f32[3,1]{0,1:T(1,128)S(1)}, f32[3,1]{0,1:T(1,128)S(1)}, u32[]{:S(2)}, u32[]{:S(2)}) collective-permute-start(f32[3,1]{0,1:T(1,128)S(1)} %bitcast.77), channel_id=1, source_target_pairs={{0,192},{32,224},{64,128},{96,160},{128,64},{160,96},{192,0},{224,... | collective-permute-start | bytes 44 | tf_op jit(solution)/shard_map/ppermute | solution.py:50
  269.4 9.5 %collective-permute-start.37 = (f32[3,1]{0,1:T(1,128)S(1)}, f32[3,1]{0,1:T(1,128)S(1)}, u32[]{:S(2)}, u32[]{:S(2)}) collective-permute-start(f32[3,1]{0,1:T(1,128)S(1)} %bitcast.78), channel_id=1, source_target_pairs={{0,224},{32,192},{64,160},{96,128},{128,96},{160,64},{192,32},{224... | collective-permute-start | bytes 44 | tf_op jit(solution)/shard_map/ppermute | solution.py:50
  269.4 10.8 %collective-permute-start.34 = (f32[3,1]{0,1:T(1,128)S(1)}, f32[3,1]{0,1:T(1,128)S(1)}, u32[]{:S(2)}, u32[]{:S(2)}) collective-permute-start(f32[3,1]{0,1:T(1,128)S(1)} %bitcast.79), channel_id=1, source_target_pairs={{0,128},{32,160},{64,192},{96,224},{128,0},{160,32},{192,64},{224,... | collective-permute-start | bytes 44 | tf_op jit(solution)/shard_map/ppermute | solution.py:50
  273.2 7.1 %collective-permute-start.35 = (f32[3,1]{0,1:T(1,128)S(1)}, f32[3,1]{0,1:T(1,128)S(1)}, u32[]{:S(2)}, u32[]{:S(2)}) collective-permute-start(f32[3,1]{0,1:T(1,128)S(1)} %bitcast.80), channel_id=1, source_target_pairs={{0,160},{32,128},{64,224},{96,192},{128,32},{160,0},{192,96},{224,... | collective-permute-start | bytes 44 | tf_op jit(solution)/shard_map/ppermute | solution.py:50
  276.2 4.4 %collective-permute-start.32 = (f32[3,1]{0,1:T(1,128)S(1)}, f32[3,1]{0,1:T(1,128)S(1)}, u32[]{:S(2)}, u32[]{:S(2)}) collective-permute-start(f32[3,1]{0,1:T(1,128)S(1)} %bitcast.81), channel_id=1, source_target_pairs={{0,64},{32,96},{64,0},{96,32},{128,192},{160,224},{192,128},{224,1... | collective-permute-start | bytes 44 | tf_op jit(solution)/shard_map/ppermute | solution.py:50
  276.8 5.3 %collective-permute-start.33 = (f32[3,1]{0,1:T(1,128)S(1)}, f32[3,1]{0,1:T(1,128)S(1)}, u32[]{:S(2)}, u32[]{:S(2)}) collective-permute-start(f32[3,1]{0,1:T(1,128)S(1)} %bitcast.82), channel_id=1, source_target_pairs={{0,96},{32,64},{64,32},{96,0},{128,224},{160,192},{192,160},{224,1... | collective-permute-start | bytes 44 | tf_op jit(solution)/shard_map/ppermute | solution.py:50
  278.9 3.5 %collective-permute-start.31 = (f32[3,1]{0,1:T(1,128)S(1)}, f32[3,1]{0,1:T(1,128)S(1)}, u32[]{:S(2)}, u32[]{:S(2)}) collective-permute-start(f32[3,1]{0,1:T(1,128)S(1)} %bitcast.83), channel_id=1, source_target_pairs={{0,32},{32,0},{64,96},{96,64},{128,160},{160,128},{192,224},{224,1... | collective-permute-start | bytes 44 | tf_op jit(solution)/shard_map/ppermute | solution.py:50
Sparse Core Ops, SparseCore 0:
  9.8 100.1 all-gather.2
  132.8 91.7 reduce-scatter.1

commit v2 on v1

v2 whole, which is shorter than its diff:
```python
import math

import jax
import jax.numpy as jnp
from jax import lax
from jax.experimental import pallas as pl
from jax.experimental.pallas import tpu as pltpu
from jax.sharding import Mesh
from jax.sharding import PartitionSpec as P

D = 4096
FF = 10240
NZ, NX, NY, NC = 8, 4, 4, 2
TOK = 512
SUB = 16
DB = D // NZ
FB = FF // (NX * NY * NC)

decay_rate = 0.8
gelu_coeff = math.sqrt(2.0 / math.pi)
COL = ("x", "y", "c")
VMEM = 48 * 1024 * 1024


def shifted(value, axis, step):
    return lax.ppermute(value, axis, [((i + step) % 4, i) for i in range(4)])


def swap(value):
    return lax.ppermute(value, "c", [(0, 1), (1, 0)])


def gather4(value, axis, model_dim, new_dim):
    right = shifted(value, axis, 1)
    left = shifted(value, axis, 3)
    low = lax.slice_in_dim(right, 0, NZ // 2, axis=model_dim)
    high = lax.slice_in_dim(left, NZ // 2, NZ, axis=model_dim)
    far = jnp.concatenate([shifted(low, axis, 1), shifted(high, axis, 3)], model_dim)
    return jnp.stack([value, right, far, left], new_dim)


def sum_over(value, axis, size):
    copies = jnp.broadcast_to(value[None], (size,) + value.shape)
    return jnp.sum(lax.all_to_all(copies, axis, 0, 0, tiled=True), 0)


def sum_col(value):
    return sum_over(value + swap(value), ("x", "y"), NX * NY)


def gelu_parts(value):
    inner = gelu_coeff * (value + 0.044715 * value * value * value)
    tangent = jnp.tanh(inner)
    gelu_value = 0.5 * value * (1.0 + tangent)
    gelu_slope = 0.5 * (1.0 + tangent) + 0.5 * value * (1.0 - tangent * tangent) * gelu_coeff * (
        1.0 + 3.0 * 0.044715 * value * value
    )
    return (gelu_value, gelu_slope)


def dot_nt(left, right):
    return lax.dot_general(
        left, right, (((1,), (1,)), ((), ())), preferred_element_type=jnp.float32
    )


def rows_of(own, other, k):
    return jnp.concatenate(
        [own[:, :, k].reshape(TOK // 2, DB), other[:, :, k].reshape(TOK // 2, DB)], 0
    )


def forward_kernel(tok0, tok1, cot0, cot1, weight, hidden_t, hidden, acc):
    i = pl.program_id(0)

    def products():
        first = second = 0.0
        for k in range(2):
            first += dot_nt(weight[k, : 2 * FB], rows_of(tok0, tok1, k))
            second += dot_nt(weight[k, 2 * FB :], rows_of(cot0, cot1, k))
        return first, second

    @pl.when(i == 0)
    def _():
        first, second = products()
        acc[: 2 * FB] = first
        acc[2 * FB :] = second

    @pl.when(i > 0)
    def _():
        first, second = products()
        acc[: 2 * FB] += first
        acc[2 * FB :] += second

    @pl.when(i == NZ // 2 - 1)
    def _():
        pre_gate = acc[:FB]
        pre_lin = acc[FB : 2 * FB]
        grad_act = acc[2 * FB :]
        gelu_value, gelu_slope = gelu_parts(pre_gate)
        gate = grad_act * pre_lin * gelu_slope
        lin = grad_act * gelu_value
        hidden_t[:FB] = gate.astype(jnp.bfloat16)
        hidden_t[FB : 2 * FB] = lin.astype(jnp.bfloat16)
        hidden_t[2 * FB :] = (gelu_value * pre_lin).astype(jnp.bfloat16)
        hidden[...] = hidden_t[: 2 * FB].T


def weight_grad_kernel(tok0, tok1, cot0, cot1, hidden_t, grad):
    for k in range(2):
        grad[k, : 2 * FB] = jnp.dot(
            hidden_t[: 2 * FB], rows_of(tok0, tok1, k), preferred_element_type=jnp.float32
        ).astype(jnp.bfloat16)
        grad[k, 2 * FB :] = jnp.dot(
            hidden_t[2 * FB :], rows_of(cot0, cot1, k), preferred_element_type=jnp.float32
        ).astype(jnp.bfloat16)


def token_grad_kernel(place, hidden, weight, grad):
    for k in range(2):
        product = jnp.dot(hidden[...], weight[k], preferred_element_type=jnp.float32)
        product = product.astype(jnp.bfloat16).reshape(2, NY, NX, SUB, DB)
        for y in range(NY):
            for x in range(NX):
                for core in range(2):
                    grad[core, place[y * NX + x], k] = product[core, y, x]


def block_specs():
    return [pl.BlockSpec((NY, NX, 2, SUB, DB), lambda i: (0, 0, i, 0, 0))] * 4


def forward(blocks, weight):
    return pl.pallas_call(
        forward_kernel,
        grid=(NZ // 2,),
        in_specs=block_specs() + [pl.BlockSpec((2, 3 * FB, DB), lambda i: (i, 0, 0))],
        out_specs=[
            pl.BlockSpec((3 * FB, TOK), lambda i: (0, 0)),
            pl.BlockSpec((TOK, 2 * FB), lambda i: (0, 0)),
        ],
        scratch_shapes=[pltpu.VMEM((3 * FB, TOK), jnp.float32)],
        out_shape=[
            jax.ShapeDtypeStruct((3 * FB, TOK), jnp.bfloat16),
            jax.ShapeDtypeStruct((TOK, 2 * FB), jnp.bfloat16),
        ],
        compiler_params=pltpu.CompilerParams(vmem_limit_bytes=VMEM),
        cost_estimate=pl.CostEstimate(
            flops=2 * 3 * FB * TOK * D, bytes_accessed=17000000, transcendentals=FB * TOK
        ),
    )(*blocks, weight)


def weight_grad(blocks, hidden_t):
    return pl.pallas_call(
        weight_grad_kernel,
        grid=(NZ // 2,),
        in_specs=block_specs() + [pl.BlockSpec((3 * FB, TOK), lambda i: (0, 0))],
        out_specs=pl.BlockSpec((2, 3 * FB, DB), lambda i: (i, 0, 0)),
        out_shape=jax.ShapeDtypeStruct((NZ, 3 * FB, DB), jnp.bfloat16),
        compiler_params=pltpu.CompilerParams(vmem_limit_bytes=VMEM),
        cost_estimate=pl.CostEstimate(
            flops=2 * 3 * FB * TOK * D, bytes_accessed=17000000, transcendentals=0
        ),
    )(*blocks, hidden_t)


def token_grad(place, hidden, weight):
    return pl.pallas_call(
        token_grad_kernel,
        grid_spec=pltpu.PrefetchScalarGridSpec(
            num_scalar_prefetch=1,
            grid=(NZ // 2,),
            in_specs=[
                pl.BlockSpec((TOK, 2 * FB), lambda i, p: (0, 0)),
                pl.BlockSpec((2, 2 * FB, DB), lambda i, p: (i, 0, 0)),
            ],
            out_specs=pl.BlockSpec((2, NX * NY, 2, SUB, DB), lambda i, p: (0, 0, i, 0, 0)),
        ),
        out_shape=jax.ShapeDtypeStruct((2, NX * NY, NZ, SUB, DB), jnp.bfloat16),
        compiler_params=pltpu.CompilerParams(vmem_limit_bytes=VMEM),
        cost_estimate=pl.CostEstimate(
            flops=2 * 2 * FB * TOK * D, bytes_accessed=10000000, transcendentals=0
        ),
    )(place, hidden, weight)


def local(
    tokens,
    cotangent,
    wi_gate,
    wi_lin,
    wo,
    rows_gate,
    cols_gate,
    rows_lin,
    cols_lin,
    rows_out,
    cols_out,
    rate,
):
    bf16 = jnp.bfloat16
    weight = lax.all_gather(jnp.concatenate([wi_gate.T, wi_lin.T, wo], 0), "z", axis=0)

    pair = jnp.stack([tokens.reshape(NZ, SUB, DB), cotangent.reshape(NZ, SUB, DB)], 1)
    pair = lax.all_to_all(pair, "z", 0, 0, tiled=True)
    tok = gather4(gather4(pair[:, 0], "x", 0, 0), "y", 1, 0)
    cot = gather4(gather4(pair[:, 1], "y", 0, 0), "x", 1, 1)
    blocks = [tok, swap(tok), cot, swap(cot)]

    hidden_t, hidden = forward(blocks, weight)
    grad_w = lax.psum_scatter(weight_grad(blocks, hidden_t), "z", scatter_dimension=0)

    shift = jnp.arange(4, dtype=jnp.int32)
    x_of = (lax.axis_index("x") + shift) % NX
    y_of = (lax.axis_index("y") + shift) % NY
    place = (x_of[None, :] * NY + y_of[:, None]).astype(jnp.int32).reshape(NX * NY)
    part = token_grad(place, hidden, weight)
    part = (part[0].astype(jnp.float32) + swap(part[1]).astype(jnp.float32)).astype(bf16)
    part = lax.all_to_all(part, ("x", "y"), 0, 0, tiled=True)
    part = jnp.sum(part.astype(jnp.float32), 0).astype(bf16)
    grad_tokens = lax.all_to_all(part, "z", 0, 0, tiled=True).reshape(tokens.shape)
    grad_w, grad_tokens = lax.optimization_barrier((grad_w, grad_tokens))

    grad = grad_w.astype(jnp.float32) * (1.0 / math.sqrt(4096.0))
    keep = 1.0 - decay_rate
    squares = grad * grad + 1e-30
    over_model = sum_over(jnp.sum(squares, 1), "z", NZ)
    hidden_old = jnp.concatenate([cols_gate, cols_lin, rows_out])
    hidden_new = decay_rate * hidden_old + keep * over_model / D
    model_old = jnp.stack([rows_gate, rows_lin, cols_out], 0)
    weighted = grad * grad / hidden_new[:, None]
    over_hidden = sum_col(
        jnp.concatenate(
            [
                jnp.sum(squares.reshape(3, FB, DB), 1),
                jnp.sum(weighted.reshape(3, FB, DB), 1),
            ],
            0,
        )
    )
    model_new = decay_rate * model_old + keep * over_hidden[:3] / FF
    totals = sum_over(jnp.sum(over_hidden[3:] / model_new, 1, keepdims=True), "z", NZ)
    factor = -rate[0] / jnp.sqrt(totals / (D * FF) + 1e-06)
    update = (
        grad.reshape(3, FB, DB)
        * lax.rsqrt(hidden_new).reshape(3, FB, 1)
        * (factor * lax.rsqrt(model_new)).reshape(3, 1, DB)
    )
    return (
        grad_tokens,
        update[0].T,
        update[1].T,
        update[2],
        model_new[0],
        hidden_new[:FB],
        model_new[1],
        hidden_new[FB : 2 * FB],
        hidden_new[2 * FB :],
        model_new[2],
    )


def solution(mesh):
    fine = Mesh(mesh.devices.reshape(NZ, NX, NY, NC), ("z",) + COL)
    return jax.shard_map(
        local,
        mesh=fine,
        in_specs=(
            P(None, COL, "z"),
            P(None, COL, "z"),
            P("z", COL),
            P("z", COL),
            P(COL, "z"),
            P("z"),
            P(COL),
            P("z"),
            P(COL),
            P(COL),
            P("z"),
            P(),
        ),
        out_specs=(
            P(None, COL, "z"),
            P("z", COL),
            P("z", COL),
            P(COL, "z"),
            P("z"),
            P(COL),
            P("z"),
            P(COL),
            P(COL),
            P("z"),
        ),
        check_vma=False,
    )
```

time: 296 us -> 269 us (0.909)
  blocking collectives: 0 us -> 68.9 us
  starting transfers between devices: 92.4 us -> 39.1 us
  waiting for transfers between devices: 138 us -> 99.2 us
  Pallas kernels: 30.6 us -> 23.1 us
  local copies, waits for them, and re-layouts: 3.63 us -> 10 us
    all_to_all x0 -> x3, blocking collectives: none -> 68.9 us  [the longest x1 34.4 us: local(): part = lax.all_to_all(part, ('x', 'y'), 0, 0, tiled=True)]
    reduce_scatter x1, waiting for transfers between devices: 71.5 us -> 29.9 us  [local(): lax.psum_scatter(weight_grad(blocks, hidden_t), 'z', scatter_dimension=0)]
    ppermute x26 -> x4, starting transfers between devices: 41.2 us -> 0.37 us  [swap(): return lax.ppermute(value, 'c', [(0, 1), (1, 0)])]
    ppermute x12 -> x16, waiting for transfers between devices: 37.4 us -> 15.4 us  [shifted(): return lax.ppermute(value, axis, [((i + step) % 4, i) for i in range(4)])]
    ppermute x12 -> x16, starting transfers between devices: 45.2 us -> 23.8 us  [shifted(): return lax.ppermute(value, axis, [((i + step) % 4, i) for i in range(4)])]
    all_to_all x1 -> x3, waiting for transfers between devices: 0.01 us -> 19.2 us  [sum_over(): return jnp.sum(lax.all_to_all(copies, axis, 0, 0, tiled=True), 0)]
    all_gather x1, waiting for transfers between devices: 10.4 us -> 26.6 us  [local(): lax.all_gather(jnp.concatenate([wi_gate.T, wi_lin.T, wo], 0), 'z', axis=0)]
    ppermute x26 -> x4, waiting for transfers between devices: 18.8 us -> 8.05 us  [swap(): return lax.ppermute(value, 'c', [(0, 1), (1, 0)])]
  transfers between devices with their start and end apart: 41 -> 25, of which waited for: 21 -> 17; matrix products, arithmetic and copies ran while one was open for 4% -> 2% of each run, Pallas kernels for 3% -> 2%
where the time goes in v2:
time: 269 us
  waiting for transfers between devices  99.2 us (37%)
  blocking collectives  68.9 us (26%)
  starting transfers between devices  39.1 us (15%)
  Pallas kernels  23.1 us (9%)
  between operations  15.1 us (6%)
  other arithmetic  13 us (5%)
  local copies, waits for them, and re-layouts  10 us (4%)
    all_to_all x1, blocking collectives, local(): part = lax.all_to_all(part, ('x', 'y'), 0, 0, tiled=True)  34.4 us
    reduce_scatter x1, waiting for transfers between devices, local(): lax.psum_scatter(weight_grad(blocks, hidden_t), 'z', scatter_dimension=0)  29.9 us
    all_gather x1, waiting for transfers between devices, local(): lax.all_gather(jnp.concatenate([wi_gate.T, wi_lin.T, wo], 0), 'z', axis=0)  26.6 us
    ppermute x16, starting transfers between devices, shifted(): return lax.ppermute(value, axis, [((i + step) % 4, i) for i in range(4)])  23.8 us
    all_to_all x1, blocking collectives, local(): pair = lax.all_to_all(pair, 'z', 0, 0, tiled=True)  20.2 us
    all_to_all x3, waiting for transfers between devices, sum_over(): return jnp.sum(lax.all_to_all(copies, axis, 0, 0, tiled=True), 0)  19.2 us
    ppermute x16, waiting for transfers between devices, shifted(): return lax.ppermute(value, axis, [((i + step) % 4, i) for i in range(4)])  15.4 us
    all_to_all x3, starting transfers between devices, sum_over(): return jnp.sum(lax.all_to_all(copies, axis, 0, 0, tiled=True), 0)  14.9 us
  transfers between devices with their start and end apart: 25, of which 17 were waited for; matrix products, arithmetic and copies ran while one was open for 2% of the time, Pallas kernels for 2%

profile of v2, /device:TPU:8, one launch (start us, length us, event | category | flops | bytes accessed | tf_op | source)
XLA Modules:
  0.0 268.5 jit_solution(13706544667572217323)
XLA Ops:
  7.2 2.2 pad_maximum_fusion.2
  9.6 20.2 %all_to_all.31 = bf16[8,2,16,512]{3,2,1,0:T(8,128)(2,1)S(1)} all-to-all(bf16[8,2,16,512]{3,2,1,0:T(8,128)(2,1)S(1)} %pad_maximum_fusion.5), channel_id=1, replica_groups=mesh['z'=8,'x'=4,'y'=4,'c'=2] {'z'}, dimensions={0} | all-to-all | bytes 524288 | tf_op jit(solution)/shard_map/all_to_all | solution.py:206
  29.8 0.5 collective-permute-start.9
  30.4 1.6 collective-permute-start.11
  32.0 2.8 %collective-permute-start = (bf16[8,16,512]{2,1,0:T(8,128)(2,1)S(1)}, bf16[8,16,512]{2,1,0:T(8,128)(2,1)S(1)}, u32[]{:S(2)}, u32[]{:S(2)}) collective-permute-start(bf16[8,16,512]{2,1,0:T(8,128)(2,1)S(1)} %get-tuple-element.32), channel_id=1, source_target_pairs={{8,0},{16,8},{24,16},{0,24},{9,1},{17,9},{25,17},{1,25},{10,2},{18... | collective-permute-start | bytes 393224 | tf_op jit(solution)/shard_map/ppermute | solution.py:26
  34.7 0.3 collective-permute-done.9
  35.0 1.2 collective-permute-start.10
  36.3 0.1 collective-permute-done.11
  36.4 0.9 collective-permute-start.12
  37.3 0.2 collective-permute-done
  37.4 3.4 %collective-permute-start.1 = (bf16[4,16,512]{2,1,0:T(8,128)(2,1)S(1)}, bf16[4,16,512]{2,1,0:T(8,128)(2,1)S(1)}, u32[]{:S(2)}, u32[]{:S(2)}) collective-permute-start(bf16[4,16,512]{2,1,0:T(8,128)(2,1)S(1)} %slice.93), channel_id=1, source_target_pairs={{8,0},{16,8},{24,16},{0,24},{9,1},{17,9},{25,17},{1,25},{10,2},{18... | collective-permute-start | bytes 196616 | tf_op jit(solution)/shard_map/ppermute | solution.py:26
  41.0 0.9 collective-permute-done.12
  41.9 0.1 fusion.11
  42.0 3.2 %collective-permute-start.13 = (bf16[4,8,16,512]{3,2,1,0:T(8,128)(2,1)S(1)}, bf16[4,8,16,512]{3,2,1,0:T(8,128)(2,1)S(1)}, u32[]{:S(2)}, u32[]{:S(2)}) collective-permute-start(bf16[4,8,16,512]{3,2,1,0:T(8,128)(2,1)S(1)} %get-tuple-element.27), channel_id=1, source_target_pairs={{8,0},{16,8},{24,16},{0,24},{9,1},{17,9},{25,17},{1,25},{10,2},{18... | collective-permute-start | bytes 1572872 | tf_op jit(solution)/shard_map/ppermute | solution.py:26
  45.3 1.9 collective-permute-done.3
  47.2 0.1 fusion.12
  47.3 2.1 collective-permute-start.4
  49.4 4.5 %collective-permute-done.13 = bf16[4,8,16,512]{3,2,1,0:T(8,128)(2,1)S(1)} collective-permute-done((bf16[4,8,16,512]{3,2,1,0:T(8,128)(2,1)S(1)}, bf16[4,8,16,512]{3,2,1,0:T(8,128)(2,1)S(1)}, u32[]{:S(2)}, u32[]{:S(2)}) %collective-permute-start.13) | collective-permute-done | bytes 524320 | tf_op jit(solution)/shard_map/ppermute | solution.py:26
  53.8 3.4 %collective-permute-start.14 = (bf16[4,4,16,512]{3,2,1,0:T(8,128)(2,1)S(1)}, bf16[4,4,16,512]{3,2,1,0:T(8,128)(2,1)S(1)}, u32[]{:S(2)}, u32[]{:S(2)}) collective-permute-start(bf16[4,4,16,512]{3,2,1,0:T(8,128)(2,1)S(1)} %slice.100), channel_id=1, source_target_pairs={{8,0},{16,8},{24,16},{0,24},{9,1},{17,9},{25,17},{1,25},{10,2},{18... | collective-permute-start | bytes 786440 | tf_op jit(solution)/shard_map/ppermute | solution.py:26
  57.4 4.3 %collective-permute-start.5 = (bf16[4,4,16,512]{3,2,1,0:T(8,128)(2,1)S(1)}, bf16[4,4,16,512]{3,2,1,0:T(8,128)(2,1)S(1)}, u32[]{:S(2)}, u32[]{:S(2)}) collective-permute-start(bf16[4,4,16,512]{3,2,1,0:T(8,128)(2,1)S(1)} %slice.95), channel_id=1, source_target_pairs={{2,0},{4,2},{6,4},{0,6},{3,1},{5,3},{7,5},{1,7},{10,8},{12,10},{14... | collective-permute-start | bytes 786440 | tf_op jit(solution)/shard_map/ppermute | solution.py:26
  61.9 3.1 %collective-permute-done.16 = bf16[4,4,16,512]{3,2,1,0:T(8,128)(2,1)S(1)} collective-permute-done((bf16[4,4,16,512]{3,2,1,0:T(8,128)(2,1)S(1)}, bf16[4,4,16,512]{3,2,1,0:T(8,128)(2,1)S(1)}, u32[]{:S(2)}, u32[]{:S(2)}) %collective-permute-start.16) | collective-permute-done | bytes 262176 | tf_op jit(solution)/shard_map/ppermute | solution.py:26
  65.0 0.3 pad_maximum_fusion.1.cot0
  65.3 0.1 collective-permute-start.17
  65.4 0.3 collective-permute-done.5
  65.7 4.2 %collective-permute-done.7 = bf16[4,4,16,512]{3,2,1,0:T(8,128)(2,1)S(1)} collective-permute-done((bf16[4,4,16,512]{3,2,1,0:T(8,128)(2,1)S(1)}, bf16[4,4,16,512]{3,2,1,0:T(8,128)(2,1)S(1)}, u32[]{:S(2)}, u32[]{:S(2)}) %collective-permute-start.7) | collective-permute-done | bytes 262176 | tf_op jit(solution)/shard_map/ppermute | solution.py:26
  69.9 0.3 pad_maximum_fusion.tok0
  70.2 0.1 collective-permute-start.8
  70.3 1.3 copy-done.3
  71.6 2.8 %collective-permute-done.8.tok1 = bf16[4,4,8,16,512]{4,3,2,1,0:T(8,128)(2,1)S(1)} collective-permute-done((bf16[4,4,8,16,512]{4,3,2,1,0:T(8,128)(2,1)S(1)}, bf16[4,4,8,16,512]{4,3,2,1,0:T(8,128)(2,1)S(1)}, u32[]{:S(2)}, u32[]{:S(2)}) %collective-permute-start.8) | collective-permute-done | bytes 2097184 | tf_op jit(solution)/shard_map/ppermute | solution.py:30
  74.5 1.4 copy-done
  75.9 26.6 %all-gather.3.cloned.1.call-done = bf16[7680,512]{1,0:T(8,128)(2,1)} async-done(((bf16[960,512]{1,0:T(8,128)(2,1)}), bf16[7680,512]{1,0:T(8,128)(2,1)}) %all-gather.3.cloned.1.call-update) | async-done | bytes 7864336 | tf_op jit(solution)/shard_map/all_gather | solution.py:203
  102.5 1.6 copy-done.1
  104.0 8.5 %shard_map.195 = (bf16[960,512]{1,0:T(8,128)(2,1)S(1)}, bf16[512,640]{1,0:T(8,128)(2,1)S(1)}) custom-call(bf16[4,4,8,16,512]{4,3,2,1,0:T(8,128)(2,1)S(1)} %pad_maximum_fusion.tok0, bf16[4,4,8,16,512]{4,3,2,1,0:T(8,128)(2,1)S(1)} %copy-done.1, bf16[4,4,8,16,512]{4,3,2,1,0:T(8,128)(2,1)} %copy-done.2, bf16[4,4,8,16,512]{4,3,2,1,0:T(8,128)(2,1)} %copy-done.3, ...), custom_call_target="tpu_custom_call" | custom-call | flops 4026531840 | bytes 17000000 | tf_op jit(solution)/shard_map/pallas_call | solution.py:134
  112.5 8.2 %shard_map.196 = bf16[8,960,512]{2,1,0:T(8,128)(2,1)} custom-call(bf16[4,4,8,16,512]{4,3,2,1,0:T(8,128)(2,1)S(1)} %pad_maximum_fusion.tok0, bf16[4,4,8,16,512]{4,3,2,1,0:T(8,128)(2,1)S(1)} %copy-done.1, bf16[4,4,8,16,512]{4,3,2,1,0:T(8,128)(2,1)} %copy-done.2, bf16[4,4,8,16,512]{4,3,2,1,0:T(8,128)(2,1)} %copy-done.3, ...), custom_call_target="tpu_custom_call" | custom-call | flops 4026531840 | bytes 17000000 | tf_op jit(solution)/shard_map/pallas_call | solution.py:155
  121.0 6.4 %shard_map.197 = bf16[2,16,8,16,512]{4,3,2,1,0:T(8,128)(2,1)S(1)} custom-call(s32[16]{0:T(128)S(1)} %add.102.place, bf16[512,640]{1,0:T(8,128)(2,1)S(1)} %get-tuple-element.15.hidden, bf16[8,960,512]{2,1,0:T(8,128)(2,1)} %bitcast.75), custom_call_target="tpu_custom_call" | custom-call | flops 2684354560 | bytes 10000000 | tf_op jit(solution)/shard_map/pallas_call | solution.py:169
  127.4 0.2 slice_bitcast_fusion
  127.6 0.1 collective-permute-start.18
  127.7 4.1 %collective-permute-done.18 = bf16[16,8,16,512]{3,2,1,0:T(8,128)(2,1)S(1)} collective-permute-done((bf16[16,8,16,512]{3,2,1,0:T(8,128)(2,1)S(1)}, bf16[16,8,16,512]{3,2,1,0:T(8,128)(2,1)S(1)}, u32[]{:S(2)}, u32[]{:S(2)}) %collective-permute-start.18) | collective-permute-done | bytes 2097184 | tf_op jit(solution)/shard_map/ppermute | solution.py:30
  131.9 0.9 fusion
  132.8 34.4 %all_to_all.32 = bf16[16,8,16,512]{3,2,1,0:T(8,128)(2,1)S(1)} all-to-all(bf16[16,8,16,512]{3,2,1,0:T(8,128)(2,1)S(1)} %fusion), channel_id=1, replica_groups=mesh['z'=8,'x'=4,'y'=4,'c'=2] {'x','y'}, dimensions={0} | all-to-all | bytes 4194304 | tf_op jit(solution)/shard_map/all_to_all | solution.py:220
  167.2 0.4 reduce_sum.75
  167.6 14.4 %all_to_all.33 = bf16[8,16,512]{2,1,0:T(8,128)(2,1)S(1)} all-to-all(bf16[8,16,512]{2,1,0:T(8,128)(2,1)S(1)} %reduce_sum.75), channel_id=1, replica_groups=mesh['z'=8,'x'=4,'y'=4,'c'=2] {'z'}, dimensions={0} | all-to-all | bytes 262144 | tf_op jit(solution)/shard_map/all_to_all | solution.py:222
  182.0 29.9 %reduce-scatter.2.cloned.1.call-done = bf16[1,960,512]{2,1,0:T(8,128)(2,1)} async-done(((bf16[8,960,512]{2,1,0:T(8,128)(2,1)}), bf16[1,960,512]{2,1,0:T(8,128)(2,1)}) %reduce-scatter.2.cloned.1.call-update) | async-done | bytes 983056 | tf_op jit(solution)/shard_map/reduce_scatter | solution.py:212
  211.8 2.8 %multiply_add_fusion = (f32[960,512]{1,0:T(8,128)}, f32[960]{0:T(1024)S(1)}, f32[960,512]{1,0:T(8,128)S(1)}) fusion(bf16[960,512]{1,0:T(8,128)(2,1)} %bitcast.79), kind=kLoop, calls=%fused_computation.9 | loop fusion | flops 2456640 | bytes 4919040 | tf_op jit(solution)/shard_map/add | solution.py:227
  214.7 0.6 broadcast_in_dim.6
  215.3 4.4 %all-to-all-start.3 = ((f32[8,1,960]{2,1,0:T(1,128)}), f32[8,1,960]{2,1,0:T(1,128)S(1)}, u32[]{:S(2)}, u32[]{:S(2)}) async-start(f32[8,1,960]{2,1,0:T(1,128)} %broadcast_in_dim.6), calls=%async_computation.4 | async-start | bytes 65536 | tf_op jit(solution)/shard_map/all_to_all | solution.py:44
  220.4 1.7 reduce_sum.78
  222.1 5.6 %all-to-all-done.3 = f32[8,1,960]{2,1,0:T(1,128)S(1)} async-done(((f32[8,1,960]{2,1,0:T(1,128)}), f32[8,1,960]{2,1,0:T(1,128)S(1)}, u32[]{:S(2)}, u32[]{:S(2)}) %all-to-all-start.3) | async-done | bytes 30752 | tf_op jit(solution)/shard_map/all_to_all | solution.py:44
  227.8 1.6 multiply_divide_fusion
  229.4 1.7 reduce_sum.79
  231.1 0.1 collective-permute-start.19
  231.3 1.1 collective-permute-done.19
  232.4 0.7 broadcast_in_dim.7
  233.2 7.2 %all-to-all-start.4 = ((f32[16,6,512]{2,1,0:T(8,128)}), f32[16,6,512]{2,1,0:T(8,128)S(1)}, u32[]{:S(2)}, u32[]{:S(2)}) async-start(f32[16,6,512]{2,1,0:T(8,128)} %broadcast_in_dim.7), calls=%async_computation.5 | async-start | bytes 524288 | tf_op jit(solution)/shard_map/all_to_all | solution.py:44
  240.4 0.7 fusion.15
  241.1 6.7 %all-to-all-done.4 = f32[16,6,512]{2,1,0:T(8,128)S(1)} async-done(((f32[16,6,512]{2,1,0:T(8,128)}), f32[16,6,512]{2,1,0:T(8,128)S(1)}, u32[]{:S(2)}, u32[]{:S(2)}) %all-to-all-start.4) | async-done | bytes 196640 | tf_op jit(solution)/shard_map/all_to_all | solution.py:44
  247.8 0.1 fusion.3
  247.9 0.6 broadcast_in_dim.8
  248.5 3.3 %all-to-all-start.5 = ((f32[8,3,1]{1,2,0:T(1,128)}), f32[8,3,1]{1,2,0:T(1,128)S(1)}, u32[]{:S(2)}, u32[]{:S(2)}) async-start(f32[8,3,1]{1,2,0:T(1,128)} %broadcast_in_dim.8), calls=%async_computation.6 | async-start | bytes 8192 | tf_op jit(solution)/shard_map/all_to_all | solution.py:44
  251.8 0.6 fusion.14
  252.4 6.9 %all-to-all-done.5 = f32[8,3,1]{1,2,0:T(1,128)S(1)} async-done(((f32[8,3,1]{1,2,0:T(1,128)}), f32[8,3,1]{1,2,0:T(1,128)S(1)}, u32[]{:S(2)}, u32[]{:S(2)}) %all-to-all-start.5) | async-done | bytes 128 | tf_op jit(solution)/shard_map/all_to_all | solution.py:44
  259.5 0.2 multiply_multiply_fusion
  259.7 1.3 slice_bitcast_fusion.2
  261.0 0.7 copy.50
  (71 shorter events, 1.3 us)
Async XLA Ops:
  7.2 2.4 copy-start.6
  7.2 2.4 copy-start.5
  7.2 95.3 %all-gather.3.cloned.1.call-start = ((), (), s32[]{:S(2)}) async-start(), calls=%async_computation.8 | async-start | bytes 8847360 | tf_op jit(solution)/shard_map/all_gather | solution.py:203
  9.5 202.3 %reduce-scatter.2.cloned.1.call-start = ((), (), s32[]{:S(2)}) async-start(), calls=%async_computation.7 | async-start | bytes 8847360 | tf_op jit(solution)/shard_map/reduce_scatter | solution.py:212
  29.8 5.2 %collective-permute-start.9 = (bf16[8,16,512]{2,1,0:T(8,128)(2,1)S(1)}, bf16[8,16,512]{2,1,0:T(8,128)(2,1)S(1)}, u32[]{:S(2)}, u32[]{:S(2)}) collective-permute-start(bf16[8,16,512]{2,1,0:T(8,128)(2,1)S(1)} %get-tuple-element.33), channel_id=1, source_target_pairs={{2,0},{4,2},{6,4},{0,6},{3,1},{5,3},{7,5},{1,7},{10,8},{12,10},{14... | collective-permute-start | bytes 393224 | tf_op jit(solution)/shard_map/ppermute | solution.py:26
  30.4 6.0 %collective-permute-start.11 = (bf16[8,16,512]{2,1,0:T(8,128)(2,1)S(1)}, bf16[8,16,512]{2,1,0:T(8,128)(2,1)S(1)}, u32[]{:S(2)}, u32[]{:S(2)}) collective-permute-start(bf16[8,16,512]{2,1,0:T(8,128)(2,1)S(1)} %get-tuple-element.33), channel_id=1, source_target_pairs={{6,0},{0,2},{2,4},{4,6},{7,1},{1,3},{3,5},{5,7},{14,8},{8,10},{10,... | collective-permute-start | bytes 393224 | tf_op jit(solution)/shard_map/ppermute | solution.py:26
  32.0 5.5 %collective-permute-start = (bf16[8,16,512]{2,1,0:T(8,128)(2,1)S(1)}, bf16[8,16,512]{2,1,0:T(8,128)(2,1)S(1)}, u32[]{:S(2)}, u32[]{:S(2)}) collective-permute-start(bf16[8,16,512]{2,1,0:T(8,128)(2,1)S(1)} %get-tuple-element.32), channel_id=1, source_target_pairs={{8,0},{16,8},{24,16},{0,24},{9,1},{17,9},{25,17},{1,25},{10,2},{18... | collective-permute-start | bytes 393224 | tf_op jit(solution)/shard_map/ppermute | solution.py:26
  34.7 6.2 %collective-permute-start.2 = (bf16[8,16,512]{2,1,0:T(8,128)(2,1)S(1)}, bf16[8,16,512]{2,1,0:T(8,128)(2,1)S(1)}, u32[]{:S(2)}, u32[]{:S(2)}) collective-permute-start(bf16[8,16,512]{2,1,0:T(8,128)(2,1)S(1)} %get-tuple-element.32), channel_id=1, source_target_pairs={{24,0},{0,8},{8,16},{16,24},{25,1},{1,9},{9,17},{17,25},{26,2},{2,... | collective-permute-start | bytes 393224 | tf_op jit(solution)/shard_map/ppermute | solution.py:26
  35.0 6.0 %collective-permute-start.10 = (bf16[4,16,512]{2,1,0:T(8,128)(2,1)S(1)}, bf16[4,16,512]{2,1,0:T(8,128)(2,1)S(1)}, u32[]{:S(2)}, u32[]{:S(2)}) collective-permute-start(bf16[4,16,512]{2,1,0:T(8,128)(2,1)S(1)} %slice.98), channel_id=1, source_target_pairs={{2,0},{4,2},{6,4},{0,6},{3,1},{5,3},{7,5},{1,7},{10,8},{12,10},{14... | collective-permute-start | bytes 196616 | tf_op jit(solution)/shard_map/ppermute | solution.py:26
  36.4 5.6 %collective-permute-start.12 = (bf16[4,16,512]{2,1,0:T(8,128)(2,1)S(1)}, bf16[4,16,512]{2,1,0:T(8,128)(2,1)S(1)}, u32[]{:S(2)}, u32[]{:S(2)}) collective-permute-start(bf16[4,16,512]{2,1,0:T(8,128)(2,1)S(1)} %slice.99), channel_id=1, source_target_pairs={{6,0},{0,2},{2,4},{4,6},{7,1},{1,3},{3,5},{5,7},{14,8},{8,10},{10,... | collective-permute-start | bytes 196616 | tf_op jit(solution)/shard_map/ppermute | solution.py:26
  37.4 7.8 %collective-permute-start.1 = (bf16[4,16,512]{2,1,0:T(8,128)(2,1)S(1)}, bf16[4,16,512]{2,1,0:T(8,128)(2,1)S(1)}, u32[]{:S(2)}, u32[]{:S(2)}) collective-permute-start(bf16[4,16,512]{2,1,0:T(8,128)(2,1)S(1)} %slice.93), channel_id=1, source_target_pairs={{8,0},{16,8},{24,16},{0,24},{9,1},{17,9},{25,17},{1,25},{10,2},{18... | collective-permute-start | bytes 196616 | tf_op jit(solution)/shard_map/ppermute | solution.py:26
  40.9 6.2 %collective-permute-start.3 = (bf16[4,16,512]{2,1,0:T(8,128)(2,1)S(1)}, bf16[4,16,512]{2,1,0:T(8,128)(2,1)S(1)}, u32[]{:S(2)}, u32[]{:S(2)}) collective-permute-start(bf16[4,16,512]{2,1,0:T(8,128)(2,1)S(1)} %slice.94), channel_id=1, source_target_pairs={{24,0},{0,8},{8,16},{16,24},{25,1},{1,9},{9,17},{17,25},{26,2},{2,... | collective-permute-start | bytes 196616 | tf_op jit(solution)/shard_map/ppermute | solution.py:26
  42.0 11.8 %collective-permute-start.13 = (bf16[4,8,16,512]{3,2,1,0:T(8,128)(2,1)S(1)}, bf16[4,8,16,512]{3,2,1,0:T(8,128)(2,1)S(1)}, u32[]{:S(2)}, u32[]{:S(2)}) collective-permute-start(bf16[4,8,16,512]{3,2,1,0:T(8,128)(2,1)S(1)} %get-tuple-element.27), channel_id=1, source_target_pairs={{8,0},{16,8},{24,16},{0,24},{9,1},{17,9},{25,17},{1,25},{10,2},{18... | collective-permute-start | bytes 1572872 | tf_op jit(solution)/shard_map/ppermute | solution.py:26
  45.3 12.0 %collective-permute-start.15 = (bf16[4,8,16,512]{3,2,1,0:T(8,128)(2,1)S(1)}, bf16[4,8,16,512]{3,2,1,0:T(8,128)(2,1)S(1)}, u32[]{:S(2)}, u32[]{:S(2)}) collective-permute-start(bf16[4,8,16,512]{3,2,1,0:T(8,128)(2,1)S(1)} %get-tuple-element.27), channel_id=1, source_target_pairs={{24,0},{0,8},{8,16},{16,24},{25,1},{1,9},{9,17},{17,25},{26,2},{2,... | collective-permute-start | bytes 1572872 | tf_op jit(solution)/shard_map/ppermute | solution.py:26
  47.3 10.1 %collective-permute-start.4 = (bf16[4,8,16,512]{3,2,1,0:T(8,128)(2,1)S(1)}, bf16[4,8,16,512]{3,2,1,0:T(8,128)(2,1)S(1)}, u32[]{:S(2)}, u32[]{:S(2)}) collective-permute-start(bf16[4,8,16,512]{3,2,1,0:T(8,128)(2,1)S(1)} %get-tuple-element.29), channel_id=1, source_target_pairs={{2,0},{4,2},{6,4},{0,6},{3,1},{5,3},{7,5},{1,7},{10,8},{12,10},{14... | collective-permute-start | bytes 1572872 | tf_op jit(solution)/shard_map/ppermute | solution.py:26
  49.3 12.4 %collective-permute-start.6 = (bf16[4,8,16,512]{3,2,1,0:T(8,128)(2,1)S(1)}, bf16[4,8,16,512]{3,2,1,0:T(8,128)(2,1)S(1)}, u32[]{:S(2)}, u32[]{:S(2)}) collective-permute-start(bf16[4,8,16,512]{3,2,1,0:T(8,128)(2,1)S(1)} %get-tuple-element.29), channel_id=1, source_target_pairs={{6,0},{0,2},{2,4},{4,6},{7,1},{1,3},{3,5},{5,7},{14,8},{8,10},{10,... | collective-permute-start | bytes 1572872 | tf_op jit(solution)/shard_map/ppermute | solution.py:26
  53.8 8.0 %collective-permute-start.14 = (bf16[4,4,16,512]{3,2,1,0:T(8,128)(2,1)S(1)}, bf16[4,4,16,512]{3,2,1,0:T(8,128)(2,1)S(1)}, u32[]{:S(2)}, u32[]{:S(2)}) collective-permute-start(bf16[4,4,16,512]{3,2,1,0:T(8,128)(2,1)S(1)} %slice.100), channel_id=1, source_target_pairs={{8,0},{16,8},{24,16},{0,24},{9,1},{17,9},{25,17},{1,25},{10,2},{18... | collective-permute-start | bytes 786440 | tf_op jit(solution)/shard_map/ppermute | solution.py:26
  57.3 7.7 %collective-permute-start.16 = (bf16[4,4,16,512]{3,2,1,0:T(8,128)(2,1)S(1)}, bf16[4,4,16,512]{3,2,1,0:T(8,128)(2,1)S(1)}, u32[]{:S(2)}, u32[]{:S(2)}) collective-permute-start(bf16[4,4,16,512]{3,2,1,0:T(8,128)(2,1)S(1)} %slice.101), channel_id=1, source_target_pairs={{24,0},{0,8},{8,16},{16,24},{25,1},{1,9},{9,17},{17,25},{26,2},{2,... | collective-permute-start | bytes 786440 | tf_op jit(solution)/shard_map/ppermute | solution.py:26
  57.4 8.3 %collective-permute-start.5 = (bf16[4,4,16,512]{3,2,1,0:T(8,128)(2,1)S(1)}, bf16[4,4,16,512]{3,2,1,0:T(8,128)(2,1)S(1)}, u32[]{:S(2)}, u32[]{:S(2)}) collective-permute-start(bf16[4,4,16,512]{3,2,1,0:T(8,128)(2,1)S(1)} %slice.95), channel_id=1, source_target_pairs={{2,0},{4,2},{6,4},{0,6},{3,1},{5,3},{7,5},{1,7},{10,8},{12,10},{14... | collective-permute-start | bytes 786440 | tf_op jit(solution)/shard_map/ppermute | solution.py:26
  61.8 8.1 %collective-permute-start.7 = (bf16[4,4,16,512]{3,2,1,0:T(8,128)(2,1)S(1)}, bf16[4,4,16,512]{3,2,1,0:T(8,128)(2,1)S(1)}, u32[]{:S(2)}, u32[]{:S(2)}) collective-permute-start(bf16[4,4,16,512]{3,2,1,0:T(8,128)(2,1)S(1)} %slice.96), channel_id=1, source_target_pairs={{6,0},{0,2},{2,4},{4,6},{7,1},{1,3},{3,5},{5,7},{14,8},{8,10},{10,... | collective-permute-start | bytes 786440 | tf_op jit(solution)/shard_map/ppermute | solution.py:26
  65.3 5.0 %copy-start.2 = (bf16[4,4,8,16,512]{4,3,2,1,0:T(8,128)(2,1)}, bf16[4,4,8,16,512]{4,3,2,1,0:T(8,128)(2,1)S(1)}, u32[]{:S(2)}) copy-start(bf16[4,4,8,16,512]{4,3,2,1,0:T(8,128)(2,1)S(1)} %pad_maximum_fusion.1.cot0) | copy-start | bytes 6291460
  65.3 5.1 %collective-permute-start.17 = (bf16[4,4,8,16,512]{4,3,2,1,0:T(8,128)(2,1)S(1)}, bf16[4,4,8,16,512]{4,3,2,1,0:T(8,128)(2,1)S(1)}, u32[]{:S(2)}, u32[]{:S(2)}) collective-permute-start(bf16[4,4,8,16,512]{4,3,2,1,0:T(8,128)(2,1)S(1)} %pad_maximum_fusion.1.cot0), channel_id=1, source_target_pairs={{0,1},{1,0},{2,3},{3,2},{4,5},{5,4},{6,7},{7,6},{8,9},{9,8},{10,11... | collective-permute-start | bytes 6291464 | tf_op jit(solution)/shard_map/ppermute | solution.py:30
  70.2 4.2 %collective-permute-start.8 = (bf16[4,4,8,16,512]{4,3,2,1,0:T(8,128)(2,1)S(1)}, bf16[4,4,8,16,512]{4,3,2,1,0:T(8,128)(2,1)S(1)}, u32[]{:S(2)}, u32[]{:S(2)}) collective-permute-start(bf16[4,4,8,16,512]{4,3,2,1,0:T(8,128)(2,1)S(1)} %pad_maximum_fusion.tok0), channel_id=1, source_target_pairs={{0,1},{1,0},{2,3},{3,2},{4,5},{5,4},{6,7},{7,6},{8,9},{9,8},{10,11... | collective-permute-start | bytes 6291464 | tf_op jit(solution)/shard_map/ppermute | solution.py:30
  70.3 1.3 copy-start.3
  74.5 1.4 copy-start
  102.5 1.6 copy-start.1
  127.6 4.2 %collective-permute-start.18 = (bf16[16,8,16,512]{3,2,1,0:T(8,128)(2,1)S(1)}, bf16[16,8,16,512]{3,2,1,0:T(8,128)(2,1)S(1)}, u32[]{:S(2)}, u32[]{:S(2)}) collective-permute-start(bf16[16,8,16,512]{3,2,1,0:T(8,128)(2,1)S(1)} %slice_bitcast_fusion), channel_id=1, source_target_pairs={{0,1},{1,0},{2,3},{3,2},{4,5},{5,4},{6,7},{7,6},{8,9},{9,8},{10,11... | collective-permute-start | bytes 6291464 | tf_op jit(solution)/shard_map/ppermute | solution.py:30
  211.8 8.5 %copy-start.9 = (f32[320]{0:T(512)S(1)}, f32[320]{0:T(512)}, u32[]{:S(2)}) copy-start(f32[320]{0:T(512)} %param.18) | copy-start | bytes 3844
  211.8 8.5 %copy-start.8 = (f32[320]{0:T(512)S(1)}, f32[320]{0:T(512)}, u32[]{:S(2)}) copy-start(f32[320]{0:T(512)} %param.20) | copy-start | bytes 3844
  211.8 8.5 %copy-start.7 = (f32[320]{0:T(512)S(1)}, f32[320]{0:T(512)}, u32[]{:S(2)}) copy-start(f32[320]{0:T(512)} %param.21) | copy-start | bytes 3844
  214.7 13.2 %copy-start.4 = (bf16[1,960,512]{2,1,0:T(8,128)(2,1)S(1)}, bf16[1,960,512]{2,1,0:T(8,128)(2,1)}, u32[]{:S(2)}) copy-start(bf16[1,960,512]{2,1,0:T(8,128)(2,1)} %reduce-scatter.2.cloned.1.call-done) | copy-start | bytes 2949124
  215.3 12.4 %all-to-all-start.3 = ((f32[8,1,960]{2,1,0:T(1,128)}), f32[8,1,960]{2,1,0:T(1,128)S(1)}, u32[]{:S(2)}, u32[]{:S(2)}) async-start(f32[8,1,960]{2,1,0:T(1,128)} %broadcast_in_dim.6), calls=%async_computation.4 | async-start | bytes 65536 | tf_op jit(solution)/shard_map/all_to_all | solution.py:44
  229.4 18.4 %copy-start.10 = (f32[512]{0:T(512)S(1)}, f32[512]{0:T(512)}, u32[]{:S(2)}) copy-start(f32[512]{0:T(512)} %param.22) | copy-start | bytes 6148
  229.4 18.4 %copy-start.11 = (f32[512]{0:T(512)S(1)}, f32[512]{0:T(512)}, u32[]{:S(2)}) copy-start(f32[512]{0:T(512)} %param.19) | copy-start | bytes 6148
  229.4 18.4 %copy-start.12 = (f32[512]{0:T(512)S(1)}, f32[512]{0:T(512)}, u32[]{:S(2)}) copy-start(f32[512]{0:T(512)} %param.17) | copy-start | bytes 6148
  231.1 1.3 collective-permute-start.19
  233.2 14.6 %all-to-all-start.4 = ((f32[16,6,512]{2,1,0:T(8,128)}), f32[16,6,512]{2,1,0:T(8,128)S(1)}, u32[]{:S(2)}, u32[]{:S(2)}) async-start(f32[16,6,512]{2,1,0:T(8,128)} %broadcast_in_dim.7), calls=%async_computation.5 | async-start | bytes 524288 | tf_op jit(solution)/shard_map/all_to_all | solution.py:44
  248.5 10.8 %all-to-all-start.5 = ((f32[8,3,1]{1,2,0:T(1,128)}), f32[8,3,1]{1,2,0:T(1,128)S(1)}, u32[]{:S(2)}, u32[]{:S(2)}) async-start(f32[8,3,1]{1,2,0:T(1,128)} %broadcast_in_dim.8), calls=%async_computation.6 | async-start | bytes 8192 | tf_op jit(solution)/shard_map/all_to_all | solution.py:44
Sparse Core Ops, SparseCore 0:
  9.8 92.5 all-gather.2
  120.9 90.8 reduce-scatter.1

commit v3 on v2

--- a/solution.py
+++ b/solution.py
@@ -64,56 +64,66 @@
     )
 
 
-def rows_of(own, other, k):
-    return jnp.concatenate(
-        [own[:, :, k].reshape(TOK // 2, DB), other[:, :, k].reshape(TOK // 2, DB)], 0
-    )
-
-
-def forward_kernel(tok0, tok1, cot0, cot1, weight, hidden_t, hidden, acc):
-    i = pl.program_id(0)
-
-    def products():
+def main_kernel(tok0, tok1, cot0, cot1, weight, grad, hidden, x, w, acc, hidden_t, sems, out_sems):
+    def loads(k):
+        sources = (tok0, tok1, cot0, cot1)
+        copies = [
+            pltpu.make_async_copy(source.at[:, :, k], x.at[m // 2, k, m % 2], sems.at[k, m])
+            for m, source in enumerate(sources)
+        ]
+        return copies + [pltpu.make_async_copy(weight.at[k], w.at[k], sems.at[k, 4])]
+
+    def store(k):
+        return pltpu.make_async_copy(w.at[k], grad.at[k], out_sems.at[k])
+
+    def start(k, carry):
+        for copy in loads(k):
+            copy.start()
+        return carry
+
+    lax.fori_loop(0, NZ, start, 0)
+    acc[...] = jnp.zeros_like(acc)
+
+    def forward(pair, carry):
         first = second = 0.0
-        for k in range(2):
-            first += dot_nt(weight[k, : 2 * FB], rows_of(tok0, tok1, k))
-            second += dot_nt(weight[k, 2 * FB :], rows_of(cot0, cot1, k))
-        return first, second
-
-    @pl.when(i == 0)
-    def _():
-        first, second = products()
-        acc[: 2 * FB] = first
-        acc[2 * FB :] = second
-
-    @pl.when(i > 0)
-    def _():
-        first, second = products()
+        for k in (2 * pair, 2 * pair + 1):
+            for copy in loads(k):
+                copy.wait()
+            first += dot_nt(w[k, : 2 * FB], x[0, k].reshape(TOK, DB))
+            second += dot_nt(w[k, 2 * FB :], x[1, k].reshape(TOK, DB))
         acc[: 2 * FB] += first
         acc[2 * FB :] += second
-
-    @pl.when(i == NZ // 2 - 1)
-    def _():
-        pre_gate = acc[:FB]
-        pre_lin = acc[FB : 2 * FB]
-        grad_act = acc[2 * FB :]
-        gelu_value, gelu_slope = gelu_parts(pre_gate)
-        gate = grad_act * pre_lin * gelu_slope
-        lin = grad_act * gelu_value
-        hidden_t[:FB] = gate.astype(jnp.bfloat16)
-        hidden_t[FB : 2 * FB] = lin.astype(jnp.bfloat16)
-        hidden_t[2 * FB :] = (gelu_value * pre_lin).astype(jnp.bfloat16)
-        hidden[...] = hidden_t[: 2 * FB].T
-
-
-def weight_grad_kernel(tok0, tok1, cot0, cot1, hidden_t, grad):
-    for k in range(2):
-        grad[k, : 2 * FB] = jnp.dot(
-            hidden_t[: 2 * FB], rows_of(tok0, tok1, k), preferred_element_type=jnp.float32
+        return carry
+
+    lax.fori_loop(0, NZ // 2, forward, 0)
+    pre_gate = acc[:FB]
+    pre_lin = acc[FB : 2 * FB]
+    grad_act = acc[2 * FB :]
+    gelu_value, gelu_slope = gelu_parts(pre_gate)
+    gate = grad_act * pre_lin * gelu_slope
+    lin = grad_act * gelu_value
+    hidden_t[:FB] = gate.astype(jnp.bfloat16)
+    hidden_t[FB : 2 * FB] = lin.astype(jnp.bfloat16)
+    hidden_t[2 * FB :] = (gelu_value * pre_lin).astype(jnp.bfloat16)
+
+    def backward(k, carry):
+        w[k, : 2 * FB] = jnp.dot(
+            hidden_t[: 2 * FB], x[0, k].reshape(TOK, DB), preferred_element_type=jnp.float32
         ).astype(jnp.bfloat16)
-        grad[k, 2 * FB :] = jnp.dot(
-            hidden_t[2 * FB :], rows_of(cot0, cot1, k), preferred_element_type=jnp.float32
+        w[k, 2 * FB :] = jnp.dot(
+            hidden_t[2 * FB :], x[1, k].reshape(TOK, DB), preferred_element_type=jnp.float32
         ).astype(jnp.bfloat16)
+        store(k).start()
+        return carry
+
+    lax.fori_loop(0, NZ, backward, 0)
+    hidden[...] = hidden_t[: 2 * FB].T
+
+    def finish(k, carry):
+        store(k).wait()
+        return carry
+
+    lax.fori_loop(0, NZ, finish, 0)
 
 
 def token_grad_kernel(place, hidden, weight, grad):
@@ -126,43 +136,29 @@
                     grad[core, place[y * NX + x], k] = product[core, y, x]
 
 
-def block_specs():
-    return [pl.BlockSpec((NY, NX, 2, SUB, DB), lambda i: (0, 0, i, 0, 0))] * 4
-
-
-def forward(blocks, weight):
+def products(blocks, weight):
+    hbm = pl.BlockSpec(memory_space=pltpu.HBM)
     return pl.pallas_call(
-        forward_kernel,
-        grid=(NZ // 2,),
-        in_specs=block_specs() + [pl.BlockSpec((2, 3 * FB, DB), lambda i: (i, 0, 0))],
-        out_specs=[
-            pl.BlockSpec((3 * FB, TOK), lambda i: (0, 0)),
-            pl.BlockSpec((TOK, 2 * FB), lambda i: (0, 0)),
+        main_kernel,
+        in_specs=[pl.BlockSpec(memory_space=pl.ANY)] * 4 + [hbm],
+        out_specs=[hbm, pl.BlockSpec(memory_space=pltpu.VMEM)],
+        scratch_shapes=[
+            pltpu.VMEM((2, NZ, 2, NY, NX, SUB, DB), jnp.bfloat16),
+            pltpu.VMEM((NZ, 3 * FB, DB), jnp.bfloat16),
+            pltpu.VMEM((3 * FB, TOK), jnp.float32),
+            pltpu.VMEM((3 * FB, TOK), jnp.bfloat16),
+            pltpu.SemaphoreType.DMA((NZ, 5)),
+            pltpu.SemaphoreType.DMA((NZ,)),
         ],
-        scratch_shapes=[pltpu.VMEM((3 * FB, TOK), jnp.float32)],
         out_shape=[
-            jax.ShapeDtypeStruct((3 * FB, TOK), jnp.bfloat16),
+            jax.ShapeDtypeStruct((NZ, 3 * FB, DB), jnp.bfloat16),
             jax.ShapeDtypeStruct((TOK, 2 * FB), jnp.bfloat16),
         ],
         compiler_params=pltpu.CompilerParams(vmem_limit_bytes=VMEM),
         cost_estimate=pl.CostEstimate(
-            flops=2 * 3 * FB * TOK * D, bytes_accessed=17000000, transcendentals=FB * TOK
+            flops=4 * 3 * FB * TOK * D, bytes_accessed=25000000, transcendentals=FB * TOK
         ),
     )(*blocks, weight)
-
-
-def weight_grad(blocks, hidden_t):
-    return pl.pallas_call(
-        weight_grad_kernel,
-        grid=(NZ // 2,),
-        in_specs=block_specs() + [pl.BlockSpec((3 * FB, TOK), lambda i: (0, 0))],
-        out_specs=pl.BlockSpec((2, 3 * FB, DB), lambda i: (i, 0, 0)),
-        out_shape=jax.ShapeDtypeStruct((NZ, 3 * FB, DB), jnp.bfloat16),
-        compiler_params=pltpu.CompilerParams(vmem_limit_bytes=VMEM),
-        cost_estimate=pl.CostEstimate(
-            flops=2 * 3 * FB * TOK * D, bytes_accessed=17000000, transcendentals=0
-        ),
-    )(*blocks, hidden_t)
 
 
 def token_grad(place, hidden, weight):
@@ -208,8 +204,8 @@
     cot = gather4(gather4(pair[:, 1], "y", 0, 0), "x", 1, 1)
     blocks = [tok, swap(tok), cot, swap(cot)]
 
-    hidden_t, hidden = forward(blocks, weight)
-    grad_w = lax.psum_scatter(weight_grad(blocks, hidden_t), "z", scatter_dimension=0)
+    grad_w, hidden = products(blocks, weight)
+    grad_w = lax.psum_scatter(grad_w, "z", scatter_dimension=0)
 
     shift = jnp.arange(4, dtype=jnp.int32)
     x_of = (lax.axis_index("x") + shift) % NX

time: 269 us -> 267 us (level)
    pallas_call x2 -> x1, Pallas kernels: 16.7 us -> 14.6 us  [products(): pl.pallas_call(main_kernel, in_specs=[pl.BlockSpec(memory_space=pl.ANY)]...]
where the time goes in v3:
time: 267 us; the launch traced here: 266 us
  waiting for transfers between devices  99.2 us (37%)
  blocking collectives  68.9 us (26%)
  starting transfers between devices  39.1 us (15%)
  Pallas kernels  21 us (8%)
  between operations  15.1 us (6%)
  other arithmetic  13 us (5%)
  local copies, waits for them, and re-layouts  10 us (4%)
    all_to_all x1, blocking collectives, local(): part = lax.all_to_all(part, ('x', 'y'), 0, 0, tiled=True)  34.4 us
    reduce_scatter x1, waiting for transfers between devices, local(): grad_w = lax.psum_scatter(grad_w, 'z', scatter_dimension=0)  29.9 us
    all_gather x1, waiting for transfers between devices, local(): lax.all_gather(jnp.concatenate([wi_gate.T, wi_lin.T, wo], 0), 'z', axis=0)  26.6 us
    ppermute x16, starting transfers between devices, shifted(): return lax.ppermute(value, axis, [((i + step) % 4, i) for i in range(4)])  23.8 us
    all_to_all x1, blocking collectives, local(): pair = lax.all_to_all(pair, 'z', 0, 0, tiled=True)  20.2 us
    all_to_all x3, waiting for transfers between devices, sum_over(): return jnp.sum(lax.all_to_all(copies, axis, 0, 0, tiled=True), 0)  19.2 us
    ppermute x16, waiting for transfers between devices, shifted(): return lax.ppermute(value, axis, [((i + step) % 4, i) for i in range(4)])  15.4 us
    all_to_all x3, starting transfers between devices, sum_over(): return jnp.sum(lax.all_to_all(copies, axis, 0, 0, tiled=True), 0)  14.9 us
  transfers between devices with their start and end apart: 25, of which 17 were waited for; matrix products, arithmetic and copies ran while one was open for 2% of the time, Pallas kernels for 2%

profile of v3, /device:TPU:8, one launch (start us, length us, event | category | flops | bytes accessed | tf_op | source)
XLA Modules:
  0.0 266.4 jit_solution(1515428982676240604)
XLA Ops:
  7.2 2.2 pad_maximum_fusion.2
  9.6 20.2 %all_to_all.31 = bf16[8,2,16,512]{3,2,1,0:T(8,128)(2,1)S(1)} all-to-all(bf16[8,2,16,512]{3,2,1,0:T(8,128)(2,1)S(1)} %pad_maximum_fusion.5), channel_id=1, replica_groups=mesh['z'=8,'x'=4,'y'=4,'c'=2] {'z'}, dimensions={0} | all-to-all | bytes 524288 | tf_op jit(solution)/shard_map/all_to_all | solution.py:202
  29.8 0.5 collective-permute-start.9
  30.4 1.6 collective-permute-start.11
  32.0 2.8 %collective-permute-start = (bf16[8,16,512]{2,1,0:T(8,128)(2,1)S(1)}, bf16[8,16,512]{2,1,0:T(8,128)(2,1)S(1)}, u32[]{:S(2)}, u32[]{:S(2)}) collective-permute-start(bf16[8,16,512]{2,1,0:T(8,128)(2,1)S(1)} %get-tuple-element.32), channel_id=1, source_target_pairs={{8,0},{16,8},{24,16},{0,24},{9,1},{17,9},{25,17},{1,25},{10,2},{18... | collective-permute-start | bytes 393224 | tf_op jit(solution)/shard_map/ppermute | solution.py:26
  34.7 0.3 collective-permute-done.9
  35.0 1.2 collective-permute-start.10
  36.3 0.1 collective-permute-done.11
  36.4 0.9 collective-permute-start.12
  37.3 0.2 collective-permute-done
  37.4 3.4 %collective-permute-start.1 = (bf16[4,16,512]{2,1,0:T(8,128)(2,1)S(1)}, bf16[4,16,512]{2,1,0:T(8,128)(2,1)S(1)}, u32[]{:S(2)}, u32[]{:S(2)}) collective-permute-start(bf16[4,16,512]{2,1,0:T(8,128)(2,1)S(1)} %slice.93), channel_id=1, source_target_pairs={{8,0},{16,8},{24,16},{0,24},{9,1},{17,9},{25,17},{1,25},{10,2},{18... | collective-permute-start | bytes 196616 | tf_op jit(solution)/shard_map/ppermute | solution.py:26
  41.0 0.9 collective-permute-done.12
  41.9 0.1 fusion.11
  42.0 3.2 %collective-permute-start.13 = (bf16[4,8,16,512]{3,2,1,0:T(8,128)(2,1)S(1)}, bf16[4,8,16,512]{3,2,1,0:T(8,128)(2,1)S(1)}, u32[]{:S(2)}, u32[]{:S(2)}) collective-permute-start(bf16[4,8,16,512]{3,2,1,0:T(8,128)(2,1)S(1)} %get-tuple-element.27), channel_id=1, source_target_pairs={{8,0},{16,8},{24,16},{0,24},{9,1},{17,9},{25,17},{1,25},{10,2},{18... | collective-permute-start | bytes 1572872 | tf_op jit(solution)/shard_map/ppermute | solution.py:26
  45.3 1.9 collective-permute-done.3
  47.2 0.1 fusion.12
  47.3 2.1 collective-permute-start.4
  49.4 4.5 %collective-permute-done.13 = bf16[4,8,16,512]{3,2,1,0:T(8,128)(2,1)S(1)} collective-permute-done((bf16[4,8,16,512]{3,2,1,0:T(8,128)(2,1)S(1)}, bf16[4,8,16,512]{3,2,1,0:T(8,128)(2,1)S(1)}, u32[]{:S(2)}, u32[]{:S(2)}) %collective-permute-start.13) | collective-permute-done | bytes 524320 | tf_op jit(solution)/shard_map/ppermute | solution.py:26
  53.8 3.4 %collective-permute-start.14 = (bf16[4,4,16,512]{3,2,1,0:T(8,128)(2,1)S(1)}, bf16[4,4,16,512]{3,2,1,0:T(8,128)(2,1)S(1)}, u32[]{:S(2)}, u32[]{:S(2)}) collective-permute-start(bf16[4,4,16,512]{3,2,1,0:T(8,128)(2,1)S(1)} %slice.100), channel_id=1, source_target_pairs={{8,0},{16,8},{24,16},{0,24},{9,1},{17,9},{25,17},{1,25},{10,2},{18... | collective-permute-start | bytes 786440 | tf_op jit(solution)/shard_map/ppermute | solution.py:26
  57.4 4.3 %collective-permute-start.5 = (bf16[4,4,16,512]{3,2,1,0:T(8,128)(2,1)S(1)}, bf16[4,4,16,512]{3,2,1,0:T(8,128)(2,1)S(1)}, u32[]{:S(2)}, u32[]{:S(2)}) collective-permute-start(bf16[4,4,16,512]{3,2,1,0:T(8,128)(2,1)S(1)} %slice.95), channel_id=1, source_target_pairs={{2,0},{4,2},{6,4},{0,6},{3,1},{5,3},{7,5},{1,7},{10,8},{12,10},{14... | collective-permute-start | bytes 786440 | tf_op jit(solution)/shard_map/ppermute | solution.py:26
  61.9 3.1 %collective-permute-done.16 = bf16[4,4,16,512]{3,2,1,0:T(8,128)(2,1)S(1)} collective-permute-done((bf16[4,4,16,512]{3,2,1,0:T(8,128)(2,1)S(1)}, bf16[4,4,16,512]{3,2,1,0:T(8,128)(2,1)S(1)}, u32[]{:S(2)}, u32[]{:S(2)}) %collective-permute-start.16) | collective-permute-done | bytes 262176 | tf_op jit(solution)/shard_map/ppermute | solution.py:26
  65.0 0.3 pad_maximum_fusion.1.cot0
  65.3 0.1 collective-permute-start.17
  65.4 0.3 collective-permute-done.5
  65.7 4.2 %collective-permute-done.7 = bf16[4,4,16,512]{3,2,1,0:T(8,128)(2,1)S(1)} collective-permute-done((bf16[4,4,16,512]{3,2,1,0:T(8,128)(2,1)S(1)}, bf16[4,4,16,512]{3,2,1,0:T(8,128)(2,1)S(1)}, u32[]{:S(2)}, u32[]{:S(2)}) %collective-permute-start.7) | collective-permute-done | bytes 262176 | tf_op jit(solution)/shard_map/ppermute | solution.py:26
  69.9 0.3 pad_maximum_fusion.tok0
  70.2 0.1 collective-permute-start.8
  70.3 1.3 copy-done.12
  71.6 2.8 %collective-permute-done.8.tok1 = bf16[4,4,8,16,512]{4,3,2,1,0:T(8,128)(2,1)S(1)} collective-permute-done((bf16[4,4,8,16,512]{4,3,2,1,0:T(8,128)(2,1)S(1)}, bf16[4,4,8,16,512]{4,3,2,1,0:T(8,128)(2,1)S(1)}, u32[]{:S(2)}, u32[]{:S(2)}) %collective-permute-start.8) | collective-permute-done | bytes 2097184 | tf_op jit(solution)/shard_map/ppermute | solution.py:30
  74.5 1.4 copy-done
  75.9 26.6 %all-gather.3.cloned.1.call-done = bf16[7680,512]{1,0:T(8,128)(2,1)} async-done(((bf16[960,512]{1,0:T(8,128)(2,1)}), bf16[7680,512]{1,0:T(8,128)(2,1)}) %all-gather.3.cloned.1.call-update) | async-done | bytes 7864336 | tf_op jit(solution)/shard_map/all_gather | solution.py:199
  102.5 1.6 copy-done.1
  104.0 14.6 %shard_map.195 = (bf16[8,960,512]{2,1,0:T(8,128)(2,1)}, bf16[512,640]{1,0:T(8,128)(2,1)S(1)}) custom-call(bf16[4,4,8,16,512]{4,3,2,1,0:T(8,128)(2,1)S(1)} %pad_maximum_fusion.tok0, bf16[4,4,8,16,512]{4,3,2,1,0:T(8,128)(2,1)S(1)} %copy-done.1, bf16[4,4,8,16,512]{4,3,2,1,0:T(8,128)(2,1)} %copy-done.3, bf16[4,4,8,16,512]{4,3,2,1,0:T(8,128)(2,1)} %copy-done.12, ...), custom_call_target="tpu_custom_call" | custom-call | flops 8053063680 | bytes 25000000 | tf_op jit(solution)/shard_map/pallas_call | solution.py:141
  118.7 0.1 add.102.place
  118.8 6.4 %shard_map.196 = bf16[2,16,8,16,512]{4,3,2,1,0:T(8,128)(2,1)S(1)} custom-call(s32[16]{0:T(128)S(1)} %add.102.place, bf16[512,640]{1,0:T(8,128)(2,1)S(1)} %get-tuple-element.15.hidden, bf16[8,960,512]{2,1,0:T(8,128)(2,1)} %bitcast.75), custom_call_target="tpu_custom_call" | custom-call | flops 2684354560 | bytes 10000000 | tf_op jit(solution)/shard_map/pallas_call | solution.py:165
  125.3 0.2 slice_bitcast_fusion
  125.5 0.1 collective-permute-start.18
  125.6 4.1 %collective-permute-done.18 = bf16[16,8,16,512]{3,2,1,0:T(8,128)(2,1)S(1)} collective-permute-done((bf16[16,8,16,512]{3,2,1,0:T(8,128)(2,1)S(1)}, bf16[16,8,16,512]{3,2,1,0:T(8,128)(2,1)S(1)}, u32[]{:S(2)}, u32[]{:S(2)}) %collective-permute-start.18) | collective-permute-done | bytes 2097184 | tf_op jit(solution)/shard_map/ppermute | solution.py:30
  129.7 0.9 fusion
  130.7 34.4 %all_to_all.32 = bf16[16,8,16,512]{3,2,1,0:T(8,128)(2,1)S(1)} all-to-all(bf16[16,8,16,512]{3,2,1,0:T(8,128)(2,1)S(1)} %fusion), channel_id=1, replica_groups=mesh['z'=8,'x'=4,'y'=4,'c'=2] {'x','y'}, dimensions={0} | all-to-all | bytes 4194304 | tf_op jit(solution)/shard_map/all_to_all | solution.py:216
  165.0 0.4 reduce_sum.75
  165.4 14.4 %all_to_all.33 = bf16[8,16,512]{2,1,0:T(8,128)(2,1)S(1)} all-to-all(bf16[8,16,512]{2,1,0:T(8,128)(2,1)S(1)} %reduce_sum.75), channel_id=1, replica_groups=mesh['z'=8,'x'=4,'y'=4,'c'=2] {'z'}, dimensions={0} | all-to-all | bytes 262144 | tf_op jit(solution)/shard_map/all_to_all | solution.py:218
  179.8 29.9 %reduce-scatter.2.cloned.1.call-done = bf16[1,960,512]{2,1,0:T(8,128)(2,1)} async-done(((bf16[8,960,512]{2,1,0:T(8,128)(2,1)}), bf16[1,960,512]{2,1,0:T(8,128)(2,1)}) %reduce-scatter.2.cloned.1.call-update) | async-done | bytes 983056 | tf_op jit(solution)/shard_map/reduce_scatter | solution.py:208
  209.7 2.8 %multiply_add_fusion = (f32[960,512]{1,0:T(8,128)}, f32[960]{0:T(1024)S(1)}, f32[960,512]{1,0:T(8,128)S(1)}) fusion(bf16[960,512]{1,0:T(8,128)(2,1)} %bitcast.79), kind=kLoop, calls=%fused_computation.9 | loop fusion | flops 2456640 | bytes 4919040 | tf_op jit(solution)/shard_map/add | solution.py:223
  212.5 0.6 broadcast_in_dim.6
  213.1 4.4 %all-to-all-start.3 = ((f32[8,1,960]{2,1,0:T(1,128)}), f32[8,1,960]{2,1,0:T(1,128)S(1)}, u32[]{:S(2)}, u32[]{:S(2)}) async-start(f32[8,1,960]{2,1,0:T(1,128)} %broadcast_in_dim.6), calls=%async_computation.4 | async-start | bytes 65536 | tf_op jit(solution)/shard_map/all_to_all | solution.py:44
  218.2 1.7 reduce_sum.78
  219.9 5.6 %all-to-all-done.3 = f32[8,1,960]{2,1,0:T(1,128)S(1)} async-done(((f32[8,1,960]{2,1,0:T(1,128)}), f32[8,1,960]{2,1,0:T(1,128)S(1)}, u32[]{:S(2)}, u32[]{:S(2)}) %all-to-all-start.3) | async-done | bytes 30752 | tf_op jit(solution)/shard_map/all_to_all | solution.py:44
  225.7 1.6 multiply_divide_fusion
  227.2 1.7 reduce_sum.79
  229.0 0.1 collective-permute-start.19
  229.2 1.1 collective-permute-done.19
  230.3 0.7 broadcast_in_dim.7
  231.0 7.2 %all-to-all-start.4 = ((f32[16,6,512]{2,1,0:T(8,128)}), f32[16,6,512]{2,1,0:T(8,128)S(1)}, u32[]{:S(2)}, u32[]{:S(2)}) async-start(f32[16,6,512]{2,1,0:T(8,128)} %broadcast_in_dim.7), calls=%async_computation.5 | async-start | bytes 524288 | tf_op jit(solution)/shard_map/all_to_all | solution.py:44
  238.2 0.7 fusion.15
  238.9 6.7 %all-to-all-done.4 = f32[16,6,512]{2,1,0:T(8,128)S(1)} async-done(((f32[16,6,512]{2,1,0:T(8,128)}), f32[16,6,512]{2,1,0:T(8,128)S(1)}, u32[]{:S(2)}, u32[]{:S(2)}) %all-to-all-start.4) | async-done | bytes 196640 | tf_op jit(solution)/shard_map/all_to_all | solution.py:44
  245.6 0.1 fusion.3
  245.8 0.6 broadcast_in_dim.8
  246.4 3.3 %all-to-all-start.5 = ((f32[8,3,1]{1,2,0:T(1,128)}), f32[8,3,1]{1,2,0:T(1,128)S(1)}, u32[]{:S(2)}, u32[]{:S(2)}) async-start(f32[8,3,1]{1,2,0:T(1,128)} %broadcast_in_dim.8), calls=%async_computation.6 | async-start | bytes 8192 | tf_op jit(solution)/shard_map/all_to_all | solution.py:44
  249.7 0.6 fusion.14
  250.3 6.9 %all-to-all-done.5 = f32[8,3,1]{1,2,0:T(1,128)S(1)} async-done(((f32[8,3,1]{1,2,0:T(1,128)}), f32[8,3,1]{1,2,0:T(1,128)S(1)}, u32[]{:S(2)}, u32[]{:S(2)}) %all-to-all-start.5) | async-done | bytes 128 | tf_op jit(solution)/shard_map/all_to_all | solution.py:44
  257.3 0.2 multiply_multiply_fusion
  257.6 1.3 slice_bitcast_fusion.2
  258.9 0.7 copy.50
  (70 shorter events, 1.2 us)
Async XLA Ops:
  7.2 2.4 copy-start.5
  7.2 2.4 copy-start.4
  7.2 95.3 %all-gather.3.cloned.1.call-start = ((), (), s32[]{:S(2)}) async-start(), calls=%async_computation.8 | async-start | bytes 8847360 | tf_op jit(solution)/shard_map/all_gather | solution.py:199
  9.5 200.2 %reduce-scatter.2.cloned.1.call-start = ((), (), s32[]{:S(2)}) async-start(), calls=%async_computation.7 | async-start | bytes 8847360 | tf_op jit(solution)/shard_map/reduce_scatter | solution.py:208
  29.8 5.2 %collective-permute-start.9 = (bf16[8,16,512]{2,1,0:T(8,128)(2,1)S(1)}, bf16[8,16,512]{2,1,0:T(8,128)(2,1)S(1)}, u32[]{:S(2)}, u32[]{:S(2)}) collective-permute-start(bf16[8,16,512]{2,1,0:T(8,128)(2,1)S(1)} %get-tuple-element.33), channel_id=1, source_target_pairs={{2,0},{4,2},{6,4},{0,6},{3,1},{5,3},{7,5},{1,7},{10,8},{12,10},{14... | collective-permute-start | bytes 393224 | tf_op jit(solution)/shard_map/ppermute | solution.py:26
  30.4 6.0 %collective-permute-start.11 = (bf16[8,16,512]{2,1,0:T(8,128)(2,1)S(1)}, bf16[8,16,512]{2,1,0:T(8,128)(2,1)S(1)}, u32[]{:S(2)}, u32[]{:S(2)}) collective-permute-start(bf16[8,16,512]{2,1,0:T(8,128)(2,1)S(1)} %get-tuple-element.33), channel_id=1, source_target_pairs={{6,0},{0,2},{2,4},{4,6},{7,1},{1,3},{3,5},{5,7},{14,8},{8,10},{10,... | collective-permute-start | bytes 393224 | tf_op jit(solution)/shard_map/ppermute | solution.py:26
  32.0 5.5 %collective-permute-start = (bf16[8,16,512]{2,1,0:T(8,128)(2,1)S(1)}, bf16[8,16,512]{2,1,0:T(8,128)(2,1)S(1)}, u32[]{:S(2)}, u32[]{:S(2)}) collective-permute-start(bf16[8,16,512]{2,1,0:T(8,128)(2,1)S(1)} %get-tuple-element.32), channel_id=1, source_target_pairs={{8,0},{16,8},{24,16},{0,24},{9,1},{17,9},{25,17},{1,25},{10,2},{18... | collective-permute-start | bytes 393224 | tf_op jit(solution)/shard_map/ppermute | solution.py:26
  34.7 6.2 %collective-permute-start.2 = (bf16[8,16,512]{2,1,0:T(8,128)(2,1)S(1)}, bf16[8,16,512]{2,1,0:T(8,128)(2,1)S(1)}, u32[]{:S(2)}, u32[]{:S(2)}) collective-permute-start(bf16[8,16,512]{2,1,0:T(8,128)(2,1)S(1)} %get-tuple-element.32), channel_id=1, source_target_pairs={{24,0},{0,8},{8,16},{16,24},{25,1},{1,9},{9,17},{17,25},{26,2},{2,... | collective-permute-start | bytes 393224 | tf_op jit(solution)/shard_map/ppermute | solution.py:26
  35.0 6.0 %collective-permute-start.10 = (bf16[4,16,512]{2,1,0:T(8,128)(2,1)S(1)}, bf16[4,16,512]{2,1,0:T(8,128)(2,1)S(1)}, u32[]{:S(2)}, u32[]{:S(2)}) collective-permute-start(bf16[4,16,512]{2,1,0:T(8,128)(2,1)S(1)} %slice.98), channel_id=1, source_target_pairs={{2,0},{4,2},{6,4},{0,6},{3,1},{5,3},{7,5},{1,7},{10,8},{12,10},{14... | collective-permute-start | bytes 196616 | tf_op jit(solution)/shard_map/ppermute | solution.py:26
  36.4 5.6 %collective-permute-start.12 = (bf16[4,16,512]{2,1,0:T(8,128)(2,1)S(1)}, bf16[4,16,512]{2,1,0:T(8,128)(2,1)S(1)}, u32[]{:S(2)}, u32[]{:S(2)}) collective-permute-start(bf16[4,16,512]{2,1,0:T(8,128)(2,1)S(1)} %slice.99), channel_id=1, source_target_pairs={{6,0},{0,2},{2,4},{4,6},{7,1},{1,3},{3,5},{5,7},{14,8},{8,10},{10,... | collective-permute-start | bytes 196616 | tf_op jit(solution)/shard_map/ppermute | solution.py:26
  37.4 7.8 %collective-permute-start.1 = (bf16[4,16,512]{2,1,0:T(8,128)(2,1)S(1)}, bf16[4,16,512]{2,1,0:T(8,128)(2,1)S(1)}, u32[]{:S(2)}, u32[]{:S(2)}) collective-permute-start(bf16[4,16,512]{2,1,0:T(8,128)(2,1)S(1)} %slice.93), channel_id=1, source_target_pairs={{8,0},{16,8},{24,16},{0,24},{9,1},{17,9},{25,17},{1,25},{10,2},{18... | collective-permute-start | bytes 196616 | tf_op jit(solution)/shard_map/ppermute | solution.py:26
  40.9 6.2 %collective-permute-start.3 = (bf16[4,16,512]{2,1,0:T(8,128)(2,1)S(1)}, bf16[4,16,512]{2,1,0:T(8,128)(2,1)S(1)}, u32[]{:S(2)}, u32[]{:S(2)}) collective-permute-start(bf16[4,16,512]{2,1,0:T(8,128)(2,1)S(1)} %slice.94), channel_id=1, source_target_pairs={{24,0},{0,8},{8,16},{16,24},{25,1},{1,9},{9,17},{17,25},{26,2},{2,... | collective-permute-start | bytes 196616 | tf_op jit(solution)/shard_map/ppermute | solution.py:26
  42.0 11.8 %collective-permute-start.13 = (bf16[4,8,16,512]{3,2,1,0:T(8,128)(2,1)S(1)}, bf16[4,8,16,512]{3,2,1,0:T(8,128)(2,1)S(1)}, u32[]{:S(2)}, u32[]{:S(2)}) collective-permute-start(bf16[4,8,16,512]{3,2,1,0:T(8,128)(2,1)S(1)} %get-tuple-element.27), channel_id=1, source_target_pairs={{8,0},{16,8},{24,16},{0,24},{9,1},{17,9},{25,17},{1,25},{10,2},{18... | collective-permute-start | bytes 1572872 | tf_op jit(solution)/shard_map/ppermute | solution.py:26
  45.3 12.0 %collective-permute-start.15 = (bf16[4,8,16,512]{3,2,1,0:T(8,128)(2,1)S(1)}, bf16[4,8,16,512]{3,2,1,0:T(8,128)(2,1)S(1)}, u32[]{:S(2)}, u32[]{:S(2)}) collective-permute-start(bf16[4,8,16,512]{3,2,1,0:T(8,128)(2,1)S(1)} %get-tuple-element.27), channel_id=1, source_target_pairs={{24,0},{0,8},{8,16},{16,24},{25,1},{1,9},{9,17},{17,25},{26,2},{2,... | collective-permute-start | bytes 1572872 | tf_op jit(solution)/shard_map/ppermute | solution.py:26
  47.3 10.1 %collective-permute-start.4 = (bf16[4,8,16,512]{3,2,1,0:T(8,128)(2,1)S(1)}, bf16[4,8,16,512]{3,2,1,0:T(8,128)(2,1)S(1)}, u32[]{:S(2)}, u32[]{:S(2)}) collective-permute-start(bf16[4,8,16,512]{3,2,1,0:T(8,128)(2,1)S(1)} %get-tuple-element.29), channel_id=1, source_target_pairs={{2,0},{4,2},{6,4},{0,6},{3,1},{5,3},{7,5},{1,7},{10,8},{12,10},{14... | collective-permute-start | bytes 1572872 | tf_op jit(solution)/shard_map/ppermute | solution.py:26
  49.3 12.4 %collective-permute-start.6 = (bf16[4,8,16,512]{3,2,1,0:T(8,128)(2,1)S(1)}, bf16[4,8,16,512]{3,2,1,0:T(8,128)(2,1)S(1)}, u32[]{:S(2)}, u32[]{:S(2)}) collective-permute-start(bf16[4,8,16,512]{3,2,1,0:T(8,128)(2,1)S(1)} %get-tuple-element.29), channel_id=1, source_target_pairs={{6,0},{0,2},{2,4},{4,6},{7,1},{1,3},{3,5},{5,7},{14,8},{8,10},{10,... | collective-permute-start | bytes 1572872 | tf_op jit(solution)/shard_map/ppermute | solution.py:26
  53.8 8.0 %collective-permute-start.14 = (bf16[4,4,16,512]{3,2,1,0:T(8,128)(2,1)S(1)}, bf16[4,4,16,512]{3,2,1,0:T(8,128)(2,1)S(1)}, u32[]{:S(2)}, u32[]{:S(2)}) collective-permute-start(bf16[4,4,16,512]{3,2,1,0:T(8,128)(2,1)S(1)} %slice.100), channel_id=1, source_target_pairs={{8,0},{16,8},{24,16},{0,24},{9,1},{17,9},{25,17},{1,25},{10,2},{18... | collective-permute-start | bytes 786440 | tf_op jit(solution)/shard_map/ppermute | solution.py:26
  57.3 7.7 %collective-permute-start.16 = (bf16[4,4,16,512]{3,2,1,0:T(8,128)(2,1)S(1)}, bf16[4,4,16,512]{3,2,1,0:T(8,128)(2,1)S(1)}, u32[]{:S(2)}, u32[]{:S(2)}) collective-permute-start(bf16[4,4,16,512]{3,2,1,0:T(8,128)(2,1)S(1)} %slice.101), channel_id=1, source_target_pairs={{24,0},{0,8},{8,16},{16,24},{25,1},{1,9},{9,17},{17,25},{26,2},{2,... | collective-permute-start | bytes 786440 | tf_op jit(solution)/shard_map/ppermute | solution.py:26
  57.4 8.3 %collective-permute-start.5 = (bf16[4,4,16,512]{3,2,1,0:T(8,128)(2,1)S(1)}, bf16[4,4,16,512]{3,2,1,0:T(8,128)(2,1)S(1)}, u32[]{:S(2)}, u32[]{:S(2)}) collective-permute-start(bf16[4,4,16,512]{3,2,1,0:T(8,128)(2,1)S(1)} %slice.95), channel_id=1, source_target_pairs={{2,0},{4,2},{6,4},{0,6},{3,1},{5,3},{7,5},{1,7},{10,8},{12,10},{14... | collective-permute-start | bytes 786440 | tf_op jit(solution)/shard_map/ppermute | solution.py:26
  61.8 8.1 %collective-permute-start.7 = (bf16[4,4,16,512]{3,2,1,0:T(8,128)(2,1)S(1)}, bf16[4,4,16,512]{3,2,1,0:T(8,128)(2,1)S(1)}, u32[]{:S(2)}, u32[]{:S(2)}) collective-permute-start(bf16[4,4,16,512]{3,2,1,0:T(8,128)(2,1)S(1)} %slice.96), channel_id=1, source_target_pairs={{6,0},{0,2},{2,4},{4,6},{7,1},{1,3},{3,5},{5,7},{14,8},{8,10},{10,... | collective-permute-start | bytes 786440 | tf_op jit(solution)/shard_map/ppermute | solution.py:26
  65.3 5.0 %copy-start.3 = (bf16[4,4,8,16,512]{4,3,2,1,0:T(8,128)(2,1)}, bf16[4,4,8,16,512]{4,3,2,1,0:T(8,128)(2,1)S(1)}, u32[]{:S(2)}) copy-start(bf16[4,4,8,16,512]{4,3,2,1,0:T(8,128)(2,1)S(1)} %pad_maximum_fusion.1.cot0) | copy-start | bytes 6291460
  65.3 5.1 %collective-permute-start.17 = (bf16[4,4,8,16,512]{4,3,2,1,0:T(8,128)(2,1)S(1)}, bf16[4,4,8,16,512]{4,3,2,1,0:T(8,128)(2,1)S(1)}, u32[]{:S(2)}, u32[]{:S(2)}) collective-permute-start(bf16[4,4,8,16,512]{4,3,2,1,0:T(8,128)(2,1)S(1)} %pad_maximum_fusion.1.cot0), channel_id=1, source_target_pairs={{0,1},{1,0},{2,3},{3,2},{4,5},{5,4},{6,7},{7,6},{8,9},{9,8},{10,11... | collective-permute-start | bytes 6291464 | tf_op jit(solution)/shard_map/ppermute | solution.py:30
  70.2 4.2 %collective-permute-start.8 = (bf16[4,4,8,16,512]{4,3,2,1,0:T(8,128)(2,1)S(1)}, bf16[4,4,8,16,512]{4,3,2,1,0:T(8,128)(2,1)S(1)}, u32[]{:S(2)}, u32[]{:S(2)}) collective-permute-start(bf16[4,4,8,16,512]{4,3,2,1,0:T(8,128)(2,1)S(1)} %pad_maximum_fusion.tok0), channel_id=1, source_target_pairs={{0,1},{1,0},{2,3},{3,2},{4,5},{5,4},{6,7},{7,6},{8,9},{9,8},{10,11... | collective-permute-start | bytes 6291464 | tf_op jit(solution)/shard_map/ppermute | solution.py:30
  70.3 1.3 copy-start.12
  74.5 1.4 copy-start
  102.5 1.6 copy-start.1
  125.5 4.2 %collective-permute-start.18 = (bf16[16,8,16,512]{3,2,1,0:T(8,128)(2,1)S(1)}, bf16[16,8,16,512]{3,2,1,0:T(8,128)(2,1)S(1)}, u32[]{:S(2)}, u32[]{:S(2)}) collective-permute-start(bf16[16,8,16,512]{3,2,1,0:T(8,128)(2,1)S(1)} %slice_bitcast_fusion), channel_id=1, source_target_pairs={{0,1},{1,0},{2,3},{3,2},{4,5},{5,4},{6,7},{7,6},{8,9},{9,8},{10,11... | collective-permute-start | bytes 6291464 | tf_op jit(solution)/shard_map/ppermute | solution.py:30
  209.7 8.5 %copy-start.8 = (f32[320]{0:T(512)S(1)}, f32[320]{0:T(512)}, u32[]{:S(2)}) copy-start(f32[320]{0:T(512)} %param.18) | copy-start | bytes 3844
  209.7 8.5 %copy-start.7 = (f32[320]{0:T(512)S(1)}, f32[320]{0:T(512)}, u32[]{:S(2)}) copy-start(f32[320]{0:T(512)} %param.20) | copy-start | bytes 3844
  209.7 8.5 %copy-start.6 = (f32[320]{0:T(512)S(1)}, f32[320]{0:T(512)}, u32[]{:S(2)}) copy-start(f32[320]{0:T(512)} %param.21) | copy-start | bytes 3844
  212.5 13.1 %copy-start.2 = (bf16[1,960,512]{2,1,0:T(8,128)(2,1)S(1)}, bf16[1,960,512]{2,1,0:T(8,128)(2,1)}, u32[]{:S(2)}) copy-start(bf16[1,960,512]{2,1,0:T(8,128)(2,1)} %reduce-scatter.2.cloned.1.call-done) | copy-start | bytes 2949124
  213.1 12.4 %all-to-all-start.3 = ((f32[8,1,960]{2,1,0:T(1,128)}), f32[8,1,960]{2,1,0:T(1,128)S(1)}, u32[]{:S(2)}, u32[]{:S(2)}) async-start(f32[8,1,960]{2,1,0:T(1,128)} %broadcast_in_dim.6), calls=%async_computation.4 | async-start | bytes 65536 | tf_op jit(solution)/shard_map/all_to_all | solution.py:44
  227.2 18.4 %copy-start.9 = (f32[512]{0:T(512)S(1)}, f32[512]{0:T(512)}, u32[]{:S(2)}) copy-start(f32[512]{0:T(512)} %param.22) | copy-start | bytes 6148
  227.2 18.4 %copy-start.10 = (f32[512]{0:T(512)S(1)}, f32[512]{0:T(512)}, u32[]{:S(2)}) copy-start(f32[512]{0:T(512)} %param.19) | copy-start | bytes 6148
  227.2 18.4 %copy-start.11 = (f32[512]{0:T(512)S(1)}, f32[512]{0:T(512)}, u32[]{:S(2)}) copy-start(f32[512]{0:T(512)} %param.17) | copy-start | bytes 6148
  229.0 1.3 collective-permute-start.19
  231.0 14.6 %all-to-all-start.4 = ((f32[16,6,512]{2,1,0:T(8,128)}), f32[16,6,512]{2,1,0:T(8,128)S(1)}, u32[]{:S(2)}, u32[]{:S(2)}) async-start(f32[16,6,512]{2,1,0:T(8,128)} %broadcast_in_dim.7), calls=%async_computation.5 | async-start | bytes 524288 | tf_op jit(solution)/shard_map/all_to_all | solution.py:44
  246.4 10.8 %all-to-all-start.5 = ((f32[8,3,1]{1,2,0:T(1,128)}), f32[8,3,1]{1,2,0:T(1,128)S(1)}, u32[]{:S(2)}, u32[]{:S(2)}) async-start(f32[8,3,1]{1,2,0:T(1,128)} %broadcast_in_dim.8), calls=%async_computation.6 | async-start | bytes 8192 | tf_op jit(solution)/shard_map/all_to_all | solution.py:44
Sparse Core Ops, SparseCore 0:
  9.8 92.5 all-gather.2
  118.8 90.8 reduce-scatter.1

commit v4 on v3

--- a/solution.py
+++ b/solution.py
@@ -19,6 +19,7 @@
 decay_rate = 0.8
 gelu_coeff = math.sqrt(2.0 / math.pi)
 COL = ("x", "y", "c")
+SCALE = 1.0 / math.sqrt(4096.0)
 VMEM = 48 * 1024 * 1024
 
 
@@ -181,6 +182,16 @@
     )(place, hidden, weight)
 
 
+def settle_kernel(value, result):
+    result[...] = value[...]
+
+
+def settle(value):
+    return pl.pallas_call(
+        settle_kernel, out_shape=jax.ShapeDtypeStruct(value.shape, value.dtype)
+    )(value)
+
+
 def local(
     tokens,
     cotangent,
@@ -215,31 +226,26 @@
     part = (part[0].astype(jnp.float32) + swap(part[1]).astype(jnp.float32)).astype(bf16)
     part = lax.all_to_all(part, ("x", "y"), 0, 0, tiled=True)
     part = jnp.sum(part.astype(jnp.float32), 0).astype(bf16)
-    grad_tokens = lax.all_to_all(part, "z", 0, 0, tiled=True).reshape(tokens.shape)
+    grad_tokens = settle(lax.all_to_all(part, "z", 0, 0, tiled=True).reshape(tokens.shape))
     grad_w, grad_tokens = lax.optimization_barrier((grad_w, grad_tokens))
 
-    grad = grad_w.astype(jnp.float32) * (1.0 / math.sqrt(4096.0))
     keep = 1.0 - decay_rate
-    squares = grad * grad + 1e-30
-    over_model = sum_over(jnp.sum(squares, 1), "z", NZ)
-    hidden_old = jnp.concatenate([cols_gate, cols_lin, rows_out])
+    first = grad_w.astype(jnp.float32) * SCALE
+    first = jnp.sum(first * first + 1e-30, 1)
+    first, grad_w = lax.optimization_barrier((first, grad_w))
+    grad = lax.optimization_barrier(grad_w.reshape(3, FB, DB).astype(jnp.float32) * SCALE)
+    over_model = sum_over(first, "z", NZ).reshape(3, FB)
+    plain = jnp.sum(grad * grad + 1e-30, 1)
+    hidden_old = jnp.stack([cols_gate, cols_lin, rows_out], 0)
     hidden_new = decay_rate * hidden_old + keep * over_model / D
     model_old = jnp.stack([rows_gate, rows_lin, cols_out], 0)
-    weighted = grad * grad / hidden_new[:, None]
-    over_hidden = sum_col(
-        jnp.concatenate(
-            [
-                jnp.sum(squares.reshape(3, FB, DB), 1),
-                jnp.sum(weighted.reshape(3, FB, DB), 1),
-            ],
-            0,
-        )
-    )
+    weighted = jnp.sum(grad * grad * (1.0 / hidden_new).reshape(3, FB, 1), 1)
+    over_hidden = sum_col(jnp.concatenate([plain, weighted], 0))
     model_new = decay_rate * model_old + keep * over_hidden[:3] / FF
     totals = sum_over(jnp.sum(over_hidden[3:] / model_new, 1, keepdims=True), "z", NZ)
     factor = -rate[0] / jnp.sqrt(totals / (D * FF) + 1e-06)
     update = (
-        grad.reshape(3, FB, DB)
+        grad
         * lax.rsqrt(hidden_new).reshape(3, FB, 1)
         * (factor * lax.rsqrt(model_new)).reshape(3, 1, DB)
     )
@@ -249,10 +255,10 @@
         update[1].T,
         update[2],
         model_new[0],
-        hidden_new[:FB],
+        hidden_new[0],
         model_new[1],
-        hidden_new[FB : 2 * FB],
-        hidden_new[2 * FB :],
+        hidden_new[1],
+        hidden_new[2],
         model_new[2],
     )
 

time: 267 us -> 262 us (0.981)
  blocking collectives: 68.9 us -> 54.6 us
  waiting for transfers between devices: 99.2 us -> 107 us
  other arithmetic: 13 us -> 9.19 us
  starting transfers between devices: 39.1 us -> 42.9 us
    all_to_all x1 -> x0, blocking collectives: 14.4 us -> none  [local(): lax.all_to_all(part, 'z', 0, 0, tiled=True).reshape(tokens.shape)]
    all_to_all x0 -> x1, waiting for transfers between devices: none -> 10.7 us  [local(): lax.all_to_all(part, 'z', 0, 0, tiled=True).reshape(tokens.shape)]
    all_to_all x0 -> x1, starting transfers between devices: none -> 3.8 us  [local(): lax.all_to_all(part, 'z', 0, 0, tiled=True).reshape(tokens.shape)]
    reduce_scatter x1, waiting for transfers between devices: 29.9 us -> 26.8 us  [local(): grad_w = lax.psum_scatter(grad_w, 'z', scatter_dimension=0)]
    add x1 -> x0, other arithmetic: 2.84 us -> none  [local(): squares = grad * grad + 1e-30]
  transfers between devices with their start and end apart: 25 -> 26, of which waited for: 17 -> 18; matrix products, arithmetic and copies ran while one was open for 2% -> 2% of each run, Pallas kernels for 2% -> 3%
where the time goes in v4:
time: 262 us
  waiting for transfers between devices  107 us (41%)
  blocking collectives  54.6 us (21%)
  starting transfers between devices  42.9 us (16%)
  Pallas kernels  22.5 us (9%)
  between operations  15.1 us (6%)
  local copies, waits for them, and re-layouts  9.94 us (4%)
  other arithmetic  9.19 us (4%)
    all_to_all x1, blocking collectives, local(): part = lax.all_to_all(part, ('x', 'y'), 0, 0, tiled=True)  34.4 us
    reduce_scatter x1, waiting for transfers between devices, local(): grad_w = lax.psum_scatter(grad_w, 'z', scatter_dimension=0)  26.8 us
    all_gather x1, waiting for transfers between devices, local(): lax.all_gather(jnp.concatenate([wi_gate.T, wi_lin.T, wo], 0), 'z', axis=0)  26.6 us
    ppermute x16, starting transfers between devices, shifted(): return lax.ppermute(value, axis, [((i + step) % 4, i) for i in range(4)])  23.8 us
    all_to_all x1, blocking collectives, local(): pair = lax.all_to_all(pair, 'z', 0, 0, tiled=True)  20.2 us
    all_to_all x3, waiting for transfers between devices, sum_over(): return jnp.sum(lax.all_to_all(copies, axis, 0, 0, tiled=True), 0)  19.5 us
    ppermute x16, waiting for transfers between devices, shifted(): return lax.ppermute(value, axis, [((i + step) % 4, i) for i in range(4)])  15.4 us
    all_to_all x3, starting transfers between devices, sum_over(): return jnp.sum(lax.all_to_all(copies, axis, 0, 0, tiled=True), 0)  14.9 us
  transfers between devices with their start and end apart: 26, of which 18 were waited for; matrix products, arithmetic and copies ran while one was open for 2% of the time, Pallas kernels for 3%

profile of v4, /device:TPU:8, one launch (start us, length us, event | category | flops | bytes accessed | tf_op | source)
XLA Modules:
  0.0 261.5 jit_solution(13018238280092261551)
XLA Ops:
  7.2 2.2 pad_maximum_fusion.2
  9.6 20.2 %all_to_all.31 = bf16[8,2,16,512]{3,2,1,0:T(8,128)(2,1)S(1)} all-to-all(bf16[8,2,16,512]{3,2,1,0:T(8,128)(2,1)S(1)} %pad_maximum_fusion.5), channel_id=1, replica_groups=mesh['z'=8,'x'=4,'y'=4,'c'=2] {'z'}, dimensions={0} | all-to-all | bytes 524288 | tf_op jit(solution)/shard_map/all_to_all | solution.py:213
  29.9 0.5 collective-permute-start.9
  30.4 1.6 collective-permute-start.11
  32.0 2.8 %collective-permute-start = (bf16[8,16,512]{2,1,0:T(8,128)(2,1)S(1)}, bf16[8,16,512]{2,1,0:T(8,128)(2,1)S(1)}, u32[]{:S(2)}, u32[]{:S(2)}) collective-permute-start(bf16[8,16,512]{2,1,0:T(8,128)(2,1)S(1)} %get-tuple-element.40), channel_id=1, source_target_pairs={{8,0},{16,8},{24,16},{0,24},{9,1},{17,9},{25,17},{1,25},{10,2},{18... | collective-permute-start | bytes 393224 | tf_op jit(solution)/shard_map/ppermute | solution.py:27
  34.7 0.3 collective-permute-done.9
  35.0 1.2 collective-permute-start.10
  36.3 0.1 collective-permute-done.11
  36.4 0.9 collective-permute-start.12
  37.3 0.2 collective-permute-done
  37.5 3.5 %collective-permute-start.1 = (bf16[4,16,512]{2,1,0:T(8,128)(2,1)S(1)}, bf16[4,16,512]{2,1,0:T(8,128)(2,1)S(1)}, u32[]{:S(2)}, u32[]{:S(2)}) collective-permute-start(bf16[4,16,512]{2,1,0:T(8,128)(2,1)S(1)} %slice.93), channel_id=1, source_target_pairs={{8,0},{16,8},{24,16},{0,24},{9,1},{17,9},{25,17},{1,25},{10,2},{18... | collective-permute-start | bytes 196616 | tf_op jit(solution)/shard_map/ppermute | solution.py:27
  41.0 0.9 collective-permute-done.12
  42.0 0.1 fusion.8
  42.0 3.2 %collective-permute-start.13 = (bf16[4,8,16,512]{3,2,1,0:T(8,128)(2,1)S(1)}, bf16[4,8,16,512]{3,2,1,0:T(8,128)(2,1)S(1)}, u32[]{:S(2)}, u32[]{:S(2)}) collective-permute-start(bf16[4,8,16,512]{3,2,1,0:T(8,128)(2,1)S(1)} %get-tuple-element.35), channel_id=1, source_target_pairs={{8,0},{16,8},{24,16},{0,24},{9,1},{17,9},{25,17},{1,25},{10,2},{18... | collective-permute-start | bytes 1572872 | tf_op jit(solution)/shard_map/ppermute | solution.py:27
  45.3 1.9 collective-permute-done.3
  47.2 0.1 fusion.9
  47.3 2.1 collective-permute-start.4
  49.4 4.5 %collective-permute-done.13 = bf16[4,8,16,512]{3,2,1,0:T(8,128)(2,1)S(1)} collective-permute-done((bf16[4,8,16,512]{3,2,1,0:T(8,128)(2,1)S(1)}, bf16[4,8,16,512]{3,2,1,0:T(8,128)(2,1)S(1)}, u32[]{:S(2)}, u32[]{:S(2)}) %collective-permute-start.13) | collective-permute-done | bytes 524320 | tf_op jit(solution)/shard_map/ppermute | solution.py:27
  53.9 3.4 %collective-permute-start.14 = (bf16[4,4,16,512]{3,2,1,0:T(8,128)(2,1)S(1)}, bf16[4,4,16,512]{3,2,1,0:T(8,128)(2,1)S(1)}, u32[]{:S(2)}, u32[]{:S(2)}) collective-permute-start(bf16[4,4,16,512]{3,2,1,0:T(8,128)(2,1)S(1)} %slice.100), channel_id=1, source_target_pairs={{8,0},{16,8},{24,16},{0,24},{9,1},{17,9},{25,17},{1,25},{10,2},{18... | collective-permute-start | bytes 786440 | tf_op jit(solution)/shard_map/ppermute | solution.py:27
  57.4 4.3 %collective-permute-start.5 = (bf16[4,4,16,512]{3,2,1,0:T(8,128)(2,1)S(1)}, bf16[4,4,16,512]{3,2,1,0:T(8,128)(2,1)S(1)}, u32[]{:S(2)}, u32[]{:S(2)}) collective-permute-start(bf16[4,4,16,512]{3,2,1,0:T(8,128)(2,1)S(1)} %slice.95), channel_id=1, source_target_pairs={{2,0},{4,2},{6,4},{0,6},{3,1},{5,3},{7,5},{1,7},{10,8},{12,10},{14... | collective-permute-start | bytes 786440 | tf_op jit(solution)/shard_map/ppermute | solution.py:27
  61.9 3.1 %collective-permute-done.16 = bf16[4,4,16,512]{3,2,1,0:T(8,128)(2,1)S(1)} collective-permute-done((bf16[4,4,16,512]{3,2,1,0:T(8,128)(2,1)S(1)}, bf16[4,4,16,512]{3,2,1,0:T(8,128)(2,1)S(1)}, u32[]{:S(2)}, u32[]{:S(2)}) %collective-permute-start.16) | collective-permute-done | bytes 262176 | tf_op jit(solution)/shard_map/ppermute | solution.py:27
  65.0 0.3 pad_maximum_fusion.1.cot0
  65.3 0.1 collective-permute-start.17
  65.4 0.3 collective-permute-done.5
  65.7 4.2 %collective-permute-done.7 = bf16[4,4,16,512]{3,2,1,0:T(8,128)(2,1)S(1)} collective-permute-done((bf16[4,4,16,512]{3,2,1,0:T(8,128)(2,1)S(1)}, bf16[4,4,16,512]{3,2,1,0:T(8,128)(2,1)S(1)}, u32[]{:S(2)}, u32[]{:S(2)}) %collective-permute-start.7) | collective-permute-done | bytes 262176 | tf_op jit(solution)/shard_map/ppermute | solution.py:27
  69.9 0.3 pad_maximum_fusion.tok0
  70.2 0.1 collective-permute-start.8
  70.3 1.3 copy-done.12
  71.6 2.8 %collective-permute-done.8.tok1 = bf16[4,4,8,16,512]{4,3,2,1,0:T(8,128)(2,1)S(1)} collective-permute-done((bf16[4,4,8,16,512]{4,3,2,1,0:T(8,128)(2,1)S(1)}, bf16[4,4,8,16,512]{4,3,2,1,0:T(8,128)(2,1)S(1)}, u32[]{:S(2)}, u32[]{:S(2)}) %collective-permute-start.8) | collective-permute-done | bytes 2097184 | tf_op jit(solution)/shard_map/ppermute | solution.py:31
  74.5 1.4 copy-done
  75.9 26.6 %all-gather.3.cloned.1.call-done = bf16[7680,512]{1,0:T(8,128)(2,1)} async-done(((bf16[960,512]{1,0:T(8,128)(2,1)}), bf16[7680,512]{1,0:T(8,128)(2,1)}) %all-gather.3.cloned.1.call-update) | async-done | bytes 7864336 | tf_op jit(solution)/shard_map/all_gather | solution.py:210
  102.5 1.6 copy-done.1
  104.0 14.5 %shard_map.195 = (bf16[8,960,512]{2,1,0:T(8,128)(2,1)}, bf16[512,640]{1,0:T(8,128)(2,1)S(1)}) custom-call(bf16[4,4,8,16,512]{4,3,2,1,0:T(8,128)(2,1)S(1)} %pad_maximum_fusion.tok0, bf16[4,4,8,16,512]{4,3,2,1,0:T(8,128)(2,1)S(1)} %copy-done.1, bf16[4,4,8,16,512]{4,3,2,1,0:T(8,128)(2,1)} %copy-done.2, bf16[4,4,8,16,512]{4,3,2,1,0:T(8,128)(2,1)} %copy-done.12, ...), custom_call_target="tpu_custom_call" | custom-call | flops 8053063680 | bytes 25000000 | tf_op jit(solution)/shard_map/pallas_call | solution.py:142
  118.8 6.4 %shard_map.196 = bf16[2,16,8,16,512]{4,3,2,1,0:T(8,128)(2,1)S(1)} custom-call(s32[16]{0:T(128)S(1)} %add.105.place, bf16[512,640]{1,0:T(8,128)(2,1)S(1)} %get-tuple-element.17.hidden, bf16[8,960,512]{2,1,0:T(8,128)(2,1)} %bitcast.75), custom_call_target="tpu_custom_call" | custom-call | flops 2684354560 | bytes 10000000 | tf_op jit(solution)/shard_map/pallas_call | solution.py:166
  125.2 0.2 slice_bitcast_fusion
  125.4 0.1 collective-permute-start.18
  125.5 4.1 %collective-permute-done.18 = bf16[16,8,16,512]{3,2,1,0:T(8,128)(2,1)S(1)} collective-permute-done((bf16[16,8,16,512]{3,2,1,0:T(8,128)(2,1)S(1)}, bf16[16,8,16,512]{3,2,1,0:T(8,128)(2,1)S(1)}, u32[]{:S(2)}, u32[]{:S(2)}) %collective-permute-start.18) | collective-permute-done | bytes 2097184 | tf_op jit(solution)/shard_map/ppermute | solution.py:31
  129.7 1.0 fusion
  130.6 34.4 %all_to_all.32 = bf16[16,8,16,512]{3,2,1,0:T(8,128)(2,1)S(1)} all-to-all(bf16[16,8,16,512]{3,2,1,0:T(8,128)(2,1)S(1)} %fusion), channel_id=1, replica_groups=mesh['z'=8,'x'=4,'y'=4,'c'=2] {'x','y'}, dimensions={0} | all-to-all | bytes 4194304 | tf_op jit(solution)/shard_map/all_to_all | solution.py:227
  165.0 1.1 reduce_sum.75
  166.1 3.8 %all-to-all-start.2 = ((bf16[8,16,512]{2,1,0:T(8,128)(2,1)}), bf16[8,16,512]{2,1,0:T(8,128)(2,1)S(1)}, u32[]{:S(2)}, u32[]{:S(2)}) async-start(bf16[8,16,512]{2,1,0:T(8,128)(2,1)} %reduce_sum.75), calls=%async_computation.3 | async-start | bytes 262144 | tf_op jit(solution)/shard_map/all_to_all | solution.py:229
  169.9 10.7 %all-to-all-done.2 = bf16[8,16,512]{2,1,0:T(8,128)(2,1)S(1)} async-done(((bf16[8,16,512]{2,1,0:T(8,128)(2,1)}), bf16[8,16,512]{2,1,0:T(8,128)(2,1)S(1)}, u32[]{:S(2)}, u32[]{:S(2)}) %all-to-all-start.2) | async-done | bytes 131104 | tf_op jit(solution)/shard_map/all_to_all | solution.py:229
  180.7 0.7 copy-done.3
  181.3 1.6 shard_map.197
  182.9 26.8 %reduce-scatter.2.cloned.1.call-done = bf16[1,960,512]{2,1,0:T(8,128)(2,1)} async-done(((bf16[8,960,512]{2,1,0:T(8,128)(2,1)}), bf16[1,960,512]{2,1,0:T(8,128)(2,1)}) %reduce-scatter.2.cloned.1.call-update) | async-done | bytes 983056 | tf_op jit(solution)/shard_map/reduce_scatter | solution.py:219
  209.6 1.6 add_reduce_fusion.1
  211.2 0.6 broadcast_in_dim.6
  211.9 4.4 %all-to-all-start.3 = ((f32[8,1,960]{2,1,0:T(1,128)}), f32[8,1,960]{2,1,0:T(1,128)S(1)}, u32[]{:S(2)}, u32[]{:S(2)}) async-start(f32[8,1,960]{2,1,0:T(1,128)} %broadcast_in_dim.6), calls=%async_computation.4 | async-start | bytes 65536 | tf_op jit(solution)/shard_map/all_to_all | solution.py:45
  216.2 1.5 convert_multiply_fusion
  217.7 6.5 %all-to-all-done.3 = f32[8,1,960]{2,1,0:T(1,128)S(1)} async-done(((f32[8,1,960]{2,1,0:T(1,128)}), f32[8,1,960]{2,1,0:T(1,128)S(1)}, u32[]{:S(2)}, u32[]{:S(2)}) %all-to-all-start.3) | async-done | bytes 30752 | tf_op jit(solution)/shard_map/all_to_all | solution.py:45
  224.4 0.4 add_reduce_fusion
  224.8 0.1 collective-permute-start.19
  224.9 1.2 collective-permute-done.19
  226.1 0.7 broadcast_in_dim.7
  226.8 7.2 %all-to-all-start.4 = ((f32[16,6,512]{2,1,0:T(8,128)}), f32[16,6,512]{2,1,0:T(8,128)S(1)}, u32[]{:S(2)}, u32[]{:S(2)}) async-start(f32[16,6,512]{2,1,0:T(8,128)} %broadcast_in_dim.7), calls=%async_computation.5 | async-start | bytes 524288 | tf_op jit(solution)/shard_map/all_to_all | solution.py:45
  234.7 0.6 slice_reduce_fusion
  235.3 6.1 %all-to-all-done.4 = f32[16,6,512]{2,1,0:T(8,128)S(1)} async-done(((f32[16,6,512]{2,1,0:T(8,128)}), f32[16,6,512]{2,1,0:T(8,128)S(1)}, u32[]{:S(2)}, u32[]{:S(2)}) %all-to-all-start.4) | async-done | bytes 196640 | tf_op jit(solution)/shard_map/all_to_all | solution.py:45
  241.5 0.1 fusion.2
  241.6 0.6 broadcast_in_dim.8
  242.2 3.3 %all-to-all-start.5 = ((f32[8,3,1]{1,2,0:T(1,128)}), f32[8,3,1]{1,2,0:T(1,128)S(1)}, u32[]{:S(2)}, u32[]{:S(2)}) async-start(f32[8,3,1]{1,2,0:T(1,128)} %broadcast_in_dim.8), calls=%async_computation.6 | async-start | bytes 8192 | tf_op jit(solution)/shard_map/all_to_all | solution.py:45
  245.5 0.6 fusion.13
  246.1 6.9 %all-to-all-done.5 = f32[8,3,1]{1,2,0:T(1,128)S(1)} async-done(((f32[8,3,1]{1,2,0:T(1,128)}), f32[8,3,1]{1,2,0:T(1,128)S(1)}, u32[]{:S(2)}, u32[]{:S(2)}) %all-to-all-start.5) | async-done | bytes 128 | tf_op jit(solution)/shard_map/all_to_all | solution.py:45
  253.1 0.2 multiply_multiply_fusion
  253.4 1.3 slice_bitcast_fusion.2
  (71 shorter events, 1.2 us)
Async XLA Ops:
  7.2 2.4 copy-start.5
  7.2 2.4 copy-start.4
  7.2 95.3 %all-gather.3.cloned.1.call-start = ((), (), s32[]{:S(2)}) async-start(), calls=%async_computation.8 | async-start | bytes 8847360 | tf_op jit(solution)/shard_map/all_gather | solution.py:210
  9.5 200.1 %reduce-scatter.2.cloned.1.call-start = ((), (), s32[]{:S(2)}) async-start(), calls=%async_computation.7 | async-start | bytes 8847360 | tf_op jit(solution)/shard_map/reduce_scatter | solution.py:219
  29.9 5.2 %collective-permute-start.9 = (bf16[8,16,512]{2,1,0:T(8,128)(2,1)S(1)}, bf16[8,16,512]{2,1,0:T(8,128)(2,1)S(1)}, u32[]{:S(2)}, u32[]{:S(2)}) collective-permute-start(bf16[8,16,512]{2,1,0:T(8,128)(2,1)S(1)} %get-tuple-element.41), channel_id=1, source_target_pairs={{2,0},{4,2},{6,4},{0,6},{3,1},{5,3},{7,5},{1,7},{10,8},{12,10},{14... | collective-permute-start | bytes 393224 | tf_op jit(solution)/shard_map/ppermute | solution.py:27
  30.4 6.0 %collective-permute-start.11 = (bf16[8,16,512]{2,1,0:T(8,128)(2,1)S(1)}, bf16[8,16,512]{2,1,0:T(8,128)(2,1)S(1)}, u32[]{:S(2)}, u32[]{:S(2)}) collective-permute-start(bf16[8,16,512]{2,1,0:T(8,128)(2,1)S(1)} %get-tuple-element.41), channel_id=1, source_target_pairs={{6,0},{0,2},{2,4},{4,6},{7,1},{1,3},{3,5},{5,7},{14,8},{8,10},{10,... | collective-permute-start | bytes 393224 | tf_op jit(solution)/shard_map/ppermute | solution.py:27
  32.0 5.5 %collective-permute-start = (bf16[8,16,512]{2,1,0:T(8,128)(2,1)S(1)}, bf16[8,16,512]{2,1,0:T(8,128)(2,1)S(1)}, u32[]{:S(2)}, u32[]{:S(2)}) collective-permute-start(bf16[8,16,512]{2,1,0:T(8,128)(2,1)S(1)} %get-tuple-element.40), channel_id=1, source_target_pairs={{8,0},{16,8},{24,16},{0,24},{9,1},{17,9},{25,17},{1,25},{10,2},{18... | collective-permute-start | bytes 393224 | tf_op jit(solution)/shard_map/ppermute | solution.py:27
  34.7 6.2 %collective-permute-start.2 = (bf16[8,16,512]{2,1,0:T(8,128)(2,1)S(1)}, bf16[8,16,512]{2,1,0:T(8,128)(2,1)S(1)}, u32[]{:S(2)}, u32[]{:S(2)}) collective-permute-start(bf16[8,16,512]{2,1,0:T(8,128)(2,1)S(1)} %get-tuple-element.40), channel_id=1, source_target_pairs={{24,0},{0,8},{8,16},{16,24},{25,1},{1,9},{9,17},{17,25},{26,2},{2,... | collective-permute-start | bytes 393224 | tf_op jit(solution)/shard_map/ppermute | solution.py:27
  35.0 6.0 %collective-permute-start.10 = (bf16[4,16,512]{2,1,0:T(8,128)(2,1)S(1)}, bf16[4,16,512]{2,1,0:T(8,128)(2,1)S(1)}, u32[]{:S(2)}, u32[]{:S(2)}) collective-permute-start(bf16[4,16,512]{2,1,0:T(8,128)(2,1)S(1)} %slice.98), channel_id=1, source_target_pairs={{2,0},{4,2},{6,4},{0,6},{3,1},{5,3},{7,5},{1,7},{10,8},{12,10},{14... | collective-permute-start | bytes 196616 | tf_op jit(solution)/shard_map/ppermute | solution.py:27
  36.4 5.6 %collective-permute-start.12 = (bf16[4,16,512]{2,1,0:T(8,128)(2,1)S(1)}, bf16[4,16,512]{2,1,0:T(8,128)(2,1)S(1)}, u32[]{:S(2)}, u32[]{:S(2)}) collective-permute-start(bf16[4,16,512]{2,1,0:T(8,128)(2,1)S(1)} %slice.99), channel_id=1, source_target_pairs={{6,0},{0,2},{2,4},{4,6},{7,1},{1,3},{3,5},{5,7},{14,8},{8,10},{10,... | collective-permute-start | bytes 196616 | tf_op jit(solution)/shard_map/ppermute | solution.py:27
  37.5 7.8 %collective-permute-start.1 = (bf16[4,16,512]{2,1,0:T(8,128)(2,1)S(1)}, bf16[4,16,512]{2,1,0:T(8,128)(2,1)S(1)}, u32[]{:S(2)}, u32[]{:S(2)}) collective-permute-start(bf16[4,16,512]{2,1,0:T(8,128)(2,1)S(1)} %slice.93), channel_id=1, source_target_pairs={{8,0},{16,8},{24,16},{0,24},{9,1},{17,9},{25,17},{1,25},{10,2},{18... | collective-permute-start | bytes 196616 | tf_op jit(solution)/shard_map/ppermute | solution.py:27
  40.9 6.2 %collective-permute-start.3 = (bf16[4,16,512]{2,1,0:T(8,128)(2,1)S(1)}, bf16[4,16,512]{2,1,0:T(8,128)(2,1)S(1)}, u32[]{:S(2)}, u32[]{:S(2)}) collective-permute-start(bf16[4,16,512]{2,1,0:T(8,128)(2,1)S(1)} %slice.94), channel_id=1, source_target_pairs={{24,0},{0,8},{8,16},{16,24},{25,1},{1,9},{9,17},{17,25},{26,2},{2,... | collective-permute-start | bytes 196616 | tf_op jit(solution)/shard_map/ppermute | solution.py:27
  42.0 11.8 %collective-permute-start.13 = (bf16[4,8,16,512]{3,2,1,0:T(8,128)(2,1)S(1)}, bf16[4,8,16,512]{3,2,1,0:T(8,128)(2,1)S(1)}, u32[]{:S(2)}, u32[]{:S(2)}) collective-permute-start(bf16[4,8,16,512]{3,2,1,0:T(8,128)(2,1)S(1)} %get-tuple-element.35), channel_id=1, source_target_pairs={{8,0},{16,8},{24,16},{0,24},{9,1},{17,9},{25,17},{1,25},{10,2},{18... | collective-permute-start | bytes 1572872 | tf_op jit(solution)/shard_map/ppermute | solution.py:27
  45.3 12.0 %collective-permute-start.15 = (bf16[4,8,16,512]{3,2,1,0:T(8,128)(2,1)S(1)}, bf16[4,8,16,512]{3,2,1,0:T(8,128)(2,1)S(1)}, u32[]{:S(2)}, u32[]{:S(2)}) collective-permute-start(bf16[4,8,16,512]{3,2,1,0:T(8,128)(2,1)S(1)} %get-tuple-element.35), channel_id=1, source_target_pairs={{24,0},{0,8},{8,16},{16,24},{25,1},{1,9},{9,17},{17,25},{26,2},{2,... | collective-permute-start | bytes 1572872 | tf_op jit(solution)/shard_map/ppermute | solution.py:27
  47.3 10.1 %collective-permute-start.4 = (bf16[4,8,16,512]{3,2,1,0:T(8,128)(2,1)S(1)}, bf16[4,8,16,512]{3,2,1,0:T(8,128)(2,1)S(1)}, u32[]{:S(2)}, u32[]{:S(2)}) collective-permute-start(bf16[4,8,16,512]{3,2,1,0:T(8,128)(2,1)S(1)} %get-tuple-element.37), channel_id=1, source_target_pairs={{2,0},{4,2},{6,4},{0,6},{3,1},{5,3},{7,5},{1,7},{10,8},{12,10},{14... | collective-permute-start | bytes 1572872 | tf_op jit(solution)/shard_map/ppermute | solution.py:27
  49.3 12.4 %collective-permute-start.6 = (bf16[4,8,16,512]{3,2,1,0:T(8,128)(2,1)S(1)}, bf16[4,8,16,512]{3,2,1,0:T(8,128)(2,1)S(1)}, u32[]{:S(2)}, u32[]{:S(2)}) collective-permute-start(bf16[4,8,16,512]{3,2,1,0:T(8,128)(2,1)S(1)} %get-tuple-element.37), channel_id=1, source_target_pairs={{6,0},{0,2},{2,4},{4,6},{7,1},{1,3},{3,5},{5,7},{14,8},{8,10},{10,... | collective-permute-start | bytes 1572872 | tf_op jit(solution)/shard_map/ppermute | solution.py:27
  53.9 8.0 %collective-permute-start.14 = (bf16[4,4,16,512]{3,2,1,0:T(8,128)(2,1)S(1)}, bf16[4,4,16,512]{3,2,1,0:T(8,128)(2,1)S(1)}, u32[]{:S(2)}, u32[]{:S(2)}) collective-permute-start(bf16[4,4,16,512]{3,2,1,0:T(8,128)(2,1)S(1)} %slice.100), channel_id=1, source_target_pairs={{8,0},{16,8},{24,16},{0,24},{9,1},{17,9},{25,17},{1,25},{10,2},{18... | collective-permute-start | bytes 786440 | tf_op jit(solution)/shard_map/ppermute | solution.py:27
  57.3 7.7 %collective-permute-start.16 = (bf16[4,4,16,512]{3,2,1,0:T(8,128)(2,1)S(1)}, bf16[4,4,16,512]{3,2,1,0:T(8,128)(2,1)S(1)}, u32[]{:S(2)}, u32[]{:S(2)}) collective-permute-start(bf16[4,4,16,512]{3,2,1,0:T(8,128)(2,1)S(1)} %slice.101), channel_id=1, source_target_pairs={{24,0},{0,8},{8,16},{16,24},{25,1},{1,9},{9,17},{17,25},{26,2},{2,... | collective-permute-start | bytes 786440 | tf_op jit(solution)/shard_map/ppermute | solution.py:27
  57.4 8.3 %collective-permute-start.5 = (bf16[4,4,16,512]{3,2,1,0:T(8,128)(2,1)S(1)}, bf16[4,4,16,512]{3,2,1,0:T(8,128)(2,1)S(1)}, u32[]{:S(2)}, u32[]{:S(2)}) collective-permute-start(bf16[4,4,16,512]{3,2,1,0:T(8,128)(2,1)S(1)} %slice.95), channel_id=1, source_target_pairs={{2,0},{4,2},{6,4},{0,6},{3,1},{5,3},{7,5},{1,7},{10,8},{12,10},{14... | collective-permute-start | bytes 786440 | tf_op jit(solution)/shard_map/ppermute | solution.py:27
  61.8 8.1 %collective-permute-start.7 = (bf16[4,4,16,512]{3,2,1,0:T(8,128)(2,1)S(1)}, bf16[4,4,16,512]{3,2,1,0:T(8,128)(2,1)S(1)}, u32[]{:S(2)}, u32[]{:S(2)}) collective-permute-start(bf16[4,4,16,512]{3,2,1,0:T(8,128)(2,1)S(1)} %slice.96), channel_id=1, source_target_pairs={{6,0},{0,2},{2,4},{4,6},{7,1},{1,3},{3,5},{5,7},{14,8},{8,10},{10,... | collective-permute-start | bytes 786440 | tf_op jit(solution)/shard_map/ppermute | solution.py:27
  65.3 5.0 %copy-start.2 = (bf16[4,4,8,16,512]{4,3,2,1,0:T(8,128)(2,1)}, bf16[4,4,8,16,512]{4,3,2,1,0:T(8,128)(2,1)S(1)}, u32[]{:S(2)}) copy-start(bf16[4,4,8,16,512]{4,3,2,1,0:T(8,128)(2,1)S(1)} %pad_maximum_fusion.1.cot0) | copy-start | bytes 6291460
  65.3 5.1 %collective-permute-start.17 = (bf16[4,4,8,16,512]{4,3,2,1,0:T(8,128)(2,1)S(1)}, bf16[4,4,8,16,512]{4,3,2,1,0:T(8,128)(2,1)S(1)}, u32[]{:S(2)}, u32[]{:S(2)}) collective-permute-start(bf16[4,4,8,16,512]{4,3,2,1,0:T(8,128)(2,1)S(1)} %pad_maximum_fusion.1.cot0), channel_id=1, source_target_pairs={{0,1},{1,0},{2,3},{3,2},{4,5},{5,4},{6,7},{7,6},{8,9},{9,8},{10,11... | collective-permute-start | bytes 6291464 | tf_op jit(solution)/shard_map/ppermute | solution.py:31
  70.2 4.2 %collective-permute-start.8 = (bf16[4,4,8,16,512]{4,3,2,1,0:T(8,128)(2,1)S(1)}, bf16[4,4,8,16,512]{4,3,2,1,0:T(8,128)(2,1)S(1)}, u32[]{:S(2)}, u32[]{:S(2)}) collective-permute-start(bf16[4,4,8,16,512]{4,3,2,1,0:T(8,128)(2,1)S(1)} %pad_maximum_fusion.tok0), channel_id=1, source_target_pairs={{0,1},{1,0},{2,3},{3,2},{4,5},{5,4},{6,7},{7,6},{8,9},{9,8},{10,11... | collective-permute-start | bytes 6291464 | tf_op jit(solution)/shard_map/ppermute | solution.py:31
  70.3 1.3 copy-start.12
  74.5 1.4 copy-start
  102.5 1.6 copy-start.1
  125.4 4.2 %collective-permute-start.18 = (bf16[16,8,16,512]{3,2,1,0:T(8,128)(2,1)S(1)}, bf16[16,8,16,512]{3,2,1,0:T(8,128)(2,1)S(1)}, u32[]{:S(2)}, u32[]{:S(2)}) collective-permute-start(bf16[16,8,16,512]{3,2,1,0:T(8,128)(2,1)S(1)} %slice_bitcast_fusion), channel_id=1, source_target_pairs={{0,1},{1,0},{2,3},{3,2},{4,5},{5,4},{6,7},{7,6},{8,9},{9,8},{10,11... | collective-permute-start | bytes 6291464 | tf_op jit(solution)/shard_map/ppermute | solution.py:31
  165.0 4.9 %copy-start.6 = (f32[320]{0:T(512)S(1)}, f32[320]{0:T(512)}, u32[]{:S(2)}) copy-start(f32[320]{0:T(512)} %param.18) | copy-start | bytes 3844
  165.0 4.9 %copy-start.7 = (f32[320]{0:T(512)S(1)}, f32[320]{0:T(512)}, u32[]{:S(2)}) copy-start(f32[320]{0:T(512)} %param.20) | copy-start | bytes 3844
  165.0 4.9 %copy-start.8 = (f32[320]{0:T(512)S(1)}, f32[320]{0:T(512)}, u32[]{:S(2)}) copy-start(f32[320]{0:T(512)} %param.21) | copy-start | bytes 3844
  166.1 14.6 %all-to-all-start.2 = ((bf16[8,16,512]{2,1,0:T(8,128)(2,1)}), bf16[8,16,512]{2,1,0:T(8,128)(2,1)S(1)}, u32[]{:S(2)}, u32[]{:S(2)}) async-start(bf16[8,16,512]{2,1,0:T(8,128)(2,1)} %reduce_sum.75), calls=%async_computation.3 | async-start | bytes 262144 | tf_op jit(solution)/shard_map/all_to_all | solution.py:229
  180.7 0.7 copy-start.3
  211.9 12.4 %all-to-all-start.3 = ((f32[8,1,960]{2,1,0:T(1,128)}), f32[8,1,960]{2,1,0:T(1,128)S(1)}, u32[]{:S(2)}, u32[]{:S(2)}) async-start(f32[8,1,960]{2,1,0:T(1,128)} %broadcast_in_dim.6), calls=%async_computation.4 | async-start | bytes 65536 | tf_op jit(solution)/shard_map/all_to_all | solution.py:45
  217.7 23.7 %copy-start.9 = (f32[512]{0:T(512)S(1)}, f32[512]{0:T(512)}, u32[]{:S(2)}) copy-start(f32[512]{0:T(512)} %param.22) | copy-start | bytes 6148
  217.7 23.7 %copy-start.10 = (f32[512]{0:T(512)S(1)}, f32[512]{0:T(512)}, u32[]{:S(2)}) copy-start(f32[512]{0:T(512)} %param.19) | copy-start | bytes 6148
  217.7 23.7 %copy-start.11 = (f32[512]{0:T(512)S(1)}, f32[512]{0:T(512)}, u32[]{:S(2)}) copy-start(f32[512]{0:T(512)} %param.17) | copy-start | bytes 6148
  224.8 1.3 collective-permute-start.19
  226.8 14.6 %all-to-all-start.4 = ((f32[16,6,512]{2,1,0:T(8,128)}), f32[16,6,512]{2,1,0:T(8,128)S(1)}, u32[]{:S(2)}, u32[]{:S(2)}) async-start(f32[16,6,512]{2,1,0:T(8,128)} %broadcast_in_dim.7), calls=%async_computation.5 | async-start | bytes 524288 | tf_op jit(solution)/shard_map/all_to_all | solution.py:45
  242.2 10.8 %all-to-all-start.5 = ((f32[8,3,1]{1,2,0:T(1,128)}), f32[8,3,1]{1,2,0:T(1,128)S(1)}, u32[]{:S(2)}, u32[]{:S(2)}) async-start(f32[8,3,1]{1,2,0:T(1,128)} %broadcast_in_dim.8), calls=%async_computation.6 | async-start | bytes 8192 | tf_op jit(solution)/shard_map/all_to_all | solution.py:45
Sparse Core Ops, SparseCore 0:
  9.8 92.5 all-gather.2
  118.7 90.8 reduce-scatter.1

commit v5 on v4

--- a/solution.py
+++ b/solution.py
@@ -96,7 +96,8 @@
         acc[2 * FB :] += second
         return carry
 
-    lax.fori_loop(0, NZ // 2, forward, 0)
+    for pair in range(NZ // 2):
+        forward(pair, 0)
     pre_gate = acc[:FB]
     pre_lin = acc[FB : 2 * FB]
     grad_act = acc[2 * FB :]
@@ -117,7 +118,8 @@
         store(k).start()
         return carry
 
-    lax.fori_loop(0, NZ, backward, 0)
+    for k in range(NZ):
+        backward(k, 0)
     hidden[...] = hidden_t[: 2 * FB].T
 
     def finish(k, carry):
@@ -155,7 +157,7 @@
             jax.ShapeDtypeStruct((NZ, 3 * FB, DB), jnp.bfloat16),
             jax.ShapeDtypeStruct((TOK, 2 * FB), jnp.bfloat16),
         ],
-        compiler_params=pltpu.CompilerParams(vmem_limit_bytes=VMEM),
+        compiler_params=pltpu.CompilerParams(vmem_limit_bytes=60 * 1024 * 1024),
         cost_estimate=pl.CostEstimate(
             flops=4 * 3 * FB * TOK * D, bytes_accessed=25000000, transcendentals=FB * TOK
         ),

time: 262 us -> 260 us (level)
  no operation moved by 1% of the time
where the time goes in v5:
time: 260 us; the launch traced here: 259 us
  waiting for transfers between devices  106 us (41%)
  blocking collectives  54.6 us (21%)
  starting transfers between devices  43 us (17%)
  Pallas kernels  21.7 us (8%)
  between operations  15.2 us (6%)
  other arithmetic  9.24 us (4%)
  local copies, waits for them, and re-layouts  9.09 us (3%)
    all_to_all x1, blocking collectives, local(): part = lax.all_to_all(part, ('x', 'y'), 0, 0, tiled=True)  34.4 us
    all_gather x1, waiting for transfers between devices, local(): lax.all_gather(jnp.concatenate([wi_gate.T, wi_lin.T, wo], 0), 'z', axis=0)  27.8 us
    reduce_scatter x1, waiting for transfers between devices, local(): grad_w = lax.psum_scatter(grad_w, 'z', scatter_dimension=0)  25.9 us
    ppermute x16, starting transfers between devices, shifted(): return lax.ppermute(value, axis, [((i + step) % 4, i) for i in range(4)])  23.8 us
    all_to_all x1, blocking collectives, local(): pair = lax.all_to_all(pair, 'z', 0, 0, tiled=True)  20.2 us
    all_to_all x3, waiting for transfers between devices, sum_over(): return jnp.sum(lax.all_to_all(copies, axis, 0, 0, tiled=True), 0)  19.5 us
    ppermute x16, waiting for transfers between devices, shifted(): return lax.ppermute(value, axis, [((i + step) % 4, i) for i in range(4)])  15.4 us
    all_to_all x3, starting transfers between devices, sum_over(): return jnp.sum(lax.all_to_all(copies, axis, 0, 0, tiled=True), 0)  14.9 us
  transfers between devices with their start and end apart: 26, of which 18 were waited for; matrix products, arithmetic and copies ran while one was open for 2% of the time, Pallas kernels for 3%

profile of v5, /device:TPU:8, one launch (start us, length us, event | category | flops | bytes accessed | tf_op | source)
XLA Modules:
  0.0 259.1 jit_solution(3604059555314376920)
XLA Ops:
  7.2 2.3 pad_maximum_fusion.2
  9.7 20.2 %all_to_all.31 = bf16[8,2,16,512]{3,2,1,0:T(8,128)(2,1)S(1)} all-to-all(bf16[8,2,16,512]{3,2,1,0:T(8,128)(2,1)S(1)} %pad_maximum_fusion.5), channel_id=1, replica_groups=mesh['z'=8,'x'=4,'y'=4,'c'=2] {'z'}, dimensions={0} | all-to-all | bytes 524288 | tf_op jit(solution)/shard_map/all_to_all | solution.py:215
  29.9 0.5 collective-permute-start.9
  30.4 1.6 collective-permute-start.11
  32.0 2.8 %collective-permute-start = (bf16[8,16,512]{2,1,0:T(8,128)(2,1)S(1)}, bf16[8,16,512]{2,1,0:T(8,128)(2,1)S(1)}, u32[]{:S(2)}, u32[]{:S(2)}) collective-permute-start(bf16[8,16,512]{2,1,0:T(8,128)(2,1)S(1)} %get-tuple-element.40), channel_id=1, source_target_pairs={{8,0},{16,8},{24,16},{0,24},{9,1},{17,9},{25,17},{1,25},{10,2},{18... | collective-permute-start | bytes 393224 | tf_op jit(solution)/shard_map/ppermute | solution.py:27
  34.8 0.3 collective-permute-done.9
  35.1 1.2 collective-permute-start.10
  36.3 0.1 collective-permute-done.11
  36.4 0.9 collective-permute-start.12
  37.3 0.2 collective-permute-done
  37.5 3.5 %collective-permute-start.1 = (bf16[4,16,512]{2,1,0:T(8,128)(2,1)S(1)}, bf16[4,16,512]{2,1,0:T(8,128)(2,1)S(1)}, u32[]{:S(2)}, u32[]{:S(2)}) collective-permute-start(bf16[4,16,512]{2,1,0:T(8,128)(2,1)S(1)} %slice.93), channel_id=1, source_target_pairs={{8,0},{16,8},{24,16},{0,24},{9,1},{17,9},{25,17},{1,25},{10,2},{18... | collective-permute-start | bytes 196616 | tf_op jit(solution)/shard_map/ppermute | solution.py:27
  41.1 0.9 collective-permute-done.12
  42.0 0.1 fusion.8
  42.1 3.2 %collective-permute-start.13 = (bf16[4,8,16,512]{3,2,1,0:T(8,128)(2,1)S(1)}, bf16[4,8,16,512]{3,2,1,0:T(8,128)(2,1)S(1)}, u32[]{:S(2)}, u32[]{:S(2)}) collective-permute-start(bf16[4,8,16,512]{3,2,1,0:T(8,128)(2,1)S(1)} %get-tuple-element.35), channel_id=1, source_target_pairs={{8,0},{16,8},{24,16},{0,24},{9,1},{17,9},{25,17},{1,25},{10,2},{18... | collective-permute-start | bytes 1572872 | tf_op jit(solution)/shard_map/ppermute | solution.py:27
  45.3 1.9 collective-permute-done.3
  47.2 0.1 fusion.9
  47.3 2.1 collective-permute-start.4
  49.4 4.5 %collective-permute-done.13 = bf16[4,8,16,512]{3,2,1,0:T(8,128)(2,1)S(1)} collective-permute-done((bf16[4,8,16,512]{3,2,1,0:T(8,128)(2,1)S(1)}, bf16[4,8,16,512]{3,2,1,0:T(8,128)(2,1)S(1)}, u32[]{:S(2)}, u32[]{:S(2)}) %collective-permute-start.13) | collective-permute-done | bytes 524320 | tf_op jit(solution)/shard_map/ppermute | solution.py:27
  53.9 3.4 %collective-permute-start.14 = (bf16[4,4,16,512]{3,2,1,0:T(8,128)(2,1)S(1)}, bf16[4,4,16,512]{3,2,1,0:T(8,128)(2,1)S(1)}, u32[]{:S(2)}, u32[]{:S(2)}) collective-permute-start(bf16[4,4,16,512]{3,2,1,0:T(8,128)(2,1)S(1)} %slice.100), channel_id=1, source_target_pairs={{8,0},{16,8},{24,16},{0,24},{9,1},{17,9},{25,17},{1,25},{10,2},{18... | collective-permute-start | bytes 786440 | tf_op jit(solution)/shard_map/ppermute | solution.py:27
  57.5 4.3 %collective-permute-start.5 = (bf16[4,4,16,512]{3,2,1,0:T(8,128)(2,1)S(1)}, bf16[4,4,16,512]{3,2,1,0:T(8,128)(2,1)S(1)}, u32[]{:S(2)}, u32[]{:S(2)}) collective-permute-start(bf16[4,4,16,512]{3,2,1,0:T(8,128)(2,1)S(1)} %slice.95), channel_id=1, source_target_pairs={{2,0},{4,2},{6,4},{0,6},{3,1},{5,3},{7,5},{1,7},{10,8},{12,10},{14... | collective-permute-start | bytes 786440 | tf_op jit(solution)/shard_map/ppermute | solution.py:27
  61.9 3.1 %collective-permute-done.16 = bf16[4,4,16,512]{3,2,1,0:T(8,128)(2,1)S(1)} collective-permute-done((bf16[4,4,16,512]{3,2,1,0:T(8,128)(2,1)S(1)}, bf16[4,4,16,512]{3,2,1,0:T(8,128)(2,1)S(1)}, u32[]{:S(2)}, u32[]{:S(2)}) %collective-permute-start.16) | collective-permute-done | bytes 262176 | tf_op jit(solution)/shard_map/ppermute | solution.py:27
  65.0 0.3 pad_maximum_fusion.1.cot0
  65.3 0.1 collective-permute-start.17
  65.4 0.3 collective-permute-done.5
  65.7 4.2 %collective-permute-done.7 = bf16[4,4,16,512]{3,2,1,0:T(8,128)(2,1)S(1)} collective-permute-done((bf16[4,4,16,512]{3,2,1,0:T(8,128)(2,1)S(1)}, bf16[4,4,16,512]{3,2,1,0:T(8,128)(2,1)S(1)}, u32[]{:S(2)}, u32[]{:S(2)}) %collective-permute-start.7) | collective-permute-done | bytes 262176 | tf_op jit(solution)/shard_map/ppermute | solution.py:27
  70.0 0.3 pad_maximum_fusion.tok0
  70.3 0.1 collective-permute-start.8
  70.4 1.2 copy-done.2
  71.6 1.3 copy-done.12
  72.9 1.7 collective-permute-done.8.tok1
  74.7 27.8 %all-gather.3.cloned.1.call-done = bf16[7680,512]{1,0:T(8,128)(2,1)} async-done(((bf16[960,512]{1,0:T(8,128)(2,1)}), bf16[7680,512]{1,0:T(8,128)(2,1)}) %all-gather.3.cloned.1.call-update) | async-done | bytes 7864336 | tf_op jit(solution)/shard_map/all_gather | solution.py:212
  102.5 13.7 %shard_map.195 = (bf16[8,960,512]{2,1,0:T(8,128)(2,1)}, bf16[512,640]{1,0:T(8,128)(2,1)}) custom-call(bf16[4,4,8,16,512]{4,3,2,1,0:T(8,128)(2,1)} %copy-done.2, bf16[4,4,8,16,512]{4,3,2,1,0:T(8,128)(2,1)} %collective-permute-done.8.tok1, bf16[4,4,8,16,512]{4,3,2,1,0:T(8,128)(2,1)} %copy-done.1, bf16[4,4,8,16,512]{4,3,2,1,0:T(8,128)(2,1)} %copy-done.12, ...), custom_call_target="tpu_custom_call" | custom-call | flops 8053063680 | bytes 25000000 | tf_op jit(solution)/shard_map/pallas_call | solution.py:144
  116.4 0.9 copy-done
  117.3 6.4 %shard_map.196 = bf16[2,16,8,16,512]{4,3,2,1,0:T(8,128)(2,1)S(1)} custom-call(s32[16]{0:T(128)S(1)} %add.105.place, bf16[512,640]{1,0:T(8,128)(2,1)S(1)} %copy-done, bf16[8,960,512]{2,1,0:T(8,128)(2,1)} %bitcast.75), custom_call_target="tpu_custom_call" | custom-call | flops 2684354560 | bytes 10000000 | tf_op jit(solution)/shard_map/pallas_call | solution.py:168
  123.7 0.2 slice_bitcast_fusion
  123.9 0.1 collective-permute-start.18
  124.0 4.1 %collective-permute-done.18 = bf16[16,8,16,512]{3,2,1,0:T(8,128)(2,1)S(1)} collective-permute-done((bf16[16,8,16,512]{3,2,1,0:T(8,128)(2,1)S(1)}, bf16[16,8,16,512]{3,2,1,0:T(8,128)(2,1)S(1)}, u32[]{:S(2)}, u32[]{:S(2)}) %collective-permute-start.18) | collective-permute-done | bytes 2097184 | tf_op jit(solution)/shard_map/ppermute | solution.py:31
  128.2 1.0 fusion
  129.1 34.4 %all_to_all.32 = bf16[16,8,16,512]{3,2,1,0:T(8,128)(2,1)S(1)} all-to-all(bf16[16,8,16,512]{3,2,1,0:T(8,128)(2,1)S(1)} %fusion), channel_id=1, replica_groups=mesh['z'=8,'x'=4,'y'=4,'c'=2] {'x','y'}, dimensions={0} | all-to-all | bytes 4194304 | tf_op jit(solution)/shard_map/all_to_all | solution.py:229
  163.5 1.1 reduce_sum.75
  164.6 3.8 %all-to-all-start.2 = ((bf16[8,16,512]{2,1,0:T(8,128)(2,1)}), bf16[8,16,512]{2,1,0:T(8,128)(2,1)S(1)}, u32[]{:S(2)}, u32[]{:S(2)}) async-start(bf16[8,16,512]{2,1,0:T(8,128)(2,1)} %reduce_sum.75), calls=%async_computation.3 | async-start | bytes 262144 | tf_op jit(solution)/shard_map/all_to_all | solution.py:231
  168.4 10.7 %all-to-all-done.2 = bf16[8,16,512]{2,1,0:T(8,128)(2,1)S(1)} async-done(((bf16[8,16,512]{2,1,0:T(8,128)(2,1)}), bf16[8,16,512]{2,1,0:T(8,128)(2,1)S(1)}, u32[]{:S(2)}, u32[]{:S(2)}) %all-to-all-start.2) | async-done | bytes 131104 | tf_op jit(solution)/shard_map/all_to_all | solution.py:231
  179.1 0.7 copy-done.3
  179.8 1.6 shard_map.197
  181.4 25.9 %reduce-scatter.2.cloned.1.call-done = bf16[1,960,512]{2,1,0:T(8,128)(2,1)} async-done(((bf16[8,960,512]{2,1,0:T(8,128)(2,1)}), bf16[1,960,512]{2,1,0:T(8,128)(2,1)}) %reduce-scatter.2.cloned.1.call-update) | async-done | bytes 983056 | tf_op jit(solution)/shard_map/reduce_scatter | solution.py:221
  207.2 1.6 add_reduce_fusion.1
  208.8 0.6 broadcast_in_dim.6
  209.5 4.4 %all-to-all-start.3 = ((f32[8,1,960]{2,1,0:T(1,128)}), f32[8,1,960]{2,1,0:T(1,128)S(1)}, u32[]{:S(2)}, u32[]{:S(2)}) async-start(f32[8,1,960]{2,1,0:T(1,128)} %broadcast_in_dim.6), calls=%async_computation.4 | async-start | bytes 65536 | tf_op jit(solution)/shard_map/all_to_all | solution.py:45
  213.9 1.5 convert_multiply_fusion
  215.4 6.5 %all-to-all-done.3 = f32[8,1,960]{2,1,0:T(1,128)S(1)} async-done(((f32[8,1,960]{2,1,0:T(1,128)}), f32[8,1,960]{2,1,0:T(1,128)S(1)}, u32[]{:S(2)}, u32[]{:S(2)}) %all-to-all-start.3) | async-done | bytes 30752 | tf_op jit(solution)/shard_map/all_to_all | solution.py:45
  222.0 0.4 add_reduce_fusion
  222.4 0.1 collective-permute-start.19
  222.5 1.2 collective-permute-done.19
  223.7 0.7 broadcast_in_dim.7
  224.4 7.2 %all-to-all-start.4 = ((f32[16,6,512]{2,1,0:T(8,128)}), f32[16,6,512]{2,1,0:T(8,128)S(1)}, u32[]{:S(2)}, u32[]{:S(2)}) async-start(f32[16,6,512]{2,1,0:T(8,128)} %broadcast_in_dim.7), calls=%async_computation.5 | async-start | bytes 524288 | tf_op jit(solution)/shard_map/all_to_all | solution.py:45
  232.3 0.6 slice_reduce_fusion
  232.9 6.1 %all-to-all-done.4 = f32[16,6,512]{2,1,0:T(8,128)S(1)} async-done(((f32[16,6,512]{2,1,0:T(8,128)}), f32[16,6,512]{2,1,0:T(8,128)S(1)}, u32[]{:S(2)}, u32[]{:S(2)}) %all-to-all-start.4) | async-done | bytes 196640 | tf_op jit(solution)/shard_map/all_to_all | solution.py:45
  239.1 0.1 fusion.2
  239.2 0.6 broadcast_in_dim.8
  239.8 3.3 %all-to-all-start.5 = ((f32[8,3,1]{1,2,0:T(1,128)}), f32[8,3,1]{1,2,0:T(1,128)S(1)}, u32[]{:S(2)}, u32[]{:S(2)}) async-start(f32[8,3,1]{1,2,0:T(1,128)} %broadcast_in_dim.8), calls=%async_computation.6 | async-start | bytes 8192 | tf_op jit(solution)/shard_map/all_to_all | solution.py:45
  243.1 0.6 fusion.13
  243.7 6.9 %all-to-all-done.5 = f32[8,3,1]{1,2,0:T(1,128)S(1)} async-done(((f32[8,3,1]{1,2,0:T(1,128)}), f32[8,3,1]{1,2,0:T(1,128)S(1)}, u32[]{:S(2)}, u32[]{:S(2)}) %all-to-all-start.5) | async-done | bytes 128 | tf_op jit(solution)/shard_map/all_to_all | solution.py:45
  250.7 0.2 multiply_multiply_fusion
  251.0 1.3 slice_bitcast_fusion.2
  (71 shorter events, 1.2 us)
Async XLA Ops:
  7.2 2.4 copy-start.5
  7.2 2.4 copy-start.4
  7.2 95.3 %all-gather.3.cloned.1.call-start = ((), (), s32[]{:S(2)}) async-start(), calls=%async_computation.8 | async-start | bytes 8847360 | tf_op jit(solution)/shard_map/all_gather | solution.py:212
  9.6 197.7 %reduce-scatter.2.cloned.1.call-start = ((), (), s32[]{:S(2)}) async-start(), calls=%async_computation.7 | async-start | bytes 8847360 | tf_op jit(solution)/shard_map/reduce_scatter | solution.py:221
  29.9 5.2 %collective-permute-start.9 = (bf16[8,16,512]{2,1,0:T(8,128)(2,1)S(1)}, bf16[8,16,512]{2,1,0:T(8,128)(2,1)S(1)}, u32[]{:S(2)}, u32[]{:S(2)}) collective-permute-start(bf16[8,16,512]{2,1,0:T(8,128)(2,1)S(1)} %get-tuple-element.41), channel_id=1, source_target_pairs={{2,0},{4,2},{6,4},{0,6},{3,1},{5,3},{7,5},{1,7},{10,8},{12,10},{14... | collective-permute-start | bytes 393224 | tf_op jit(solution)/shard_map/ppermute | solution.py:27
  30.4 6.0 %collective-permute-start.11 = (bf16[8,16,512]{2,1,0:T(8,128)(2,1)S(1)}, bf16[8,16,512]{2,1,0:T(8,128)(2,1)S(1)}, u32[]{:S(2)}, u32[]{:S(2)}) collective-permute-start(bf16[8,16,512]{2,1,0:T(8,128)(2,1)S(1)} %get-tuple-element.41), channel_id=1, source_target_pairs={{6,0},{0,2},{2,4},{4,6},{7,1},{1,3},{3,5},{5,7},{14,8},{8,10},{10,... | collective-permute-start | bytes 393224 | tf_op jit(solution)/shard_map/ppermute | solution.py:27
  32.0 5.5 %collective-permute-start = (bf16[8,16,512]{2,1,0:T(8,128)(2,1)S(1)}, bf16[8,16,512]{2,1,0:T(8,128)(2,1)S(1)}, u32[]{:S(2)}, u32[]{:S(2)}) collective-permute-start(bf16[8,16,512]{2,1,0:T(8,128)(2,1)S(1)} %get-tuple-element.40), channel_id=1, source_target_pairs={{8,0},{16,8},{24,16},{0,24},{9,1},{17,9},{25,17},{1,25},{10,2},{18... | collective-permute-start | bytes 393224 | tf_op jit(solution)/shard_map/ppermute | solution.py:27
  34.8 6.2 %collective-permute-start.2 = (bf16[8,16,512]{2,1,0:T(8,128)(2,1)S(1)}, bf16[8,16,512]{2,1,0:T(8,128)(2,1)S(1)}, u32[]{:S(2)}, u32[]{:S(2)}) collective-permute-start(bf16[8,16,512]{2,1,0:T(8,128)(2,1)S(1)} %get-tuple-element.40), channel_id=1, source_target_pairs={{24,0},{0,8},{8,16},{16,24},{25,1},{1,9},{9,17},{17,25},{26,2},{2,... | collective-permute-start | bytes 393224 | tf_op jit(solution)/shard_map/ppermute | solution.py:27
  35.1 6.0 %collective-permute-start.10 = (bf16[4,16,512]{2,1,0:T(8,128)(2,1)S(1)}, bf16[4,16,512]{2,1,0:T(8,128)(2,1)S(1)}, u32[]{:S(2)}, u32[]{:S(2)}) collective-permute-start(bf16[4,16,512]{2,1,0:T(8,128)(2,1)S(1)} %slice.98), channel_id=1, source_target_pairs={{2,0},{4,2},{6,4},{0,6},{3,1},{5,3},{7,5},{1,7},{10,8},{12,10},{14... | collective-permute-start | bytes 196616 | tf_op jit(solution)/shard_map/ppermute | solution.py:27
  36.4 5.6 %collective-permute-start.12 = (bf16[4,16,512]{2,1,0:T(8,128)(2,1)S(1)}, bf16[4,16,512]{2,1,0:T(8,128)(2,1)S(1)}, u32[]{:S(2)}, u32[]{:S(2)}) collective-permute-start(bf16[4,16,512]{2,1,0:T(8,128)(2,1)S(1)} %slice.99), channel_id=1, source_target_pairs={{6,0},{0,2},{2,4},{4,6},{7,1},{1,3},{3,5},{5,7},{14,8},{8,10},{10,... | collective-permute-start | bytes 196616 | tf_op jit(solution)/shard_map/ppermute | solution.py:27
  37.5 7.8 %collective-permute-start.1 = (bf16[4,16,512]{2,1,0:T(8,128)(2,1)S(1)}, bf16[4,16,512]{2,1,0:T(8,128)(2,1)S(1)}, u32[]{:S(2)}, u32[]{:S(2)}) collective-permute-start(bf16[4,16,512]{2,1,0:T(8,128)(2,1)S(1)} %slice.93), channel_id=1, source_target_pairs={{8,0},{16,8},{24,16},{0,24},{9,1},{17,9},{25,17},{1,25},{10,2},{18... | collective-permute-start | bytes 196616 | tf_op jit(solution)/shard_map/ppermute | solution.py:27
  41.0 6.2 %collective-permute-start.3 = (bf16[4,16,512]{2,1,0:T(8,128)(2,1)S(1)}, bf16[4,16,512]{2,1,0:T(8,128)(2,1)S(1)}, u32[]{:S(2)}, u32[]{:S(2)}) collective-permute-start(bf16[4,16,512]{2,1,0:T(8,128)(2,1)S(1)} %slice.94), channel_id=1, source_target_pairs={{24,0},{0,8},{8,16},{16,24},{25,1},{1,9},{9,17},{17,25},{26,2},{2,... | collective-permute-start | bytes 196616 | tf_op jit(solution)/shard_map/ppermute | solution.py:27
  42.1 11.8 %collective-permute-start.13 = (bf16[4,8,16,512]{3,2,1,0:T(8,128)(2,1)S(1)}, bf16[4,8,16,512]{3,2,1,0:T(8,128)(2,1)S(1)}, u32[]{:S(2)}, u32[]{:S(2)}) collective-permute-start(bf16[4,8,16,512]{3,2,1,0:T(8,128)(2,1)S(1)} %get-tuple-element.35), channel_id=1, source_target_pairs={{8,0},{16,8},{24,16},{0,24},{9,1},{17,9},{25,17},{1,25},{10,2},{18... | collective-permute-start | bytes 1572872 | tf_op jit(solution)/shard_map/ppermute | solution.py:27
  45.3 12.0 %collective-permute-start.15 = (bf16[4,8,16,512]{3,2,1,0:T(8,128)(2,1)S(1)}, bf16[4,8,16,512]{3,2,1,0:T(8,128)(2,1)S(1)}, u32[]{:S(2)}, u32[]{:S(2)}) collective-permute-start(bf16[4,8,16,512]{3,2,1,0:T(8,128)(2,1)S(1)} %get-tuple-element.35), channel_id=1, source_target_pairs={{24,0},{0,8},{8,16},{16,24},{25,1},{1,9},{9,17},{17,25},{26,2},{2,... | collective-permute-start | bytes 1572872 | tf_op jit(solution)/shard_map/ppermute | solution.py:27
  47.3 10.1 %collective-permute-start.4 = (bf16[4,8,16,512]{3,2,1,0:T(8,128)(2,1)S(1)}, bf16[4,8,16,512]{3,2,1,0:T(8,128)(2,1)S(1)}, u32[]{:S(2)}, u32[]{:S(2)}) collective-permute-start(bf16[4,8,16,512]{3,2,1,0:T(8,128)(2,1)S(1)} %get-tuple-element.37), channel_id=1, source_target_pairs={{2,0},{4,2},{6,4},{0,6},{3,1},{5,3},{7,5},{1,7},{10,8},{12,10},{14... | collective-permute-start | bytes 1572872 | tf_op jit(solution)/shard_map/ppermute | solution.py:27
  49.4 12.4 %collective-permute-start.6 = (bf16[4,8,16,512]{3,2,1,0:T(8,128)(2,1)S(1)}, bf16[4,8,16,512]{3,2,1,0:T(8,128)(2,1)S(1)}, u32[]{:S(2)}, u32[]{:S(2)}) collective-permute-start(bf16[4,8,16,512]{3,2,1,0:T(8,128)(2,1)S(1)} %get-tuple-element.37), channel_id=1, source_target_pairs={{6,0},{0,2},{2,4},{4,6},{7,1},{1,3},{3,5},{5,7},{14,8},{8,10},{10,... | collective-permute-start | bytes 1572872 | tf_op jit(solution)/shard_map/ppermute | solution.py:27
  53.9 8.0 %collective-permute-start.14 = (bf16[4,4,16,512]{3,2,1,0:T(8,128)(2,1)S(1)}, bf16[4,4,16,512]{3,2,1,0:T(8,128)(2,1)S(1)}, u32[]{:S(2)}, u32[]{:S(2)}) collective-permute-start(bf16[4,4,16,512]{3,2,1,0:T(8,128)(2,1)S(1)} %slice.100), channel_id=1, source_target_pairs={{8,0},{16,8},{24,16},{0,24},{9,1},{17,9},{25,17},{1,25},{10,2},{18... | collective-permute-start | bytes 786440 | tf_op jit(solution)/shard_map/ppermute | solution.py:27
  57.3 7.7 %collective-permute-start.16 = (bf16[4,4,16,512]{3,2,1,0:T(8,128)(2,1)S(1)}, bf16[4,4,16,512]{3,2,1,0:T(8,128)(2,1)S(1)}, u32[]{:S(2)}, u32[]{:S(2)}) collective-permute-start(bf16[4,4,16,512]{3,2,1,0:T(8,128)(2,1)S(1)} %slice.101), channel_id=1, source_target_pairs={{24,0},{0,8},{8,16},{16,24},{25,1},{1,9},{9,17},{17,25},{26,2},{2,... | collective-permute-start | bytes 786440 | tf_op jit(solution)/shard_map/ppermute | solution.py:27
  57.5 8.3 %collective-permute-start.5 = (bf16[4,4,16,512]{3,2,1,0:T(8,128)(2,1)S(1)}, bf16[4,4,16,512]{3,2,1,0:T(8,128)(2,1)S(1)}, u32[]{:S(2)}, u32[]{:S(2)}) collective-permute-start(bf16[4,4,16,512]{3,2,1,0:T(8,128)(2,1)S(1)} %slice.95), channel_id=1, source_target_pairs={{2,0},{4,2},{6,4},{0,6},{3,1},{5,3},{7,5},{1,7},{10,8},{12,10},{14... | collective-permute-start | bytes 786440 | tf_op jit(solution)/shard_map/ppermute | solution.py:27
  61.8 8.1 %collective-permute-start.7 = (bf16[4,4,16,512]{3,2,1,0:T(8,128)(2,1)S(1)}, bf16[4,4,16,512]{3,2,1,0:T(8,128)(2,1)S(1)}, u32[]{:S(2)}, u32[]{:S(2)}) collective-permute-start(bf16[4,4,16,512]{3,2,1,0:T(8,128)(2,1)S(1)} %slice.96), channel_id=1, source_target_pairs={{6,0},{0,2},{2,4},{4,6},{7,1},{1,3},{3,5},{5,7},{14,8},{8,10},{10,... | collective-permute-start | bytes 786440 | tf_op jit(solution)/shard_map/ppermute | solution.py:27
  65.3 5.0 %copy-start.1 = (bf16[4,4,8,16,512]{4,3,2,1,0:T(8,128)(2,1)}, bf16[4,4,8,16,512]{4,3,2,1,0:T(8,128)(2,1)S(1)}, u32[]{:S(2)}) copy-start(bf16[4,4,8,16,512]{4,3,2,1,0:T(8,128)(2,1)S(1)} %pad_maximum_fusion.1.cot0) | copy-start | bytes 6291460
  65.3 5.1 %collective-permute-start.17 = (bf16[4,4,8,16,512]{4,3,2,1,0:T(8,128)(2,1)S(1)}, bf16[4,4,8,16,512]{4,3,2,1,0:T(8,128)(2,1)S(1)}, u32[]{:S(2)}, u32[]{:S(2)}) collective-permute-start(bf16[4,4,8,16,512]{4,3,2,1,0:T(8,128)(2,1)S(1)} %pad_maximum_fusion.1.cot0), channel_id=1, source_target_pairs={{0,1},{1,0},{2,3},{3,2},{4,5},{5,4},{6,7},{7,6},{8,9},{9,8},{10,11... | collective-permute-start | bytes 6291464 | tf_op jit(solution)/shard_map/ppermute | solution.py:31
  70.3 1.3 copy-start.2
  70.3 4.4 %collective-permute-start.8 = (bf16[4,4,8,16,512]{4,3,2,1,0:T(8,128)(2,1)S(1)}, bf16[4,4,8,16,512]{4,3,2,1,0:T(8,128)(2,1)}, u32[]{:S(2)}, u32[]{:S(2)}) collective-permute-start(bf16[4,4,8,16,512]{4,3,2,1,0:T(8,128)(2,1)S(1)} %pad_maximum_fusion.tok0), channel_id=1, source_target_pairs={{0,1},{1,0},{2,3},{3,2},{4,5},{5,4},{6,7},{7,6},{8,9},{9,8},{10,11... | collective-permute-start | bytes 6291464 | tf_op jit(solution)/shard_map/ppermute | solution.py:31
  71.6 1.3 copy-start.12
  116.2 1.1 copy-start
  123.9 4.2 %collective-permute-start.18 = (bf16[16,8,16,512]{3,2,1,0:T(8,128)(2,1)S(1)}, bf16[16,8,16,512]{3,2,1,0:T(8,128)(2,1)S(1)}, u32[]{:S(2)}, u32[]{:S(2)}) collective-permute-start(bf16[16,8,16,512]{3,2,1,0:T(8,128)(2,1)S(1)} %slice_bitcast_fusion), channel_id=1, source_target_pairs={{0,1},{1,0},{2,3},{3,2},{4,5},{5,4},{6,7},{7,6},{8,9},{9,8},{10,11... | collective-permute-start | bytes 6291464 | tf_op jit(solution)/shard_map/ppermute | solution.py:31
  163.5 4.9 %copy-start.6 = (f32[320]{0:T(512)S(1)}, f32[320]{0:T(512)}, u32[]{:S(2)}) copy-start(f32[320]{0:T(512)} %param.18) | copy-start | bytes 3844
  163.5 4.9 %copy-start.7 = (f32[320]{0:T(512)S(1)}, f32[320]{0:T(512)}, u32[]{:S(2)}) copy-start(f32[320]{0:T(512)} %param.20) | copy-start | bytes 3844
  163.5 4.9 %copy-start.8 = (f32[320]{0:T(512)S(1)}, f32[320]{0:T(512)}, u32[]{:S(2)}) copy-start(f32[320]{0:T(512)} %param.21) | copy-start | bytes 3844
  164.6 14.6 %all-to-all-start.2 = ((bf16[8,16,512]{2,1,0:T(8,128)(2,1)}), bf16[8,16,512]{2,1,0:T(8,128)(2,1)S(1)}, u32[]{:S(2)}, u32[]{:S(2)}) async-start(bf16[8,16,512]{2,1,0:T(8,128)(2,1)} %reduce_sum.75), calls=%async_computation.3 | async-start | bytes 262144 | tf_op jit(solution)/shard_map/all_to_all | solution.py:231
  179.1 0.7 copy-start.3
  209.5 12.4 %all-to-all-start.3 = ((f32[8,1,960]{2,1,0:T(1,128)}), f32[8,1,960]{2,1,0:T(1,128)S(1)}, u32[]{:S(2)}, u32[]{:S(2)}) async-start(f32[8,1,960]{2,1,0:T(1,128)} %broadcast_in_dim.6), calls=%async_computation.4 | async-start | bytes 65536 | tf_op jit(solution)/shard_map/all_to_all | solution.py:45
  215.3 23.7 %copy-start.9 = (f32[512]{0:T(512)S(1)}, f32[512]{0:T(512)}, u32[]{:S(2)}) copy-start(f32[512]{0:T(512)} %param.22) | copy-start | bytes 6148
  215.3 23.7 %copy-start.10 = (f32[512]{0:T(512)S(1)}, f32[512]{0:T(512)}, u32[]{:S(2)}) copy-start(f32[512]{0:T(512)} %param.19) | copy-start | bytes 6148
  215.3 23.7 %copy-start.11 = (f32[512]{0:T(512)S(1)}, f32[512]{0:T(512)}, u32[]{:S(2)}) copy-start(f32[512]{0:T(512)} %param.17) | copy-start | bytes 6148
  222.4 1.3 collective-permute-start.19
  224.4 14.6 %all-to-all-start.4 = ((f32[16,6,512]{2,1,0:T(8,128)}), f32[16,6,512]{2,1,0:T(8,128)S(1)}, u32[]{:S(2)}, u32[]{:S(2)}) async-start(f32[16,6,512]{2,1,0:T(8,128)} %broadcast_in_dim.7), calls=%async_computation.5 | async-start | bytes 524288 | tf_op jit(solution)/shard_map/all_to_all | solution.py:45
  239.8 10.8 %all-to-all-start.5 = ((f32[8,3,1]{1,2,0:T(1,128)}), f32[8,3,1]{1,2,0:T(1,128)S(1)}, u32[]{:S(2)}, u32[]{:S(2)}) async-start(f32[8,3,1]{1,2,0:T(1,128)} %broadcast_in_dim.8), calls=%async_computation.6 | async-start | bytes 8192 | tf_op jit(solution)/shard_map/all_to_all | solution.py:45
Sparse Core Ops, SparseCore 0:
  9.8 92.6 all-gather.2
  116.4 90.8 reduce-scatter.1

commit v6 on v5

--- a/solution.py
+++ b/solution.py
@@ -83,7 +83,6 @@
         return carry
 
     lax.fori_loop(0, NZ, start, 0)
-    acc[...] = jnp.zeros_like(acc)
 
     def forward(pair, carry):
         first = second = 0.0
@@ -92,8 +91,8 @@
                 copy.wait()
             first += dot_nt(w[k, : 2 * FB], x[0, k].reshape(TOK, DB))
             second += dot_nt(w[k, 2 * FB :], x[1, k].reshape(TOK, DB))
-        acc[: 2 * FB] += first
-        acc[2 * FB :] += second
+        acc[: 2 * FB] = first if pair == 0 else acc[: 2 * FB] + first
+        acc[2 * FB :] = second if pair == 0 else acc[2 * FB :] + second
         return carry
 
     for pair in range(NZ // 2):

time: 260 us -> 260 us (level)
  no operation moved by 1% of the time
where the time goes in v6:
time: 260 us; the launch traced here: 259 us
  waiting for transfers between devices  106 us (41%)
  blocking collectives  54.6 us (21%)
  starting transfers between devices  43 us (17%)
  Pallas kernels  21.7 us (8%)
  between operations  15.2 us (6%)
  other arithmetic  9.24 us (4%)
  local copies, waits for them, and re-layouts  9.09 us (3%)
    all_to_all x1, blocking collectives, local(): part = lax.all_to_all(part, ('x', 'y'), 0, 0, tiled=True)  34.4 us
    all_gather x1, waiting for transfers between devices, local(): lax.all_gather(jnp.concatenate([wi_gate.T, wi_lin.T, wo], 0), 'z', axis=0)  27.8 us
    reduce_scatter x1, waiting for transfers between devices, local(): grad_w = lax.psum_scatter(grad_w, 'z', scatter_dimension=0)  25.9 us
    ppermute x16, starting transfers between devices, shifted(): return lax.ppermute(value, axis, [((i + step) % 4, i) for i in range(4)])  23.8 us
    all_to_all x1, blocking collectives, local(): pair = lax.all_to_all(pair, 'z', 0, 0, tiled=True)  20.2 us
    all_to_all x3, waiting for transfers between devices, sum_over(): return jnp.sum(lax.all_to_all(copies, axis, 0, 0, tiled=True), 0)  19.5 us
    ppermute x16, waiting for transfers between devices, shifted(): return lax.ppermute(value, axis, [((i + step) % 4, i) for i in range(4)])  15.4 us
    all_to_all x3, starting transfers between devices, sum_over(): return jnp.sum(lax.all_to_all(copies, axis, 0, 0, tiled=True), 0)  14.9 us
  transfers between devices with their start and end apart: 26, of which 18 were waited for; matrix products, arithmetic and copies ran while one was open for 2% of the time, Pallas kernels for 3%

profile of v6, /device:TPU:8, one launch (start us, length us, event | category | flops | bytes accessed | tf_op | source)
XLA Modules:
  0.0 259.1 jit_solution(3604059555314376920)
XLA Ops:
  7.2 2.3 pad_maximum_fusion.2
  9.7 20.2 %all_to_all.31 = bf16[8,2,16,512]{3,2,1,0:T(8,128)(2,1)S(1)} all-to-all(bf16[8,2,16,512]{3,2,1,0:T(8,128)(2,1)S(1)} %pad_maximum_fusion.5), channel_id=1, replica_groups=mesh['z'=8,'x'=4,'y'=4,'c'=2] {'z'}, dimensions={0} | all-to-all | bytes 524288 | tf_op jit(solution)/shard_map/all_to_all | solution.py:214
  29.9 0.5 collective-permute-start.9
  30.4 1.6 collective-permute-start.11
  32.0 2.8 %collective-permute-start = (bf16[8,16,512]{2,1,0:T(8,128)(2,1)S(1)}, bf16[8,16,512]{2,1,0:T(8,128)(2,1)S(1)}, u32[]{:S(2)}, u32[]{:S(2)}) collective-permute-start(bf16[8,16,512]{2,1,0:T(8,128)(2,1)S(1)} %get-tuple-element.40), channel_id=1, source_target_pairs={{8,0},{16,8},{24,16},{0,24},{9,1},{17,9},{25,17},{1,25},{10,2},{18... | collective-permute-start | bytes 393224 | tf_op jit(solution)/shard_map/ppermute | solution.py:27
  34.8 0.3 collective-permute-done.9
  35.1 1.2 collective-permute-start.10
  36.3 0.1 collective-permute-done.11
  36.4 0.9 collective-permute-start.12
  37.3 0.2 collective-permute-done
  37.5 3.5 %collective-permute-start.1 = (bf16[4,16,512]{2,1,0:T(8,128)(2,1)S(1)}, bf16[4,16,512]{2,1,0:T(8,128)(2,1)S(1)}, u32[]{:S(2)}, u32[]{:S(2)}) collective-permute-start(bf16[4,16,512]{2,1,0:T(8,128)(2,1)S(1)} %slice.93), channel_id=1, source_target_pairs={{8,0},{16,8},{24,16},{0,24},{9,1},{17,9},{25,17},{1,25},{10,2},{18... | collective-permute-start | bytes 196616 | tf_op jit(solution)/shard_map/ppermute | solution.py:27
  41.1 0.9 collective-permute-done.12
  42.0 0.1 fusion.8
  42.1 3.2 %collective-permute-start.13 = (bf16[4,8,16,512]{3,2,1,0:T(8,128)(2,1)S(1)}, bf16[4,8,16,512]{3,2,1,0:T(8,128)(2,1)S(1)}, u32[]{:S(2)}, u32[]{:S(2)}) collective-permute-start(bf16[4,8,16,512]{3,2,1,0:T(8,128)(2,1)S(1)} %get-tuple-element.35), channel_id=1, source_target_pairs={{8,0},{16,8},{24,16},{0,24},{9,1},{17,9},{25,17},{1,25},{10,2},{18... | collective-permute-start | bytes 1572872 | tf_op jit(solution)/shard_map/ppermute | solution.py:27
  45.3 1.9 collective-permute-done.3
  47.2 0.1 fusion.9
  47.3 2.1 collective-permute-start.4
  49.4 4.5 %collective-permute-done.13 = bf16[4,8,16,512]{3,2,1,0:T(8,128)(2,1)S(1)} collective-permute-done((bf16[4,8,16,512]{3,2,1,0:T(8,128)(2,1)S(1)}, bf16[4,8,16,512]{3,2,1,0:T(8,128)(2,1)S(1)}, u32[]{:S(2)}, u32[]{:S(2)}) %collective-permute-start.13) | collective-permute-done | bytes 524320 | tf_op jit(solution)/shard_map/ppermute | solution.py:27
  53.9 3.4 %collective-permute-start.14 = (bf16[4,4,16,512]{3,2,1,0:T(8,128)(2,1)S(1)}, bf16[4,4,16,512]{3,2,1,0:T(8,128)(2,1)S(1)}, u32[]{:S(2)}, u32[]{:S(2)}) collective-permute-start(bf16[4,4,16,512]{3,2,1,0:T(8,128)(2,1)S(1)} %slice.100), channel_id=1, source_target_pairs={{8,0},{16,8},{24,16},{0,24},{9,1},{17,9},{25,17},{1,25},{10,2},{18... | collective-permute-start | bytes 786440 | tf_op jit(solution)/shard_map/ppermute | solution.py:27
  57.5 4.3 %collective-permute-start.5 = (bf16[4,4,16,512]{3,2,1,0:T(8,128)(2,1)S(1)}, bf16[4,4,16,512]{3,2,1,0:T(8,128)(2,1)S(1)}, u32[]{:S(2)}, u32[]{:S(2)}) collective-permute-start(bf16[4,4,16,512]{3,2,1,0:T(8,128)(2,1)S(1)} %slice.95), channel_id=1, source_target_pairs={{2,0},{4,2},{6,4},{0,6},{3,1},{5,3},{7,5},{1,7},{10,8},{12,10},{14... | collective-permute-start | bytes 786440 | tf_op jit(solution)/shard_map/ppermute | solution.py:27
  61.9 3.1 %collective-permute-done.16 = bf16[4,4,16,512]{3,2,1,0:T(8,128)(2,1)S(1)} collective-permute-done((bf16[4,4,16,512]{3,2,1,0:T(8,128)(2,1)S(1)}, bf16[4,4,16,512]{3,2,1,0:T(8,128)(2,1)S(1)}, u32[]{:S(2)}, u32[]{:S(2)}) %collective-permute-start.16) | collective-permute-done | bytes 262176 | tf_op jit(solution)/shard_map/ppermute | solution.py:27
  65.0 0.3 pad_maximum_fusion.1.cot0
  65.3 0.1 collective-permute-start.17
  65.4 0.3 collective-permute-done.5
  65.7 4.2 %collective-permute-done.7 = bf16[4,4,16,512]{3,2,1,0:T(8,128)(2,1)S(1)} collective-permute-done((bf16[4,4,16,512]{3,2,1,0:T(8,128)(2,1)S(1)}, bf16[4,4,16,512]{3,2,1,0:T(8,128)(2,1)S(1)}, u32[]{:S(2)}, u32[]{:S(2)}) %collective-permute-start.7) | collective-permute-done | bytes 262176 | tf_op jit(solution)/shard_map/ppermute | solution.py:27
  70.0 0.3 pad_maximum_fusion.tok0
  70.3 0.1 collective-permute-start.8
  70.4 1.2 copy-done.2
  71.6 1.3 copy-done.12
  72.9 1.7 collective-permute-done.8.tok1
  74.7 27.8 %all-gather.3.cloned.1.call-done = bf16[7680,512]{1,0:T(8,128)(2,1)} async-done(((bf16[960,512]{1,0:T(8,128)(2,1)}), bf16[7680,512]{1,0:T(8,128)(2,1)}) %all-gather.3.cloned.1.call-update) | async-done | bytes 7864336 | tf_op jit(solution)/shard_map/all_gather | solution.py:211
  102.5 13.7 %shard_map.195 = (bf16[8,960,512]{2,1,0:T(8,128)(2,1)}, bf16[512,640]{1,0:T(8,128)(2,1)}) custom-call(bf16[4,4,8,16,512]{4,3,2,1,0:T(8,128)(2,1)} %copy-done.2, bf16[4,4,8,16,512]{4,3,2,1,0:T(8,128)(2,1)} %collective-permute-done.8.tok1, bf16[4,4,8,16,512]{4,3,2,1,0:T(8,128)(2,1)} %copy-done.1, bf16[4,4,8,16,512]{4,3,2,1,0:T(8,128)(2,1)} %copy-done.12, ...), custom_call_target="tpu_custom_call" | custom-call | flops 8053063680 | bytes 25000000 | tf_op jit(solution)/shard_map/pallas_call | solution.py:143
  116.4 0.9 copy-done
  117.3 6.4 %shard_map.196 = bf16[2,16,8,16,512]{4,3,2,1,0:T(8,128)(2,1)S(1)} custom-call(s32[16]{0:T(128)S(1)} %add.105.place, bf16[512,640]{1,0:T(8,128)(2,1)S(1)} %copy-done, bf16[8,960,512]{2,1,0:T(8,128)(2,1)} %bitcast.75), custom_call_target="tpu_custom_call" | custom-call | flops 2684354560 | bytes 10000000 | tf_op jit(solution)/shard_map/pallas_call | solution.py:167
  123.7 0.2 slice_bitcast_fusion
  123.9 0.1 collective-permute-start.18
  124.0 4.1 %collective-permute-done.18 = bf16[16,8,16,512]{3,2,1,0:T(8,128)(2,1)S(1)} collective-permute-done((bf16[16,8,16,512]{3,2,1,0:T(8,128)(2,1)S(1)}, bf16[16,8,16,512]{3,2,1,0:T(8,128)(2,1)S(1)}, u32[]{:S(2)}, u32[]{:S(2)}) %collective-permute-start.18) | collective-permute-done | bytes 2097184 | tf_op jit(solution)/shard_map/ppermute | solution.py:31
  128.2 1.0 fusion
  129.1 34.4 %all_to_all.32 = bf16[16,8,16,512]{3,2,1,0:T(8,128)(2,1)S(1)} all-to-all(bf16[16,8,16,512]{3,2,1,0:T(8,128)(2,1)S(1)} %fusion), channel_id=1, replica_groups=mesh['z'=8,'x'=4,'y'=4,'c'=2] {'x','y'}, dimensions={0} | all-to-all | bytes 4194304 | tf_op jit(solution)/shard_map/all_to_all | solution.py:228
  163.5 1.1 reduce_sum.75
  164.6 3.8 %all-to-all-start.2 = ((bf16[8,16,512]{2,1,0:T(8,128)(2,1)}), bf16[8,16,512]{2,1,0:T(8,128)(2,1)S(1)}, u32[]{:S(2)}, u32[]{:S(2)}) async-start(bf16[8,16,512]{2,1,0:T(8,128)(2,1)} %reduce_sum.75), calls=%async_computation.3 | async-start | bytes 262144 | tf_op jit(solution)/shard_map/all_to_all | solution.py:230
  168.4 10.7 %all-to-all-done.2 = bf16[8,16,512]{2,1,0:T(8,128)(2,1)S(1)} async-done(((bf16[8,16,512]{2,1,0:T(8,128)(2,1)}), bf16[8,16,512]{2,1,0:T(8,128)(2,1)S(1)}, u32[]{:S(2)}, u32[]{:S(2)}) %all-to-all-start.2) | async-done | bytes 131104 | tf_op jit(solution)/shard_map/all_to_all | solution.py:230
  179.1 0.7 copy-done.3
  179.8 1.6 shard_map.197
  181.4 25.9 %reduce-scatter.2.cloned.1.call-done = bf16[1,960,512]{2,1,0:T(8,128)(2,1)} async-done(((bf16[8,960,512]{2,1,0:T(8,128)(2,1)}), bf16[1,960,512]{2,1,0:T(8,128)(2,1)}) %reduce-scatter.2.cloned.1.call-update) | async-done | bytes 983056 | tf_op jit(solution)/shard_map/reduce_scatter | solution.py:220
  207.2 1.6 add_reduce_fusion.1
  208.8 0.6 broadcast_in_dim.6
  209.5 4.4 %all-to-all-start.3 = ((f32[8,1,960]{2,1,0:T(1,128)}), f32[8,1,960]{2,1,0:T(1,128)S(1)}, u32[]{:S(2)}, u32[]{:S(2)}) async-start(f32[8,1,960]{2,1,0:T(1,128)} %broadcast_in_dim.6), calls=%async_computation.4 | async-start | bytes 65536 | tf_op jit(solution)/shard_map/all_to_all | solution.py:45
  213.9 1.5 convert_multiply_fusion
  215.4 6.5 %all-to-all-done.3 = f32[8,1,960]{2,1,0:T(1,128)S(1)} async-done(((f32[8,1,960]{2,1,0:T(1,128)}), f32[8,1,960]{2,1,0:T(1,128)S(1)}, u32[]{:S(2)}, u32[]{:S(2)}) %all-to-all-start.3) | async-done | bytes 30752 | tf_op jit(solution)/shard_map/all_to_all | solution.py:45
  222.0 0.4 add_reduce_fusion
  222.4 0.1 collective-permute-start.19
  222.5 1.2 collective-permute-done.19
  223.7 0.7 broadcast_in_dim.7
  224.4 7.2 %all-to-all-start.4 = ((f32[16,6,512]{2,1,0:T(8,128)}), f32[16,6,512]{2,1,0:T(8,128)S(1)}, u32[]{:S(2)}, u32[]{:S(2)}) async-start(f32[16,6,512]{2,1,0:T(8,128)} %broadcast_in_dim.7), calls=%async_computation.5 | async-start | bytes 524288 | tf_op jit(solution)/shard_map/all_to_all | solution.py:45
  232.3 0.6 slice_reduce_fusion
  232.9 6.1 %all-to-all-done.4 = f32[16,6,512]{2,1,0:T(8,128)S(1)} async-done(((f32[16,6,512]{2,1,0:T(8,128)}), f32[16,6,512]{2,1,0:T(8,128)S(1)}, u32[]{:S(2)}, u32[]{:S(2)}) %all-to-all-start.4) | async-done | bytes 196640 | tf_op jit(solution)/shard_map/all_to_all | solution.py:45
  239.1 0.1 fusion.2
  239.2 0.6 broadcast_in_dim.8
  239.8 3.3 %all-to-all-start.5 = ((f32[8,3,1]{1,2,0:T(1,128)}), f32[8,3,1]{1,2,0:T(1,128)S(1)}, u32[]{:S(2)}, u32[]{:S(2)}) async-start(f32[8,3,1]{1,2,0:T(1,128)} %broadcast_in_dim.8), calls=%async_computation.6 | async-start | bytes 8192 | tf_op jit(solution)/shard_map/all_to_all | solution.py:45
  243.1 0.6 fusion.13
  243.7 6.9 %all-to-all-done.5 = f32[8,3,1]{1,2,0:T(1,128)S(1)} async-done(((f32[8,3,1]{1,2,0:T(1,128)}), f32[8,3,1]{1,2,0:T(1,128)S(1)}, u32[]{:S(2)}, u32[]{:S(2)}) %all-to-all-start.5) | async-done | bytes 128 | tf_op jit(solution)/shard_map/all_to_all | solution.py:45
  250.7 0.2 multiply_multiply_fusion
  251.0 1.3 slice_bitcast_fusion.2
  (71 shorter events, 1.2 us)
Async XLA Ops:
  7.2 2.4 copy-start.5
  7.2 2.4 copy-start.4
  7.2 95.3 %all-gather.3.cloned.1.call-start = ((), (), s32[]{:S(2)}) async-start(), calls=%async_computation.8 | async-start | bytes 8847360 | tf_op jit(solution)/shard_map/all_gather | solution.py:211
  9.6 197.7 %reduce-scatter.2.cloned.1.call-start = ((), (), s32[]{:S(2)}) async-start(), calls=%async_computation.7 | async-start | bytes 8847360 | tf_op jit(solution)/shard_map/reduce_scatter | solution.py:220
  29.9 5.2 %collective-permute-start.9 = (bf16[8,16,512]{2,1,0:T(8,128)(2,1)S(1)}, bf16[8,16,512]{2,1,0:T(8,128)(2,1)S(1)}, u32[]{:S(2)}, u32[]{:S(2)}) collective-permute-start(bf16[8,16,512]{2,1,0:T(8,128)(2,1)S(1)} %get-tuple-element.41), channel_id=1, source_target_pairs={{2,0},{4,2},{6,4},{0,6},{3,1},{5,3},{7,5},{1,7},{10,8},{12,10},{14... | collective-permute-start | bytes 393224 | tf_op jit(solution)/shard_map/ppermute | solution.py:27
  30.4 6.0 %collective-permute-start.11 = (bf16[8,16,512]{2,1,0:T(8,128)(2,1)S(1)}, bf16[8,16,512]{2,1,0:T(8,128)(2,1)S(1)}, u32[]{:S(2)}, u32[]{:S(2)}) collective-permute-start(bf16[8,16,512]{2,1,0:T(8,128)(2,1)S(1)} %get-tuple-element.41), channel_id=1, source_target_pairs={{6,0},{0,2},{2,4},{4,6},{7,1},{1,3},{3,5},{5,7},{14,8},{8,10},{10,... | collective-permute-start | bytes 393224 | tf_op jit(solution)/shard_map/ppermute | solution.py:27
  32.0 5.5 %collective-permute-start = (bf16[8,16,512]{2,1,0:T(8,128)(2,1)S(1)}, bf16[8,16,512]{2,1,0:T(8,128)(2,1)S(1)}, u32[]{:S(2)}, u32[]{:S(2)}) collective-permute-start(bf16[8,16,512]{2,1,0:T(8,128)(2,1)S(1)} %get-tuple-element.40), channel_id=1, source_target_pairs={{8,0},{16,8},{24,16},{0,24},{9,1},{17,9},{25,17},{1,25},{10,2},{18... | collective-permute-start | bytes 393224 | tf_op jit(solution)/shard_map/ppermute | solution.py:27
  34.8 6.2 %collective-permute-start.2 = (bf16[8,16,512]{2,1,0:T(8,128)(2,1)S(1)}, bf16[8,16,512]{2,1,0:T(8,128)(2,1)S(1)}, u32[]{:S(2)}, u32[]{:S(2)}) collective-permute-start(bf16[8,16,512]{2,1,0:T(8,128)(2,1)S(1)} %get-tuple-element.40), channel_id=1, source_target_pairs={{24,0},{0,8},{8,16},{16,24},{25,1},{1,9},{9,17},{17,25},{26,2},{2,... | collective-permute-start | bytes 393224 | tf_op jit(solution)/shard_map/ppermute | solution.py:27
  35.1 6.0 %collective-permute-start.10 = (bf16[4,16,512]{2,1,0:T(8,128)(2,1)S(1)}, bf16[4,16,512]{2,1,0:T(8,128)(2,1)S(1)}, u32[]{:S(2)}, u32[]{:S(2)}) collective-permute-start(bf16[4,16,512]{2,1,0:T(8,128)(2,1)S(1)} %slice.98), channel_id=1, source_target_pairs={{2,0},{4,2},{6,4},{0,6},{3,1},{5,3},{7,5},{1,7},{10,8},{12,10},{14... | collective-permute-start | bytes 196616 | tf_op jit(solution)/shard_map/ppermute | solution.py:27
  36.4 5.6 %collective-permute-start.12 = (bf16[4,16,512]{2,1,0:T(8,128)(2,1)S(1)}, bf16[4,16,512]{2,1,0:T(8,128)(2,1)S(1)}, u32[]{:S(2)}, u32[]{:S(2)}) collective-permute-start(bf16[4,16,512]{2,1,0:T(8,128)(2,1)S(1)} %slice.99), channel_id=1, source_target_pairs={{6,0},{0,2},{2,4},{4,6},{7,1},{1,3},{3,5},{5,7},{14,8},{8,10},{10,... | collective-permute-start | bytes 196616 | tf_op jit(solution)/shard_map/ppermute | solution.py:27
  37.5 7.8 %collective-permute-start.1 = (bf16[4,16,512]{2,1,0:T(8,128)(2,1)S(1)}, bf16[4,16,512]{2,1,0:T(8,128)(2,1)S(1)}, u32[]{:S(2)}, u32[]{:S(2)}) collective-permute-start(bf16[4,16,512]{2,1,0:T(8,128)(2,1)S(1)} %slice.93), channel_id=1, source_target_pairs={{8,0},{16,8},{24,16},{0,24},{9,1},{17,9},{25,17},{1,25},{10,2},{18... | collective-permute-start | bytes 196616 | tf_op jit(solution)/shard_map/ppermute | solution.py:27
  41.0 6.2 %collective-permute-start.3 = (bf16[4,16,512]{2,1,0:T(8,128)(2,1)S(1)}, bf16[4,16,512]{2,1,0:T(8,128)(2,1)S(1)}, u32[]{:S(2)}, u32[]{:S(2)}) collective-permute-start(bf16[4,16,512]{2,1,0:T(8,128)(2,1)S(1)} %slice.94), channel_id=1, source_target_pairs={{24,0},{0,8},{8,16},{16,24},{25,1},{1,9},{9,17},{17,25},{26,2},{2,... | collective-permute-start | bytes 196616 | tf_op jit(solution)/shard_map/ppermute | solution.py:27
  42.1 11.8 %collective-permute-start.13 = (bf16[4,8,16,512]{3,2,1,0:T(8,128)(2,1)S(1)}, bf16[4,8,16,512]{3,2,1,0:T(8,128)(2,1)S(1)}, u32[]{:S(2)}, u32[]{:S(2)}) collective-permute-start(bf16[4,8,16,512]{3,2,1,0:T(8,128)(2,1)S(1)} %get-tuple-element.35), channel_id=1, source_target_pairs={{8,0},{16,8},{24,16},{0,24},{9,1},{17,9},{25,17},{1,25},{10,2},{18... | collective-permute-start | bytes 1572872 | tf_op jit(solution)/shard_map/ppermute | solution.py:27
  45.3 12.0 %collective-permute-start.15 = (bf16[4,8,16,512]{3,2,1,0:T(8,128)(2,1)S(1)}, bf16[4,8,16,512]{3,2,1,0:T(8,128)(2,1)S(1)}, u32[]{:S(2)}, u32[]{:S(2)}) collective-permute-start(bf16[4,8,16,512]{3,2,1,0:T(8,128)(2,1)S(1)} %get-tuple-element.35), channel_id=1, source_target_pairs={{24,0},{0,8},{8,16},{16,24},{25,1},{1,9},{9,17},{17,25},{26,2},{2,... | collective-permute-start | bytes 1572872 | tf_op jit(solution)/shard_map/ppermute | solution.py:27
  47.3 10.1 %collective-permute-start.4 = (bf16[4,8,16,512]{3,2,1,0:T(8,128)(2,1)S(1)}, bf16[4,8,16,512]{3,2,1,0:T(8,128)(2,1)S(1)}, u32[]{:S(2)}, u32[]{:S(2)}) collective-permute-start(bf16[4,8,16,512]{3,2,1,0:T(8,128)(2,1)S(1)} %get-tuple-element.37), channel_id=1, source_target_pairs={{2,0},{4,2},{6,4},{0,6},{3,1},{5,3},{7,5},{1,7},{10,8},{12,10},{14... | collective-permute-start | bytes 1572872 | tf_op jit(solution)/shard_map/ppermute | solution.py:27
  49.4 12.4 %collective-permute-start.6 = (bf16[4,8,16,512]{3,2,1,0:T(8,128)(2,1)S(1)}, bf16[4,8,16,512]{3,2,1,0:T(8,128)(2,1)S(1)}, u32[]{:S(2)}, u32[]{:S(2)}) collective-permute-start(bf16[4,8,16,512]{3,2,1,0:T(8,128)(2,1)S(1)} %get-tuple-element.37), channel_id=1, source_target_pairs={{6,0},{0,2},{2,4},{4,6},{7,1},{1,3},{3,5},{5,7},{14,8},{8,10},{10,... | collective-permute-start | bytes 1572872 | tf_op jit(solution)/shard_map/ppermute | solution.py:27
  53.9 8.0 %collective-permute-start.14 = (bf16[4,4,16,512]{3,2,1,0:T(8,128)(2,1)S(1)}, bf16[4,4,16,512]{3,2,1,0:T(8,128)(2,1)S(1)}, u32[]{:S(2)}, u32[]{:S(2)}) collective-permute-start(bf16[4,4,16,512]{3,2,1,0:T(8,128)(2,1)S(1)} %slice.100), channel_id=1, source_target_pairs={{8,0},{16,8},{24,16},{0,24},{9,1},{17,9},{25,17},{1,25},{10,2},{18... | collective-permute-start | bytes 786440 | tf_op jit(solution)/shard_map/ppermute | solution.py:27
  57.3 7.7 %collective-permute-start.16 = (bf16[4,4,16,512]{3,2,1,0:T(8,128)(2,1)S(1)}, bf16[4,4,16,512]{3,2,1,0:T(8,128)(2,1)S(1)}, u32[]{:S(2)}, u32[]{:S(2)}) collective-permute-start(bf16[4,4,16,512]{3,2,1,0:T(8,128)(2,1)S(1)} %slice.101), channel_id=1, source_target_pairs={{24,0},{0,8},{8,16},{16,24},{25,1},{1,9},{9,17},{17,25},{26,2},{2,... | collective-permute-start | bytes 786440 | tf_op jit(solution)/shard_map/ppermute | solution.py:27
  57.5 8.3 %collective-permute-start.5 = (bf16[4,4,16,512]{3,2,1,0:T(8,128)(2,1)S(1)}, bf16[4,4,16,512]{3,2,1,0:T(8,128)(2,1)S(1)}, u32[]{:S(2)}, u32[]{:S(2)}) collective-permute-start(bf16[4,4,16,512]{3,2,1,0:T(8,128)(2,1)S(1)} %slice.95), channel_id=1, source_target_pairs={{2,0},{4,2},{6,4},{0,6},{3,1},{5,3},{7,5},{1,7},{10,8},{12,10},{14... | collective-permute-start | bytes 786440 | tf_op jit(solution)/shard_map/ppermute | solution.py:27
  61.8 8.1 %collective-permute-start.7 = (bf16[4,4,16,512]{3,2,1,0:T(8,128)(2,1)S(1)}, bf16[4,4,16,512]{3,2,1,0:T(8,128)(2,1)S(1)}, u32[]{:S(2)}, u32[]{:S(2)}) collective-permute-start(bf16[4,4,16,512]{3,2,1,0:T(8,128)(2,1)S(1)} %slice.96), channel_id=1, source_target_pairs={{6,0},{0,2},{2,4},{4,6},{7,1},{1,3},{3,5},{5,7},{14,8},{8,10},{10,... | collective-permute-start | bytes 786440 | tf_op jit(solution)/shard_map/ppermute | solution.py:27
  65.3 5.0 %copy-start.1 = (bf16[4,4,8,16,512]{4,3,2,1,0:T(8,128)(2,1)}, bf16[4,4,8,16,512]{4,3,2,1,0:T(8,128)(2,1)S(1)}, u32[]{:S(2)}) copy-start(bf16[4,4,8,16,512]{4,3,2,1,0:T(8,128)(2,1)S(1)} %pad_maximum_fusion.1.cot0) | copy-start | bytes 6291460
  65.3 5.1 %collective-permute-start.17 = (bf16[4,4,8,16,512]{4,3,2,1,0:T(8,128)(2,1)S(1)}, bf16[4,4,8,16,512]{4,3,2,1,0:T(8,128)(2,1)S(1)}, u32[]{:S(2)}, u32[]{:S(2)}) collective-permute-start(bf16[4,4,8,16,512]{4,3,2,1,0:T(8,128)(2,1)S(1)} %pad_maximum_fusion.1.cot0), channel_id=1, source_target_pairs={{0,1},{1,0},{2,3},{3,2},{4,5},{5,4},{6,7},{7,6},{8,9},{9,8},{10,11... | collective-permute-start | bytes 6291464 | tf_op jit(solution)/shard_map/ppermute | solution.py:31
  70.3 1.3 copy-start.2
  70.3 4.4 %collective-permute-start.8 = (bf16[4,4,8,16,512]{4,3,2,1,0:T(8,128)(2,1)S(1)}, bf16[4,4,8,16,512]{4,3,2,1,0:T(8,128)(2,1)}, u32[]{:S(2)}, u32[]{:S(2)}) collective-permute-start(bf16[4,4,8,16,512]{4,3,2,1,0:T(8,128)(2,1)S(1)} %pad_maximum_fusion.tok0), channel_id=1, source_target_pairs={{0,1},{1,0},{2,3},{3,2},{4,5},{5,4},{6,7},{7,6},{8,9},{9,8},{10,11... | collective-permute-start | bytes 6291464 | tf_op jit(solution)/shard_map/ppermute | solution.py:31
  71.6 1.3 copy-start.12
  116.2 1.1 copy-start
  123.9 4.2 %collective-permute-start.18 = (bf16[16,8,16,512]{3,2,1,0:T(8,128)(2,1)S(1)}, bf16[16,8,16,512]{3,2,1,0:T(8,128)(2,1)S(1)}, u32[]{:S(2)}, u32[]{:S(2)}) collective-permute-start(bf16[16,8,16,512]{3,2,1,0:T(8,128)(2,1)S(1)} %slice_bitcast_fusion), channel_id=1, source_target_pairs={{0,1},{1,0},{2,3},{3,2},{4,5},{5,4},{6,7},{7,6},{8,9},{9,8},{10,11... | collective-permute-start | bytes 6291464 | tf_op jit(solution)/shard_map/ppermute | solution.py:31
  163.5 4.9 %copy-start.6 = (f32[320]{0:T(512)S(1)}, f32[320]{0:T(512)}, u32[]{:S(2)}) copy-start(f32[320]{0:T(512)} %param.18) | copy-start | bytes 3844
  163.5 4.9 %copy-start.7 = (f32[320]{0:T(512)S(1)}, f32[320]{0:T(512)}, u32[]{:S(2)}) copy-start(f32[320]{0:T(512)} %param.20) | copy-start | bytes 3844
  163.5 4.9 %copy-start.8 = (f32[320]{0:T(512)S(1)}, f32[320]{0:T(512)}, u32[]{:S(2)}) copy-start(f32[320]{0:T(512)} %param.21) | copy-start | bytes 3844
  164.6 14.6 %all-to-all-start.2 = ((bf16[8,16,512]{2,1,0:T(8,128)(2,1)}), bf16[8,16,512]{2,1,0:T(8,128)(2,1)S(1)}, u32[]{:S(2)}, u32[]{:S(2)}) async-start(bf16[8,16,512]{2,1,0:T(8,128)(2,1)} %reduce_sum.75), calls=%async_computation.3 | async-start | bytes 262144 | tf_op jit(solution)/shard_map/all_to_all | solution.py:230
  179.1 0.7 copy-start.3
  209.5 12.4 %all-to-all-start.3 = ((f32[8,1,960]{2,1,0:T(1,128)}), f32[8,1,960]{2,1,0:T(1,128)S(1)}, u32[]{:S(2)}, u32[]{:S(2)}) async-start(f32[8,1,960]{2,1,0:T(1,128)} %broadcast_in_dim.6), calls=%async_computation.4 | async-start | bytes 65536 | tf_op jit(solution)/shard_map/all_to_all | solution.py:45
  215.3 23.7 %copy-start.9 = (f32[512]{0:T(512)S(1)}, f32[512]{0:T(512)}, u32[]{:S(2)}) copy-start(f32[512]{0:T(512)} %param.22) | copy-start | bytes 6148
  215.3 23.7 %copy-start.10 = (f32[512]{0:T(512)S(1)}, f32[512]{0:T(512)}, u32[]{:S(2)}) copy-start(f32[512]{0:T(512)} %param.19) | copy-start | bytes 6148
  215.3 23.7 %copy-start.11 = (f32[512]{0:T(512)S(1)}, f32[512]{0:T(512)}, u32[]{:S(2)}) copy-start(f32[512]{0:T(512)} %param.17) | copy-start | bytes 6148
  222.4 1.3 collective-permute-start.19
  224.4 14.6 %all-to-all-start.4 = ((f32[16,6,512]{2,1,0:T(8,128)}), f32[16,6,512]{2,1,0:T(8,128)S(1)}, u32[]{:S(2)}, u32[]{:S(2)}) async-start(f32[16,6,512]{2,1,0:T(8,128)} %broadcast_in_dim.7), calls=%async_computation.5 | async-start | bytes 524288 | tf_op jit(solution)/shard_map/all_to_all | solution.py:45
  239.8 10.8 %all-to-all-start.5 = ((f32[8,3,1]{1,2,0:T(1,128)}), f32[8,3,1]{1,2,0:T(1,128)S(1)}, u32[]{:S(2)}, u32[]{:S(2)}) async-start(f32[8,3,1]{1,2,0:T(1,128)} %broadcast_in_dim.8), calls=%async_computation.6 | async-start | bytes 8192 | tf_op jit(solution)/shard_map/all_to_all | solution.py:45
Sparse Core Ops, SparseCore 0:
  9.8 92.6 all-gather.2
  116.4 90.8 reduce-scatter.1
